TPU v7x, 256 devices: a whole 4x4x8 slice. The times are simulated.
256 devices in a mesh: gx: 4 (over y), gy: 4 (over z_lo), gz: 16 (over z_hi, x, core).
Axes of the slice: x: 4, y: 4, z: 8 (z_hi: 2, z_lo: 4; z = z_hi * 4 + z_lo), core: 2. Of those that a mesh axis runs over, the one named last changes fastest.
Arguments:
- offsets: float32 [8, 8, 32, 3, 1024], P('gx', 'gy', 'gz'), may hold values from 0 to 1
- probes: bfloat16 [8, 8, 32, 32, 1024], P('gx', 'gy', 'gz'), may hold values from -6 to 6
- counts: int32 [8, 8, 32], P('gx', 'gy', 'gz'), may hold values from 1 to 1024, as said below
- req_box: int32 [4, 4, 16, 64, 2], P('gx', 'gy', 'gz'), may hold values from -1 to 7, as said below
- req_tgt: int32 [4, 4, 16, 64, 2], P('gx', 'gy', 'gz'), may hold values from 0 to 7, as said below
Outputs:
- kv: bfloat16 [8, 8, 32, 32, 1024], P('gx', 'gy', 'gz')
- quad: float32 [32], replicated
Inputs may be any that keep to these rules, and one draw needn't show every extreme that they name: `counts`: every device has a box with 1024 points. `req_box`: A local box index of the peer, or -1 for an unused slot; the live slots of a pair come first; a pair whose gy indices and gz indices both differ by less than 2 has no live slot; some pair has all 2 slots live. `req_tgt`: A local box index of the requesting device.
All inputs are finite; a program needn't handle non-finite values.
Results may differ from a plain program's by a relative error of at most 0.0012.
The roundings to bfloat16 on the way count: a program that leaves them out, or rounds other values in their place, can miss the bound.
Values may be sent and summed in bfloat16 or wider, within the bound.
No kernel may reach another device: no remote copies, remote signals or barrier semaphores. Data moves between devices by JAX's collectives and lax.ppermute only.
A program may use at most 64 MiB of HBM per device.

v0:
```python
import functools
import math

import jax
import jax.numpy as jnp
from jax import lax
from jax.experimental import pallas as pl
from jax.experimental.pallas import tpu as pltpu
from jax.sharding import PartitionSpec as P

ORDER = 4
CHUNK = 128
BOXES = 8
FEATS = 48
ROWS = 48
F32 = jnp.float32
BF16 = jnp.bfloat16
NODES = [math.cos((2.0 * a + 1.0) * math.pi / (2.0 * ORDER)) for a in range(ORDER)]


def box_id(axis, at, first, second):
    place = [0, 0, 0]
    rest = [d for d in range(3) if d != axis]
    place[axis] = at
    place[rest[0]] = first
    place[rest[1]] = second
    return (place[0] * 2 + place[1]) * 2 + place[2]


def face_boxes(axis, at):
    return [box_id(axis, at, i, j) for i in range(2) for j in range(2)]


def split3(value):
    high = value.astype(BF16).astype(F32)
    rest = value - high
    mid = rest.astype(BF16).astype(F32)
    return high, mid, rest - mid


def row_ids(points):
    return lax.broadcasted_iota(jnp.int32, (8, points), 0)


def source_rows(pos, row):
    p1, p2, p3 = split3(pos)
    n1, n2, n3 = split3(1.0 + jnp.sum(pos * pos, axis=0, keepdims=True))
    s1 = jnp.where(row < 3, p1, jnp.where(row == 3, n1, jnp.where(row == 4, n2, jnp.where(row == 5, n3, 1.0))))
    s2 = p2 + pltpu.roll(p3, 3, 0)
    return jnp.concatenate([s1, s1, s2, s2, s1, jnp.zeros_like(s1)], axis=0).astype(BF16)


def target_rows(pos, row):
    p1, p2, p3 = split3(-2.0 * pos)
    m1, m2, m3 = split3(jnp.sum(pos * pos, axis=0, keepdims=True))
    qa = jnp.where(row < 3, p1, jnp.where(row < 6, 1.0, jnp.where(row == 6, m1, m2)))
    qb = jnp.where(row < 3, p2, jnp.where(row == 6, m3, 0.0))
    qc = p1 + pltpu.roll(p1, 3, 0)
    return jnp.concatenate([qa, qb, qc, p2, p3, jnp.zeros_like(qa)], axis=0).astype(BF16)


def prep_kernel(counts, offs, probes, pay, fa, fb, tab, mom, momf, f0, f1, f2, pad):
    points = offs.shape[-1]
    row = row_ids(points)
    lane = lax.broadcasted_iota(jnp.int32, (1, points), 1)
    faces = (f0, f1, f2)
    pay[BOXES] = jnp.zeros_like(pay[BOXES])
    for k in range(BOXES):
        place = (k // 4, k // 2 % 2, k % 2)
        pad[...] = jnp.zeros_like(pad)
        for d in range(3):
            pad[d:d + 1, :] = offs[place[0], place[1], d, place[2]:place[2] + 1, :]
        off = pad[...]
        shift = jnp.where(row == 0, place[0] - 1.0, jnp.where(row == 1, place[1] - 1.0, jnp.where(row == 2, place[2] - 1.0, 0.0)))
        pos = off + shift
        src = source_rows(pos, row)
        fa[k] = src
        fb[k] = target_rows(pos, row)
        if k == 0:
            fa[BOXES] = src
        count = counts[place]
        chunks = ((count + CHUNK - 1) // CHUNK).astype(F32)
        p1, p2, p3 = split3(pos)
        rows_a = jnp.where(row == 6, chunks, p1 + pltpu.roll(p2, 3, 0))
        tail = jnp.concatenate([rows_a, p3], axis=0).astype(BF16)
        vec = jnp.where(lane < count, probes[place].astype(F32), 0.0).astype(BF16)
        pay[k, 0:32, :] = vec
        pay[k, 32:48, :] = tail
        for axis in range(3):
            if place[axis] == 0:
                other = [d for d in range(3) if d != axis]
                slot = place[other[0]] * 2 + place[other[1]]
                faces[axis][slot, 0:32, :] = vec
                faces[axis][slot, 32:48, :] = tail
        unit = 2.0 * off - 1.0
        t2 = 2.0 * unit * unit - 1.0
        t3 = 2.0 * unit * t2 - unit
        weights = []
        for c in NODES:
            e2 = 2.0 * c * c - 1.0
            e3 = 2.0 * c * e2 - c
            weights.append(0.25 + 0.5 * (c * unit + e2 * t2 + e3 * t3))
        third = jnp.zeros_like(off)
        for d in range(ORDER):
            third = jnp.where(row % 4 == d, weights[d][2:3, :], third)
        seconds = []
        for half in range(2):
            seconds.append(jnp.where(row < 4, weights[2 * half][1:2, :], weights[2 * half + 1][1:2, :]))
        parts = []
        for a in range(ORDER):
            for half in range(2):
                parts.append(weights[a][0:1, :] * seconds[half] * third)
        table = jnp.concatenate(parts, axis=0).astype(BF16)
        tab[k] = table
        moment = lax.dot_general(table, vec, (((1,), (1,)), ((), ())), preferred_element_type=F32)
        momf[:, k * 32:(k + 1) * 32] = moment
    mom[...] = momf[...].astype(BF16)


WIDTHS = (768, 1024)
REGION = 160


def run_steps(targets, sources_of, chunks_of, width_of, dummy, fa, vec, fb, own, out, back, tiles, flips, steps, owner, filled):
    for c in range(len(WIDTHS)):
        filled[c] = 0
    for b in targets:
        count_b = width_of(b)
        kind = jnp.int32(0)
        for width in WIDTHS[:-1]:
            kind = kind + (count_b > width).astype(jnp.int32)
        base = kind * REGION
        at = base + filled[kind]
        for s in sources_of(b):
            for c in range(8):
                steps[at + c] = s * 8 + c
            for c in range(5):
                owner[(at >> 1) + c] = b
            at = at + chunks_of(s)
        steps[at] = dummy * 8
        at = at + (at & 1)
        filled[kind] = at - base
    for c in range(len(WIDTHS)):
        end = c * REGION + filled[c]
        for extra in range(8):
            steps[end + extra] = dummy * 8
            owner[(end + extra) >> 1] = targets[0]

    def columns(index):
        return pl.ds(pl.multiple_of((index & 7) * CHUNK, CHUNK), CHUNK)

    for c, width in enumerate(WIDTHS):
        first_step = c * (REGION // 2)
        total = filled[c] >> 1

        def flip(t, slot):
            for h in range(2):
                index = steps[2 * t + h]
                flips[slot, h * CHUNK:(h + 1) * CHUNK, :] = fa[index >> 3, :, columns(index)].T

        def make(t, slot, width=width):
            target = fb[owner[t], :, 0:width]
            squares = jnp.dot(flips[slot], target, preferred_element_type=F32)
            tiles[slot, :, 0:width] = lax.rsqrt(squares).astype(BF16)

        def use(t, slot, width=width):
            b = owner[t]
            first = steps[2 * t]
            second = steps[2 * t + 1]
            tile = tiles[slot, :, 0:width]
            both = jnp.concatenate([vec[first >> 3, 0:32, columns(first)], vec[second >> 3, 0:32, columns(second)]], axis=1)
            out[b, :, 0:width] += jnp.dot(both, tile, preferred_element_type=F32)
            if back is not None:
                sent = lax.dot_general(own[b, 0:32, 0:width], tile, (((1,), (1,)), ((), ())), preferred_element_type=F32)
                back[first >> 3, :, columns(first)] += sent[:, 0:CHUNK]
                back[second >> 3, :, columns(second)] += sent[:, CHUNK:]

        @pl.when(total > 0)
        def _(flip=flip, make=make, use=use, first_step=first_step, total=total):
            flip(first_step, 0)
            flip(first_step + 1, 1)
            make(first_step, 0)

            def body(k, carry):
                t = first_step + 2 * k
                make(t + 1, 1)
                flip(t + 2, 0)
                use(t, 0)
                make(t + 2, 0)
                flip(t + 3, 1)
                use(t + 1, 1)
                return carry

            lax.fori_loop(0, (total + 1) >> 1, body, 0)


INNER = {4: (0,), 2: (0,), 1: (0,), 6: (2, 4), 5: (1, 4), 3: (1, 2), 7: (3, 5, 6)}


def count_of(counts, k):
    return counts[k // 4, k // 2 % 2, k % 2]


def inner_kernel(targets, sources_of, two_way, counts, fa, pay, fb, acc_in, after, out, done, tiles, flips, steps, owner, filled):
    if acc_in is None:
        out[...] = jnp.zeros_like(out)
    else:
        out[...] = acc_in[...]
    run_steps(
        targets, sources_of, lambda s: (count_of(counts, s) + CHUNK - 1) >> 7, lambda b: count_of(counts, b), BOXES,
        fa, pay, fb, pay, out, out if two_way else None, tiles, flips, steps, owner, filled,
    )
    done[...] = jnp.zeros_like(done)


def outer_kernel(counts, fb, pay, acc_self, acc_in, after, halo0, halo1, halo2, near, b0, b1, b2, probe_sums,
                 fa, vec, plus, back, tiles, flips, steps, owner, filled, chunk_no):
    halos = (halo0, halo1, halo2)
    points = fb.shape[-1]
    row = row_ids(points)
    plus[...] = jnp.zeros_like(plus)
    back[...] = jnp.zeros_like(back)
    sources = {b: [] for b in range(BOXES)}
    spare = 12
    for axis in range(3):
        halo = halos[axis]
        name = ("gx", "gy", "gz")[axis]
        at_edge = lax.axis_index(name) == lax.axis_size(name) - 1
        targets = face_boxes(axis, 1)
        for i in range(4):
            s = axis * 4 + i
            sources[targets[i]].append(s)
            tail = halo[i, 32:48, :].astype(F32)
            rows_a = tail[0:8]
            pos = rows_a + pltpu.roll(rows_a, 5, 0) + tail[8:16]
            pos = jnp.where(row < 3, pos + jnp.where(row == axis, 2.0, 0.0), 0.0)
            feats = source_rows(pos, row)
            fa[s] = feats
            if s == 0:
                fa[spare] = feats
            vec[s] = halo[i, 0:32, :]
            chunk_no[s] = jnp.where(at_edge, 0, jnp.max(rows_a[6:7, 0:128]).astype(jnp.int32))
    vec[spare] = jnp.zeros_like(vec[spare])
    order = [b for b in range(BOXES) if sources[b]]
    run_steps(
        order, lambda b: sources[b], lambda s: chunk_no[s], lambda b: count_of(counts, b), spare,
        fa, vec, fb, pay, plus, back, tiles, flips, steps, owner, filled,
    )
    total = jnp.zeros((32, 128), F32)
    for b in range(BOXES):
        extra = plus[b]
        base = acc_self[b] + acc_in[b]
        near[b] = base + extra
        weighted = pay[b, 0:32, :].astype(F32) * (base + 2.0 * extra)
        for j in range(points // 128):
            total = total + weighted[:, j * 128:(j + 1) * 128]
    probe_sums[...] = total
    for axis, ref in enumerate((b0, b1, b2)):
        ref[...] = back[4 * axis:4 * axis + 4]


def local_kernel(counts, req_box, req_tgt, here, there, momf, probe_sums, loc, sums, slab, far_acc, live, sems):
    first_copy = pltpu.make_async_copy(here, slab.at[pl.ds(0, 32)], sems.at[0])
    second_copy = pltpu.make_async_copy(there, slab.at[pl.ds(32, 32)], sems.at[1])
    first_copy.start()
    second_copy.start()
    my_y = lax.axis_index("gy")
    my_z = lax.axis_index("gz")
    far_acc[...] = jnp.zeros_like(far_acc)

    def keep(i, n):
        live[n] = i
        return n + (req_box[i >> 6, i & 63] >= 0).astype(jnp.int32)

    used = lax.fori_loop(0, 128, keep, jnp.int32(0))
    shape = (64, 64)
    source_q = lax.broadcasted_iota(jnp.int32, shape, 1)
    target_q = lax.broadcasted_iota(jnp.int32, shape, 0)

    def node(index):
        value = jnp.full(shape, 0.5 + 0.5 * NODES[0], F32)
        for a in range(1, ORDER):
            value = jnp.where(index == a, 0.5 + 0.5 * NODES[a], value)
        return value

    gaps = [node((source_q >> s) & 3) - node((target_q >> s) & 3) for s in (4, 2, 0)]
    group = lax.broadcasted_iota(jnp.int32, (64, 256), 1) >> 5
    first_copy.wait()
    second_copy.wait()

    def step(g, carry):
        for u in range(8):
            k = g * 8 + u
            i = live[jnp.minimum(k, used - 1)]
            peer = i & 63
            box = req_box[i >> 6, peer]
            tgt = req_tgt[i >> 6, peer]
            peer_y = peer >> 4
            peer_z = peer & 15
            dx = (box >> 2) - (tgt >> 2)
            dy = (peer_y - my_y) * 2 + ((box >> 1) & 1) - ((tgt >> 1) & 1)
            dz = (peer_z - my_z) * 2 + (box & 1) - (tgt & 1)
            ex = gaps[0] + dx.astype(F32)
            ey = gaps[1] + dy.astype(F32)
            ez = gaps[2] + dz.astype(F32)
            coupling = lax.rsqrt(1.0 + ex * ex + ey * ey + ez * ez).astype(BF16)
            rel_y = peer_y ^ my_y
            rel_z = peer_z ^ my_z
            at = (rel_z & 1) * 32 + ((rel_z >> 1) & 3) * 8 + rel_y * 2 + (rel_z >> 3)
            term = jnp.dot(coupling, slab[at], preferred_element_type=F32)
            wanted = jnp.where(k < used, box, -1)
            far_acc[tgt] += jnp.where(group == wanted, term, 0.0)
        return carry

    lax.fori_loop(0, (used + 7) >> 3, step, 0)
    lane = lax.broadcasted_iota(jnp.int32, (64, 128), 1)
    far_sums = jnp.zeros((64, 128), F32)
    live_points = jnp.int32(0)
    for b in range(BOXES):
        wide = far_acc[b]
        half = wide[:, 0:128] + wide[:, 128:256]
        half = half + pltpu.roll(half, 64, 1)
        half = half + pltpu.roll(half, 32, 1)
        rounded = half.astype(BF16)
        loc[b] = rounded
        moment = momf[:, (b // 4) * 128:(b // 4 + 1) * 128]
        far_sums = far_sums + jnp.where((lane >> 5) == b % 4, rounded.astype(F32) * moment, 0.0)
        live_points = live_points + count_of(counts, b)
    folded = jnp.sum(far_sums, axis=0, keepdims=True)
    folded = folded + pltpu.roll(folded, 64, 1)
    folded = folded + pltpu.roll(folded, 32, 1)
    lane32 = lax.broadcasted_iota(jnp.int32, (32, 128), 1)
    row32 = lax.broadcasted_iota(jnp.int32, (32, 128), 0)
    per_probe = jnp.sum(probe_sums[...], axis=1, keepdims=True)
    flat = jnp.sum(jnp.where(lane32 == row32, per_probe, 0.0), axis=0, keepdims=True)
    row_sums = jnp.where(lane32[0:1] < 32, flat + folded, jnp.where(lane32[0:1] == 32, live_points.astype(F32), 0.0))
    sums[...] = jnp.broadcast_to(row_sums.reshape(1, 1, 128), sums.shape)


def total_kernel(counts, near, r2, r0, r1, loc, tab, kv, done):
    points = tab.shape[-1]
    lane = lax.broadcasted_iota(jnp.int32, (1, points), 1)
    for b in range(BOXES):
        place = (b // 4, b // 2 % 2, b % 2)
        far = lax.dot_general(loc[b][:, 0:32], tab[b], (((0,), (0,)), ((), ())), preferred_element_type=F32)
        total = near[b] + far
        for axis, ref in enumerate((r0, r1, r2)):
            if place[axis] == 0:
                other = [d for d in range(3) if d != axis]
                total = total + ref[place[other[0]] * 2 + place[other[1]]]
        if b == 0:
            done[...] = jnp.zeros_like(done)
        kv[b] = jnp.where(lane < count_of(counts, b), total * (1.0 / math.sqrt(7.0 * points)), 0.0).astype(BF16)


def quad_kernel(gathered, after, quad):
    lane = lax.broadcasted_iota(jnp.int32, (1, 128), 1)
    whole = jnp.sum(gathered[...], axis=0)
    live_points = jnp.sum(jnp.where(lane == 32, whole, 0.0), axis=1, keepdims=True)
    scaled = whole * (1.0 / math.sqrt(7.0 * 1024)) / live_points
    quad[...] = scaled[0, 0:32]


VMEM = pl.BlockSpec(memory_space=pltpu.VMEM)
SMEM = pl.BlockSpec(memory_space=pltpu.SMEM)
ANY = pl.BlockSpec(memory_space=pl.ANY)
PARAMS = pltpu.CompilerParams(vmem_limit_bytes=20 * 2**20)


COST = pl.CostEstimate(flops=12 * 10**9, bytes_accessed=4 * 2**20, transcendentals=10**7)


def join(name, *arrays):
    return pl.pallas_call(
        lambda *refs: None,
        out_shape=[jax.ShapeDtypeStruct(a.shape, a.dtype) for a in arrays],
        in_specs=[ANY] * len(arrays),
        out_specs=[ANY] * len(arrays),
        input_output_aliases={i: i for i in range(len(arrays))},
        compiler_params=pltpu.CompilerParams(vmem_limit_bytes=2**20),
        name=name,
    )(*arrays)


def xor_permute(value, axis, bits):
    count = lax.axis_size(axis)
    return lax.ppermute(value, axis, [(i, i ^ bits) for i in range(count)])


def shards(offsets, probes, counts, req_box, req_tgt):
    points = offsets.shape[-1]
    shape = jax.ShapeDtypeStruct
    face = shape((4, ROWS, points), BF16)
    pay, fa, fb, tab, mom, momf, *faces = pl.pallas_call(
        prep_kernel,
        out_shape=[
            shape((BOXES + 1, ROWS, points), BF16),
            shape((BOXES + 1, FEATS, points), BF16),
            shape((BOXES, FEATS, points), BF16),
            shape((BOXES, 64, points), BF16),
            shape((64, 256), BF16),
            shape((64, 256), F32),
        ] + [face] * 3,
        in_specs=[SMEM, VMEM, VMEM],
        out_specs=[VMEM] * 9,
        scratch_shapes=[
            pltpu.VMEM((8, points), F32),
        ],
        compiler_params=PARAMS,
        name="prep",
    )(counts, jnp.swapaxes(offsets, 2, 3), probes)

    acc_shape = shape((BOXES, 32, points), F32)
    lists = [
        pltpu.VMEM((2, 2 * CHUNK, points), BF16),
        pltpu.VMEM((2, 2 * CHUNK, FEATS), BF16),
        pltpu.SMEM((len(WIDTHS) * REGION,), jnp.int32),
        pltpu.SMEM((len(WIDTHS) * REGION // 2,), jnp.int32),
        pltpu.SMEM((8,), jnp.int32),
    ]

    def inner(name, targets, sources_of, two_way, acc, after):
        has_acc = acc is not None

        def kernel(*refs):
            refs = list(refs)
            head = refs[:4]
            rest = refs[4:]
            acc_ref = rest.pop(0) if has_acc else None
            inner_kernel(targets, sources_of, two_way, *head, acc_ref, *rest)

        args = [counts, fa, pay, fb] + ([acc] if has_acc else []) + [after]
        return pl.pallas_call(
            kernel,
            out_shape=[shape((BOXES + 1, 32, points), F32), shape((8, 128), F32)],
            in_specs=[SMEM, VMEM, VMEM, VMEM] + [VMEM] * has_acc + [ANY],
            out_specs=[VMEM, VMEM],
            scratch_shapes=lists,
            compiler_params=PARAMS,
            cost_estimate=COST,
            name=name,
        )(*args)

    def along(axis, value, step):
        name = ("gx", "gy", "gz")[axis]
        size = lax.axis_size(name)
        return lax.ppermute(value, name, [(i, (i + step) % size) for i in range(size)])

    block = mom.reshape(1, 64, 256)
    twin = xor_permute(block, "gz", 8)
    got = [None] * 3
    for axis in (2, 0, 1):
        got[axis] = along(axis, faces[axis], -1)
    acc_self, tick = inner("self_tiles", list(range(BOXES)), lambda b: [b], False, None, mom)
    tick, twin, got[0], got[1] = join("join_first", tick, twin, got[0], got[1])
    block = jnp.concatenate([block, twin], axis=0)
    more = [xor_permute(block, "gy", k) for k in (1, 2, 3)]
    acc, tick = inner("pairs_low", [1, 2, 4, 3], lambda b: INNER[b], True, None, tick)
    tick, got[2], *more = join("join_second", tick, got[2], *more)
    block = jnp.concatenate([block] + more, axis=0)
    more = [xor_permute(block, "gz", 2 * k) for k in (1, 2, 3)]
    acc, tick = inner("pairs_high", [5, 6, 7], lambda b: INNER[b], True, acc, tick)
    tick, *more = join("join_third", tick, *more)
    block = jnp.concatenate([block] + more, axis=0)
    other = xor_permute(block, "gz", 1)
    near, *backs, probe_sums = pl.pallas_call(
        outer_kernel,
        out_shape=[acc_shape] + [shape((4, 32, points), F32)] * 3 + [shape((32, 128), F32)],
        in_specs=[SMEM, VMEM, VMEM, VMEM, VMEM, ANY, VMEM, VMEM, VMEM],
        out_specs=[VMEM] * 5,
        scratch_shapes=[
            pltpu.VMEM((13, FEATS, points), BF16),
            pltpu.VMEM((13, 32, points), BF16),
            pltpu.VMEM((BOXES, 32, points), F32),
            pltpu.VMEM((13, 32, points), F32),
        ] + lists + [pltpu.SMEM((16,), jnp.int32)],
        compiler_params=PARAMS,
        cost_estimate=COST,
        name="face_tiles",
    )(counts, fb, pay, acc_self, acc, tick, *got)
    returned = [None] * 3
    for axis in (2, 0, 1):
        returned[axis] = along(axis, backs[axis], 1)
    devices = lax.axis_size("gx") * lax.axis_size("gy") * lax.axis_size("gz")
    loc, sums = pl.pallas_call(
        local_kernel,
        out_shape=[shape((BOXES, 64, 128), BF16), shape((devices, 1, 128), F32)],
        in_specs=[SMEM, SMEM, SMEM, ANY, ANY, VMEM, VMEM],
        out_specs=[VMEM, VMEM],
        scratch_shapes=[
            pltpu.VMEM((64, 64, 256), BF16),
            pltpu.VMEM((BOXES, 64, 256), F32),
            pltpu.SMEM((136,), jnp.int32),
            pltpu.SemaphoreType.DMA((2,)),
        ],
        compiler_params=PARAMS,
        name="locals",
    )(counts, *[jnp.swapaxes(r, 3, 4).reshape(2, 64) for r in (req_box, req_tgt)], block, other, momf, probe_sums)
    gathered = lax.all_to_all(sums, ("gx", "gy", "gz"), 0, 0, tiled=True)
    kv, total_tick = pl.pallas_call(
        total_kernel,
        out_shape=[shape((BOXES, 32, points), BF16), shape((8, 128), F32)],
        in_specs=[SMEM] + [VMEM] * 6,
        out_specs=[VMEM, VMEM],
        compiler_params=PARAMS,
        cost_estimate=COST,
        name="total",
    )(counts, near, returned[2], returned[0], returned[1], loc, tab)
    quad = pl.pallas_call(
        quad_kernel,
        out_shape=shape((32,), F32),
        in_specs=[VMEM, ANY],
        out_specs=VMEM,
        compiler_params=pltpu.CompilerParams(vmem_limit_bytes=2**21),
        name="quad",
    )(gathered, total_tick)
    return kv.reshape(probes.shape), quad


def solution(mesh):
    placed = (
        P("gx", "gy", "gz", None, None),
        P("gx", "gy", "gz", None, None),
        P("gx", "gy", "gz"),
        P("gx", "gy", "gz", None, None),
        P("gx", "gy", "gz", None, None),
    )
    return jax.shard_map(
        shards,
        mesh=mesh,
        in_specs=placed,
        out_specs=(P("gx", "gy", "gz", None, None), P()),
        check_vma=False,
    )
```

profile of v0, /device:TPU:1, one launch (start us, length us, event | category | flops | bytes accessed | tf_op | source)
XLA Modules:
  0.0 107.8 jit_solution(2217637024965775254)
XLA Ops:
  0.6 1.0 copy-done
  1.7 0.9 copy-done.1
  2.6 0.7 copy-done.2
  3.2 2.2 %prep.1 = (bf16[9,48,1024]{2,1,0:T(8,128)(2,1)S(1)}, bf16[9,48,1024]{2,1,0:T(8,128)(2,1)S(1)}, bf16[8,48,1024]{2,1,0:T(8,128)(2,1)S(1)}, bf16[8,64,1024]{2,1,0:T...) custom-call(s32[2,2,2]{2,1,0:T(2,128)S(1)} %copy-done.2, ...), custom_call_target="tpu_custom_call" | custom-call | tf_op jit(solution)/shard_map/prep/pallas_call | solution.py:394
  5.4 7.8 %collective-permute-start = (bf16[1,64,256]{2,1,0:T(8,128)(2,1)S(1)}, bf16[1,64,256]{2,1,0:T(8,128)(2,1)S(1)}, u32[]{:S(2)}, u32[]{:S(2)}) collective-permute-start(bf16[1,64,256]{2,1,0:T(8,128)(2,1)S(1)} %bitcast.11), channel_id=1, source_target_pairs={{0,8},{1,9},{2,10},{3,11},{4,12},{5,13},{6,14},{7,15},{8,0},{9,1},... | collective-permute-start | bytes 98312 | tf_op jit(solution)/shard_map/ppermute | solution.py:387
  13.2 2.7 %collective-permute-start.1 = (bf16[4,48,1024]{2,1,0:T(8,128)(2,1)S(1)}, bf16[4,48,1024]{2,1,0:T(8,128)(2,1)S(1)}, u32[]{:S(2)}, u32[]{:S(2)}) collective-permute-start(bf16[4,48,1024]{2,1,0:T(8,128)(2,1)S(1)} %get-tuple-element.45), channel_id=1, source_target_pairs={{0,192},{64,0},{128,64},{192,128},{1,193},{65,1},{129,65},{193,129... | collective-permute-start | bytes 1179656 | tf_op jit(solution)/shard_map/ppermute | solution.py:447
  16.0 1.6 %collective-permute-start.2 = (bf16[4,48,1024]{2,1,0:T(8,128)(2,1)S(1)}, bf16[4,48,1024]{2,1,0:T(8,128)(2,1)S(1)}, u32[]{:S(2)}, u32[]{:S(2)}) collective-permute-start(bf16[4,48,1024]{2,1,0:T(8,128)(2,1)S(1)} %get-tuple-element.46), channel_id=1, source_target_pairs={{0,48},{16,0},{32,16},{48,32},{1,49},{17,1},{33,17},{49,33},{2,50}... | collective-permute-start | bytes 1179656 | tf_op jit(solution)/shard_map/ppermute | solution.py:447
  17.6 1.5 %collective-permute-start.3 = (bf16[4,48,1024]{2,1,0:T(8,128)(2,1)S(1)}, bf16[4,48,1024]{2,1,0:T(8,128)(2,1)S(1)}, u32[]{:S(2)}, u32[]{:S(2)}) collective-permute-start(bf16[4,48,1024]{2,1,0:T(8,128)(2,1)S(1)} %get-tuple-element.50), channel_id=1, source_target_pairs={{0,15},{1,0},{2,1},{3,2},{4,3},{5,4},{6,5},{7,6},{8,7},{9,8},{10,9... | collective-permute-start | bytes 1179656 | tf_op jit(solution)/shard_map/ppermute | solution.py:447
  19.1 8.3 %self_tiles.1 = (f32[9,32,1024]{2,1,0:T(8,128)S(1)}, f32[8,128]{1,0:T(8,128)S(1)}) custom-call(s32[2,2,2]{2,1,0:T(2,128)S(1)} %copy-done.2, bf16[9,48,1024]{2,1,0:T(8,128)(2,1)S(1)} %get-tuple-element.41.refs_1_, bf16[9,48,1024]{2,1,0:T(8,128)(2,1)S(1)} %get-tuple-element.40.refs_2_.pay, bf16[8,48,1024]{2,1,0:T(8,128)(2,1)S(1)} %get-tuple-element.39.refs_3_.fb, ...), custom_call_target="tpu_custom_call" | custom-call | flops 12000000000 | bytes 4194304 | tf_op jit(solution)/shard_map/self_tiles/pallas_call | solution.py:433
  27.5 1.4 %collective-permute-start.6 = (bf16[2,64,256]{2,1,0:T(8,128)(2,1)S(1)}, bf16[2,64,256]{2,1,0:T(8,128)(2,1)S(1)}, u32[]{:S(2)}, u32[]{:S(2)}) collective-permute-start(bf16[2,64,256]{2,1,0:T(8,128)(2,1)S(1)} %pad_maximum_fusion), channel_id=1, source_target_pairs={{0,48},{16,32},{32,16},{48,0},{1,49},{17,33},{33,17},{49,1},{2,50}... | collective-permute-start | bytes 196616 | tf_op jit(solution)/shard_map/ppermute | solution.py:387
  29.3 1.9 %collective-permute-start.4 = (bf16[2,64,256]{2,1,0:T(8,128)(2,1)S(1)}, bf16[2,64,256]{2,1,0:T(8,128)(2,1)S(1)}, u32[]{:S(2)}, u32[]{:S(2)}) collective-permute-start(bf16[2,64,256]{2,1,0:T(8,128)(2,1)S(1)} %pad_maximum_fusion), channel_id=1, source_target_pairs={{0,16},{16,0},{32,48},{48,32},{1,17},{17,1},{33,49},{49,33},{2,18}... | collective-permute-start | bytes 196616 | tf_op jit(solution)/shard_map/ppermute | solution.py:387
  31.2 7.6 %pairs_low.1 = (f32[9,32,1024]{2,1,0:T(8,128)S(1)}, f32[8,128]{1,0:T(8,128)S(1)}) custom-call(s32[2,2,2]{2,1,0:T(2,128)S(1)} %copy-done.2, bf16[9,48,1024]{2,1,0:T(8,128)(2,1)S(1)} %get-tuple-element.41.refs_1_, bf16[9,48,1024]{2,1,0:T(8,128)(2,1)S(1)} %get-tuple-element.40.refs_2_.pay, bf16[8,48,1024]{2,1,0:T(8,128)(2,1)S(1)} %get-tuple-element.39.refs_3_.fb, ...), custom_call_target="tpu_custom_call" | custom-call | flops 12000000000 | bytes 4194304 | tf_op jit(solution)/shard_map/pairs_low/pallas_call | solution.py:433
  38.9 3.1 %collective-permute-done.5.refs_3_ = bf16[2,64,256]{2,1,0:T(8,128)(2,1)S(1)} collective-permute-done((bf16[2,64,256]{2,1,0:T(8,128)(2,1)S(1)}, bf16[2,64,256]{2,1,0:T(8,128)(2,1)S(1)}, u32[]{:S(2)}, u32[]{:S(2)}) %collective-permute-start.5) | collective-permute-done | bytes 65568 | tf_op jit(solution)/shard_map/ppermute | solution.py:387
  42.2 3.1 %collective-permute-start.7 = (bf16[8,64,256]{2,1,0:T(8,128)(2,1)S(1)}, bf16[8,64,256]{2,1,0:T(8,128)(2,1)S(1)}, u32[]{:S(2)}, u32[]{:S(2)}) collective-permute-start(bf16[8,64,256]{2,1,0:T(8,128)(2,1)S(1)} %get-tuple-element.77), channel_id=1, source_target_pairs={{0,2},{1,3},{2,0},{3,1},{4,6},{5,7},{6,4},{7,5},{8,10},{9,11},{10,... | collective-permute-start | bytes 786440 | tf_op jit(solution)/shard_map/ppermute | solution.py:387
  45.4 10.1 %pairs_high.1 = (f32[9,32,1024]{2,1,0:T(8,128)S(1)}, f32[8,128]{1,0:T(8,128)S(1)}) custom-call(s32[2,2,2]{2,1,0:T(2,128)S(1)} %copy-done.2, bf16[9,48,1024]{2,1,0:T(8,128)(2,1)S(1)} %get-tuple-element.41.refs_1_, bf16[9,48,1024]{2,1,0:T(8,128)(2,1)S(1)} %get-tuple-element.40.refs_2_.pay, bf16[8,48,1024]{2,1,0:T(8,128)(2,1)S(1)} %get-tuple-element.39.refs_3_.fb, ...), custom_call_target="tpu_custom_call" | custom-call | flops 12000000000 | bytes 4194304 | tf_op jit(solution)/shard_map/pairs_high/pallas_call | solution.py:433
  55.4 1.3 %collective-permute-done.9.refs_3_ = bf16[8,64,256]{2,1,0:T(8,128)(2,1)S(1)} collective-permute-done((bf16[8,64,256]{2,1,0:T(8,128)(2,1)S(1)}, bf16[8,64,256]{2,1,0:T(8,128)(2,1)S(1)}, u32[]{:S(2)}, u32[]{:S(2)}) %collective-permute-start.9) | collective-permute-done | bytes 262176 | tf_op jit(solution)/shard_map/ppermute | solution.py:387
  56.8 1.7 %collective-permute-start.13 = (bf16[32,64,256]{2,1,0:T(8,128)(2,1)S(1)}, bf16[32,64,256]{2,1,0:T(8,128)(2,1)S(1)}, u32[]{:S(2)}, u32[]{:S(2)}) collective-permute-start(bf16[32,64,256]{2,1,0:T(8,128)(2,1)S(1)} %constant_dynamic-update-slice_fusion.5.here), channel_id=1, source_target_pairs={{0,1},{1,0},{2,3},{3,2},{4,5},{5,4},{6,7},{7,6},{8,9},{9,8},{10,11... | collective-permute-start | bytes 3145736 | tf_op jit(solution)/shard_map/ppermute | solution.py:387
  58.5 19.0 %face_tiles.1 = (f32[8,32,1024]{2,1,0:T(8,128)S(1)}, f32[4,32,1024]{2,1,0:T(8,128)S(1)}, f32[4,32,1024]{2,1,0:T(8,128)S(1)}, f32[4,32,1024]{2,1,0:T(8,128)}, f32[32,128]{1,0:T(8,128)S(1)}) custom-call(s32[2,2,2]{2,1,0:T(2,128)S(1)} %copy-done.2, bf16[8,48,1024]{2,1,0:T(8,128)(2,1)S(1)} %get-tuple-element.39.refs_3_.fb, ...), custom_call_target="tpu_custom_call" | custom-call | flops 12000000000 | bytes 4194304 | tf_op jit(solution)/shard_map/face_tiles/pallas_call | solution.py:466
  77.6 5.4 %locals.1 = (bf16[8,64,128]{2,1,0:T(8,128)(2,1)S(1)}, f32[256,1,128]{2,1,0:T(1,128)}) custom-call(s32[2,2,2]{2,1,0:T(2,128)S(1)} %copy-done.2, s32[2,64]{1,0:T(2,128)S(1)} %bitcast.14, s32[2,64]{1,0:T(2,128)S(1)} %bitcast.15, bf16[32,64,256]{2,1,0:T(8,128)(2,1)S(1)} %constant_dynamic-update-slice_fusion.5.here, ...), custom_call_target="tpu_custom_call" | custom-call | tf_op jit(solution)/shard_map/locals/pallas_call | solution.py:485
  83.0 10.9 %all-to-all-start = ((f32[256,1,128]{2,1,0:T(1,128)}), f32[256,1,128]{2,1,0:T(1,128)S(1)}, u32[]{:S(2)}, u32[]{:S(2)}) async-start(f32[256,1,128]{2,1,0:T(1,128)} %get-tuple-element.74), calls=%async_computation | async-start | bytes 262144 | tf_op jit(solution)/shard_map/all_to_all | solution.py:499
  94.0 1.2 %copy-done.7 = f32[8,32,1024]{2,1,0:T(8,128)S(1)} copy-done((f32[8,32,1024]{2,1,0:T(8,128)S(1)}, f32[8,32,1024]{2,1,0:T(8,128)}, u32[]{:S(2)}) %copy-start.7) | copy-done | bytes 1048600
  95.2 2.3 %total.1 = (bf16[8,32,1024]{2,1,0:T(8,128)(2,1)}, f32[8,128]{1,0:T(8,128)S(1)}) custom-call(s32[2,2,2]{2,1,0:T(2,128)S(1)} %copy-done.3, f32[8,32,1024]{2,1,0:T(8,128)S(1)} %copy-done.7, f32[4,32,1024]{2,1,0:T(8,128)S(1)} %collective-permute-done.10.r2, f32[4,32,1024]{2,1,0:T(8,128)S(1)} %collective-permute-done.11.r0, ...), custom_call_target="tpu_custom_call" | custom-call | flops 12000000000 | bytes 4194304 | tf_op jit(solution)/shard_map/total/pallas_call | solution.py:500
  97.5 9.5 %all-to-all-done.gathered = f32[256,1,128]{2,1,0:T(1,128)S(1)} async-done(((f32[256,1,128]{2,1,0:T(1,128)}), f32[256,1,128]{2,1,0:T(1,128)S(1)}, u32[]{:S(2)}, u32[]{:S(2)}) %all-to-all-start) | async-done | bytes 131104 | tf_op jit(solution)/shard_map/all_to_all | solution.py:499
  107.0 0.9 quad.1
  (42 shorter events, 0.8 us)
Async XLA Ops:
  0.6 1.0 copy-start
  1.7 0.9 copy-start.1
  2.6 0.7 copy-start.2
  5.4 22.1 %collective-permute-start = (bf16[1,64,256]{2,1,0:T(8,128)(2,1)S(1)}, bf16[1,64,256]{2,1,0:T(8,128)(2,1)S(1)}, u32[]{:S(2)}, u32[]{:S(2)}) collective-permute-start(bf16[1,64,256]{2,1,0:T(8,128)(2,1)S(1)} %bitcast.11), channel_id=1, source_target_pairs={{0,8},{1,9},{2,10},{3,11},{4,12},{5,13},{6,14},{7,15},{8,0},{9,1},... | collective-permute-start | bytes 98312 | tf_op jit(solution)/shard_map/ppermute | solution.py:387
  13.2 14.3 %collective-permute-start.1 = (bf16[4,48,1024]{2,1,0:T(8,128)(2,1)S(1)}, bf16[4,48,1024]{2,1,0:T(8,128)(2,1)S(1)}, u32[]{:S(2)}, u32[]{:S(2)}) collective-permute-start(bf16[4,48,1024]{2,1,0:T(8,128)(2,1)S(1)} %get-tuple-element.45), channel_id=1, source_target_pairs={{0,192},{64,0},{128,64},{192,128},{1,193},{65,1},{129,65},{193,129... | collective-permute-start | bytes 1179656 | tf_op jit(solution)/shard_map/ppermute | solution.py:447
  16.0 11.5 %collective-permute-start.2 = (bf16[4,48,1024]{2,1,0:T(8,128)(2,1)S(1)}, bf16[4,48,1024]{2,1,0:T(8,128)(2,1)S(1)}, u32[]{:S(2)}, u32[]{:S(2)}) collective-permute-start(bf16[4,48,1024]{2,1,0:T(8,128)(2,1)S(1)} %get-tuple-element.46), channel_id=1, source_target_pairs={{0,48},{16,0},{32,16},{48,32},{1,49},{17,1},{33,17},{49,33},{2,50}... | collective-permute-start | bytes 1179656 | tf_op jit(solution)/shard_map/ppermute | solution.py:447
  17.6 21.2 %collective-permute-start.3 = (bf16[4,48,1024]{2,1,0:T(8,128)(2,1)S(1)}, bf16[4,48,1024]{2,1,0:T(8,128)(2,1)S(1)}, u32[]{:S(2)}, u32[]{:S(2)}) collective-permute-start(bf16[4,48,1024]{2,1,0:T(8,128)(2,1)S(1)} %get-tuple-element.50), channel_id=1, source_target_pairs={{0,15},{1,0},{2,1},{3,2},{4,3},{5,4},{6,5},{7,6},{8,7},{9,8},{10,9... | collective-permute-start | bytes 1179656 | tf_op jit(solution)/shard_map/ppermute | solution.py:447
  27.5 11.3 %collective-permute-start.6 = (bf16[2,64,256]{2,1,0:T(8,128)(2,1)S(1)}, bf16[2,64,256]{2,1,0:T(8,128)(2,1)S(1)}, u32[]{:S(2)}, u32[]{:S(2)}) collective-permute-start(bf16[2,64,256]{2,1,0:T(8,128)(2,1)S(1)} %pad_maximum_fusion), channel_id=1, source_target_pairs={{0,48},{16,32},{32,16},{48,0},{1,49},{17,33},{33,17},{49,1},{2,50}... | collective-permute-start | bytes 196616 | tf_op jit(solution)/shard_map/ppermute | solution.py:387
  29.0 13.0 %collective-permute-start.5 = (bf16[2,64,256]{2,1,0:T(8,128)(2,1)S(1)}, bf16[2,64,256]{2,1,0:T(8,128)(2,1)S(1)}, u32[]{:S(2)}, u32[]{:S(2)}) collective-permute-start(bf16[2,64,256]{2,1,0:T(8,128)(2,1)S(1)} %pad_maximum_fusion), channel_id=1, source_target_pairs={{0,32},{16,48},{32,0},{48,16},{1,33},{17,49},{33,1},{49,17},{2,34}... | collective-permute-start | bytes 196616 | tf_op jit(solution)/shard_map/ppermute | solution.py:387
  29.3 12.7 %collective-permute-start.4 = (bf16[2,64,256]{2,1,0:T(8,128)(2,1)S(1)}, bf16[2,64,256]{2,1,0:T(8,128)(2,1)S(1)}, u32[]{:S(2)}, u32[]{:S(2)}) collective-permute-start(bf16[2,64,256]{2,1,0:T(8,128)(2,1)S(1)} %pad_maximum_fusion), channel_id=1, source_target_pairs={{0,16},{16,0},{32,48},{48,32},{1,17},{17,1},{33,49},{49,33},{2,18}... | collective-permute-start | bytes 196616 | tf_op jit(solution)/shard_map/ppermute | solution.py:387
  42.0 14.7 %collective-permute-start.9 = (bf16[8,64,256]{2,1,0:T(8,128)(2,1)S(1)}, bf16[8,64,256]{2,1,0:T(8,128)(2,1)S(1)}, u32[]{:S(2)}, u32[]{:S(2)}) collective-permute-start(bf16[8,64,256]{2,1,0:T(8,128)(2,1)S(1)} %get-tuple-element.77), channel_id=1, source_target_pairs={{0,6},{1,7},{2,4},{3,5},{4,2},{5,3},{6,0},{7,1},{8,14},{9,15},{10,... | collective-permute-start | bytes 786440 | tf_op jit(solution)/shard_map/ppermute | solution.py:387
  42.1 14.6 %collective-permute-start.8 = (bf16[8,64,256]{2,1,0:T(8,128)(2,1)S(1)}, bf16[8,64,256]{2,1,0:T(8,128)(2,1)S(1)}, u32[]{:S(2)}, u32[]{:S(2)}) collective-permute-start(bf16[8,64,256]{2,1,0:T(8,128)(2,1)S(1)} %get-tuple-element.77), channel_id=1, source_target_pairs={{0,4},{1,5},{2,6},{3,7},{4,0},{5,1},{6,2},{7,3},{8,12},{9,13},{10,... | collective-permute-start | bytes 786440 | tf_op jit(solution)/shard_map/ppermute | solution.py:387
  42.2 14.5 %collective-permute-start.7 = (bf16[8,64,256]{2,1,0:T(8,128)(2,1)S(1)}, bf16[8,64,256]{2,1,0:T(8,128)(2,1)S(1)}, u32[]{:S(2)}, u32[]{:S(2)}) collective-permute-start(bf16[8,64,256]{2,1,0:T(8,128)(2,1)S(1)} %get-tuple-element.77), channel_id=1, source_target_pairs={{0,2},{1,3},{2,0},{3,1},{4,6},{5,7},{6,4},{7,5},{8,10},{9,11},{10,... | collective-permute-start | bytes 786440 | tf_op jit(solution)/shard_map/ppermute | solution.py:387
  56.8 20.7 %collective-permute-start.13 = (bf16[32,64,256]{2,1,0:T(8,128)(2,1)S(1)}, bf16[32,64,256]{2,1,0:T(8,128)(2,1)S(1)}, u32[]{:S(2)}, u32[]{:S(2)}) collective-permute-start(bf16[32,64,256]{2,1,0:T(8,128)(2,1)S(1)} %constant_dynamic-update-slice_fusion.5.here), channel_id=1, source_target_pairs={{0,1},{1,0},{2,3},{3,2},{4,5},{5,4},{6,7},{7,6},{8,9},{9,8},{10,11... | collective-permute-start | bytes 3145736 | tf_op jit(solution)/shard_map/ppermute | solution.py:387
  58.4 19.1 %copy-start.4 = (s32[1,1,1,64,2]{3,4,2,1,0:T(2,128)S(1)}, s32[1,1,1,64,2]{3,4,2,1,0:T(2,128)}, u32[]{:S(2)}) copy-start(s32[1,1,1,64,2]{3,4,2,1,0:T(2,128)} %param.8) | copy-start | bytes 1540
  58.5 19.1 %copy-start.5 = (s32[1,1,1,64,2]{3,4,2,1,0:T(2,128)S(1)}, s32[1,1,1,64,2]{3,4,2,1,0:T(2,128)}, u32[]{:S(2)}) copy-start(s32[1,1,1,64,2]{3,4,2,1,0:T(2,128)} %param.9) | copy-start | bytes 1540
  77.4 5.6 %copy-start.6 = (f32[8,32,1024]{2,1,0:T(8,128)}, f32[8,32,1024]{2,1,0:T(8,128)S(1)}, u32[]{:S(2)}) copy-start(f32[8,32,1024]{2,1,0:T(8,128)S(1)} %get-tuple-element.62.near) | copy-start | bytes 3145732
  77.4 16.5 %collective-permute-start.10 = (f32[4,32,1024]{2,1,0:T(8,128)}, f32[4,32,1024]{2,1,0:T(8,128)S(1)}, u32[]{:S(2)}, u32[]{:S(2)}) collective-permute-start(f32[4,32,1024]{2,1,0:T(8,128)} %get-tuple-element.63), channel_id=1, source_target_pairs={{0,1},{1,2},{2,3},{3,4},{4,5},{5,6},{6,7},{7,8},{8,9},{9,10},{10,1... | collective-permute-start | bytes 1572872 | tf_op jit(solution)/shard_map/ppermute | solution.py:447
  77.4 16.6 %collective-permute-start.11 = (f32[4,32,1024]{2,1,0:T(8,128)S(1)}, f32[4,32,1024]{2,1,0:T(8,128)S(1)}, u32[]{:S(2)}, u32[]{:S(2)}) collective-permute-start(f32[4,32,1024]{2,1,0:T(8,128)S(1)} %get-tuple-element.64), channel_id=1, source_target_pairs={{0,64},{64,128},{128,192},{192,0},{1,65},{65,129},{129,193},{193,1... | collective-permute-start | bytes 1572872 | tf_op jit(solution)/shard_map/ppermute | solution.py:447
  77.4 16.6 %collective-permute-start.12 = (f32[4,32,1024]{2,1,0:T(8,128)S(1)}, f32[4,32,1024]{2,1,0:T(8,128)}, u32[]{:S(2)}, u32[]{:S(2)}) collective-permute-start(f32[4,32,1024]{2,1,0:T(8,128)S(1)} %get-tuple-element.65), channel_id=1, source_target_pairs={{0,16},{16,32},{32,48},{48,0},{1,17},{17,33},{33,49},{49,1},{2,18}... | collective-permute-start | bytes 1572872 | tf_op jit(solution)/shard_map/ppermute | solution.py:447
  77.5 16.4 %copy-start.3 = (s32[2,2,2]{2,1,0:T(2,128)S(1)}, s32[2,2,2]{2,1,0:T(2,128)}, u32[]{:S(2)}) copy-start(s32[2,2,2]{2,1,0:T(2,128)} %counts.7) | copy-start | bytes 100
  83.0 24.0 %all-to-all-start = ((f32[256,1,128]{2,1,0:T(1,128)}), f32[256,1,128]{2,1,0:T(1,128)S(1)}, u32[]{:S(2)}, u32[]{:S(2)}) async-start(f32[256,1,128]{2,1,0:T(1,128)} %get-tuple-element.74), calls=%async_computation | async-start | bytes 262144 | tf_op jit(solution)/shard_map/all_to_all | solution.py:499
  94.0 1.2 %copy-start.7 = (f32[8,32,1024]{2,1,0:T(8,128)S(1)}, f32[8,32,1024]{2,1,0:T(8,128)}, u32[]{:S(2)}) copy-start(f32[8,32,1024]{2,1,0:T(8,128)} %copy-done.6) | copy-start | bytes 3145732
where the time goes:
time: 109 us; the launch traced here: 108 us
  Pallas kernels  55.7 us (51%)
  starting transfers between devices  33.4 us (31%)
  waiting for transfers between devices  13.9 us (13%)
  local copies, waits for them, and re-layouts  3.95 us (4%)
    pallas_call x3, Pallas kernels, inner(): pl.pallas_call(kernel, out_shape=[shape((BOXES + 1, 32, points), F32), sh...  26 us
    pallas_call x1, Pallas kernels, shards(): pl.pallas_call(outer_kernel, out_shape=[acc_shape] + [shape((4, 32, point...  19 us
    ppermute x8, starting transfers between devices, xor_permute(): return lax.ppermute(value, axis, [(i, i ^ bits) for i in range(count)])  16.4 us
    all_to_all x1, starting transfers between devices, shards(): gathered = lax.all_to_all(sums, ('gx', 'gy', 'gz'), 0, 0, tiled=True)  10.9 us
    all_to_all x1, waiting for transfers between devices, shards(): gathered = lax.all_to_all(sums, ('gx', 'gy', 'gz'), 0, 0, tiled=True)  9.5 us
    ppermute x6, starting transfers between devices, along(): lax.ppermute(value, name, [(i, (i + step) % size) for i in range(size)])  5.99 us
    pallas_call x1, Pallas kernels, shards(): pl.pallas_call(local_kernel, out_shape=[shape((BOXES, 64, 128), BF16), sh...  5.44 us
    ppermute x8, waiting for transfers between devices, xor_permute(): return lax.ppermute(value, axis, [(i, i ^ bits) for i in range(count)])  4.4 us
  transfers between devices with their start and end apart: 15, of which 3 were waited for; matrix products, arithmetic and copies ran while one was open for 0% of the time, Pallas kernels for 49%

commit v1 on v0

--- a/solution.py
+++ b/solution.py
@@ -259,11 +259,7 @@
         ref[...] = back[4 * axis:4 * axis + 4]
 
 
-def local_kernel(counts, req_box, req_tgt, here, there, momf, probe_sums, loc, sums, slab, far_acc, live, sems):
-    first_copy = pltpu.make_async_copy(here, slab.at[pl.ds(0, 32)], sems.at[0])
-    second_copy = pltpu.make_async_copy(there, slab.at[pl.ds(32, 32)], sems.at[1])
-    first_copy.start()
-    second_copy.start()
+def local_kernel(counts, req_box, req_tgt, here, there, momf, probe_sums, loc, sums, far_acc, live):
     my_y = lax.axis_index("gy")
     my_z = lax.axis_index("gz")
     far_acc[...] = jnp.zeros_like(far_acc)
@@ -272,7 +268,7 @@
         live[n] = i
         return n + (req_box[i >> 6, i & 63] >= 0).astype(jnp.int32)
 
-    used = lax.fori_loop(0, 128, keep, jnp.int32(0))
+    used = lax.fori_loop(0, 128, keep, jnp.int32(0), unroll=16)
     shape = (64, 64)
     source_q = lax.broadcasted_iota(jnp.int32, shape, 1)
     target_q = lax.broadcasted_iota(jnp.int32, shape, 0)
@@ -285,8 +281,6 @@
 
     gaps = [node((source_q >> s) & 3) - node((target_q >> s) & 3) for s in (4, 2, 0)]
     group = lax.broadcasted_iota(jnp.int32, (64, 256), 1) >> 5
-    first_copy.wait()
-    second_copy.wait()
 
     def step(g, carry):
         for u in range(8):
@@ -306,8 +300,9 @@
             coupling = lax.rsqrt(1.0 + ex * ex + ey * ey + ez * ez).astype(BF16)
             rel_y = peer_y ^ my_y
             rel_z = peer_z ^ my_z
-            at = (rel_z & 1) * 32 + ((rel_z >> 1) & 3) * 8 + rel_y * 2 + (rel_z >> 3)
-            term = jnp.dot(coupling, slab[at], preferred_element_type=F32)
+            at = ((rel_z >> 1) & 3) * 8 + rel_y * 2 + (rel_z >> 3)
+            block = jnp.where((rel_z & 1) == 0, here[at], there[at])
+            term = jnp.dot(coupling, block, preferred_element_type=F32)
             wanted = jnp.where(k < used, box, -1)
             far_acc[tgt] += jnp.where(group == wanted, term, 0.0)
         return carry
@@ -452,11 +447,11 @@
     for axis in (2, 0, 1):
         got[axis] = along(axis, faces[axis], -1)
     acc_self, tick = inner("self_tiles", list(range(BOXES)), lambda b: [b], False, None, mom)
-    tick, twin, got[0], got[1] = join("join_first", tick, twin, got[0], got[1])
+    tick, twin, got[0] = join("join_first", tick, twin, got[0])
     block = jnp.concatenate([block, twin], axis=0)
     more = [xor_permute(block, "gy", k) for k in (1, 2, 3)]
     acc, tick = inner("pairs_low", [1, 2, 4, 3], lambda b: INNER[b], True, None, tick)
-    tick, got[2], *more = join("join_second", tick, got[2], *more)
+    tick, got[1], got[2], *more = join("join_second", tick, got[1], got[2], *more)
     block = jnp.concatenate([block] + more, axis=0)
     more = [xor_permute(block, "gz", 2 * k) for k in (1, 2, 3)]
     acc, tick = inner("pairs_high", [5, 6, 7], lambda b: INNER[b], True, acc, tick)
@@ -485,13 +480,11 @@
     loc, sums = pl.pallas_call(
         local_kernel,
         out_shape=[shape((BOXES, 64, 128), BF16), shape((devices, 1, 128), F32)],
-        in_specs=[SMEM, SMEM, SMEM, ANY, ANY, VMEM, VMEM],
+        in_specs=[SMEM, SMEM, SMEM, VMEM, VMEM, VMEM, VMEM],
         out_specs=[VMEM, VMEM],
         scratch_shapes=[
-            pltpu.VMEM((64, 64, 256), BF16),
             pltpu.VMEM((BOXES, 64, 256), F32),
             pltpu.SMEM((136,), jnp.int32),
-            pltpu.SemaphoreType.DMA((2,)),
         ],
         compiler_params=PARAMS,
         name="locals",

time: 109 us -> 108 us (level); the launches traced: 108 us -> 108 us
  starting transfers between devices: 33.4 us -> 38.4 us
  waiting for transfers between devices: 13.9 us -> 9.66 us
    ppermute x8, waiting for transfers between devices: 4.4 us -> 0.18 us  [xor_permute(): return lax.ppermute(value, axis, [(i, i ^ bits) for i in range(count)])]
    all_to_all x1, starting transfers between devices: 10.9 us -> 15.1 us  [shards(): gathered = lax.all_to_all(sums, ('gx', 'gy', 'gz'), 0, 0, tiled=True)]
    pallas_call x3, Pallas kernels: 26 us -> 29.8 us  [inner(): pl.pallas_call(kernel, out_shape=[shape((BOXES + 1, 32, points), F32), sh...]
    pallas_call x1, Pallas kernels: 19 us -> 15.6 us  [shards(): pl.pallas_call(outer_kernel, out_shape=[acc_shape] + [shape((4, 32, point...]
  transfers between devices with their start and end apart: 15 -> 15, of which waited for: 3 -> 2; matrix products, arithmetic and copies ran while one was open for 0% -> 0% of each run, Pallas kernels for 49% -> 48%
where the time goes in v1:
time: 108 us
  Pallas kernels  55.2 us (51%)
  starting transfers between devices  38.4 us (36%)
  waiting for transfers between devices  9.66 us (9%)
  local copies, waits for them, and re-layouts  3.95 us (4%)
    pallas_call x3, Pallas kernels, inner(): pl.pallas_call(kernel, out_shape=[shape((BOXES + 1, 32, points), F32), sh...  29.8 us
    ppermute x8, starting transfers between devices, xor_permute(): return lax.ppermute(value, axis, [(i, i ^ bits) for i in range(count)])  16.4 us
    pallas_call x1, Pallas kernels, shards(): pl.pallas_call(outer_kernel, out_shape=[acc_shape] + [shape((4, 32, point...  15.6 us
    all_to_all x1, starting transfers between devices, shards(): gathered = lax.all_to_all(sums, ('gx', 'gy', 'gz'), 0, 0, tiled=True)  15.1 us
    all_to_all x1, waiting for transfers between devices, shards(): gathered = lax.all_to_all(sums, ('gx', 'gy', 'gz'), 0, 0, tiled=True)  9.46 us
    ppermute x6, starting transfers between devices, along(): lax.ppermute(value, name, [(i, (i + step) % size) for i in range(size)])  6.9 us
    pallas_call x1, Pallas kernels, shards(): pl.pallas_call(local_kernel, out_shape=[shape((BOXES, 64, 128), BF16), sh...  4.58 us
    unnamed x23, local copies, waits for them, and re-layouts  3.93 us
  transfers between devices with their start and end apart: 15, of which 2 were waited for; matrix products, arithmetic and copies ran while one was open for 0% of the time, Pallas kernels for 48%

profile of v1, /device:TPU:1, one launch (start us, length us, event | category | flops | bytes accessed | tf_op | source)
XLA Modules:
  0.0 108.1 jit_solution(5491731570691898025)
XLA Ops:
  0.6 1.0 copy-done
  1.7 0.9 copy-done.1
  2.6 0.7 copy-done.2
  3.2 2.2 %prep.1 = (bf16[9,48,1024]{2,1,0:T(8,128)(2,1)S(1)}, bf16[9,48,1024]{2,1,0:T(8,128)(2,1)S(1)}, bf16[8,48,1024]{2,1,0:T(8,128)(2,1)S(1)}, bf16[8,64,1024]{2,1,0:T...) custom-call(s32[2,2,2]{2,1,0:T(2,128)S(1)} %copy-done.2, ...), custom_call_target="tpu_custom_call" | custom-call | tf_op jit(solution)/shard_map/prep/pallas_call | solution.py:389
  5.4 7.8 %collective-permute-start = (bf16[1,64,256]{2,1,0:T(8,128)(2,1)S(1)}, bf16[1,64,256]{2,1,0:T(8,128)(2,1)S(1)}, u32[]{:S(2)}, u32[]{:S(2)}) collective-permute-start(bf16[1,64,256]{2,1,0:T(8,128)(2,1)S(1)} %bitcast.11), channel_id=1, source_target_pairs={{0,8},{1,9},{2,10},{3,11},{4,12},{5,13},{6,14},{7,15},{8,0},{9,1},... | collective-permute-start | bytes 98312 | tf_op jit(solution)/shard_map/ppermute | solution.py:382
  13.2 2.7 %collective-permute-start.1 = (bf16[4,48,1024]{2,1,0:T(8,128)(2,1)S(1)}, bf16[4,48,1024]{2,1,0:T(8,128)(2,1)S(1)}, u32[]{:S(2)}, u32[]{:S(2)}) collective-permute-start(bf16[4,48,1024]{2,1,0:T(8,128)(2,1)S(1)} %get-tuple-element.45), channel_id=1, source_target_pairs={{0,192},{64,0},{128,64},{192,128},{1,193},{65,1},{129,65},{193,129... | collective-permute-start | bytes 1179656 | tf_op jit(solution)/shard_map/ppermute | solution.py:442
  16.0 1.6 %collective-permute-start.2 = (bf16[4,48,1024]{2,1,0:T(8,128)(2,1)S(1)}, bf16[4,48,1024]{2,1,0:T(8,128)(2,1)S(1)}, u32[]{:S(2)}, u32[]{:S(2)}) collective-permute-start(bf16[4,48,1024]{2,1,0:T(8,128)(2,1)S(1)} %get-tuple-element.49), channel_id=1, source_target_pairs={{0,48},{16,0},{32,16},{48,32},{1,49},{17,1},{33,17},{49,33},{2,50}... | collective-permute-start | bytes 1179656 | tf_op jit(solution)/shard_map/ppermute | solution.py:442
  17.6 1.5 %collective-permute-start.3 = (bf16[4,48,1024]{2,1,0:T(8,128)(2,1)S(1)}, bf16[4,48,1024]{2,1,0:T(8,128)(2,1)S(1)}, u32[]{:S(2)}, u32[]{:S(2)}) collective-permute-start(bf16[4,48,1024]{2,1,0:T(8,128)(2,1)S(1)} %get-tuple-element.50), channel_id=1, source_target_pairs={{0,15},{1,0},{2,1},{3,2},{4,3},{5,4},{6,5},{7,6},{8,7},{9,8},{10,9... | collective-permute-start | bytes 1179656 | tf_op jit(solution)/shard_map/ppermute | solution.py:442
  19.1 9.3 %self_tiles.1 = (f32[9,32,1024]{2,1,0:T(8,128)S(1)}, f32[8,128]{1,0:T(8,128)S(1)}) custom-call(s32[2,2,2]{2,1,0:T(2,128)S(1)} %copy-done.2, bf16[9,48,1024]{2,1,0:T(8,128)(2,1)S(1)} %get-tuple-element.41.refs_1_, bf16[9,48,1024]{2,1,0:T(8,128)(2,1)S(1)} %get-tuple-element.40.refs_2_.pay, bf16[8,48,1024]{2,1,0:T(8,128)(2,1)S(1)} %get-tuple-element.39.refs_3_.fb, ...), custom_call_target="tpu_custom_call" | custom-call | flops 12000000000 | bytes 4194304 | tf_op jit(solution)/shard_map/self_tiles/pallas_call | solution.py:428
  28.5 0.8 collective-permute-start.6
  29.3 2.8 %collective-permute-start.4 = (bf16[2,64,256]{2,1,0:T(8,128)(2,1)S(1)}, bf16[2,64,256]{2,1,0:T(8,128)(2,1)S(1)}, u32[]{:S(2)}, u32[]{:S(2)}) collective-permute-start(bf16[2,64,256]{2,1,0:T(8,128)(2,1)S(1)} %pad_maximum_fusion), channel_id=1, source_target_pairs={{0,16},{16,0},{32,48},{48,32},{1,17},{17,1},{33,49},{49,33},{2,18}... | collective-permute-start | bytes 196616 | tf_op jit(solution)/shard_map/ppermute | solution.py:382
  32.1 9.3 %pairs_low.1 = (f32[9,32,1024]{2,1,0:T(8,128)S(1)}, f32[8,128]{1,0:T(8,128)S(1)}) custom-call(s32[2,2,2]{2,1,0:T(2,128)S(1)} %copy-done.2, bf16[9,48,1024]{2,1,0:T(8,128)(2,1)S(1)} %get-tuple-element.41.refs_1_, bf16[9,48,1024]{2,1,0:T(8,128)(2,1)S(1)} %get-tuple-element.40.refs_2_.pay, bf16[8,48,1024]{2,1,0:T(8,128)(2,1)S(1)} %get-tuple-element.39.refs_3_.fb, ...), custom_call_target="tpu_custom_call" | custom-call | flops 12000000000 | bytes 4194304 | tf_op jit(solution)/shard_map/pairs_low/pallas_call | solution.py:428
  41.7 3.1 %collective-permute-start.7 = (bf16[8,64,256]{2,1,0:T(8,128)(2,1)S(1)}, bf16[8,64,256]{2,1,0:T(8,128)(2,1)S(1)}, u32[]{:S(2)}, u32[]{:S(2)}) collective-permute-start(bf16[8,64,256]{2,1,0:T(8,128)(2,1)S(1)} %get-tuple-element.77), channel_id=1, source_target_pairs={{0,2},{1,3},{2,0},{3,1},{4,6},{5,7},{6,4},{7,5},{8,10},{9,11},{10,... | collective-permute-start | bytes 786440 | tf_op jit(solution)/shard_map/ppermute | solution.py:382
  44.9 11.2 %pairs_high.1 = (f32[9,32,1024]{2,1,0:T(8,128)S(1)}, f32[8,128]{1,0:T(8,128)S(1)}) custom-call(s32[2,2,2]{2,1,0:T(2,128)S(1)} %copy-done.2, bf16[9,48,1024]{2,1,0:T(8,128)(2,1)S(1)} %get-tuple-element.41.refs_1_, bf16[9,48,1024]{2,1,0:T(8,128)(2,1)S(1)} %get-tuple-element.40.refs_2_.pay, bf16[8,48,1024]{2,1,0:T(8,128)(2,1)S(1)} %get-tuple-element.39.refs_3_.fb, ...), custom_call_target="tpu_custom_call" | custom-call | flops 12000000000 | bytes 4194304 | tf_op jit(solution)/shard_map/pairs_high/pallas_call | solution.py:428
  56.1 0.2 collective-permute-done.9.refs_3_
  56.4 1.6 %collective-permute-start.13 = (bf16[32,64,256]{2,1,0:T(8,128)(2,1)S(1)}, bf16[32,64,256]{2,1,0:T(8,128)(2,1)S(1)}, u32[]{:S(2)}, u32[]{:S(2)}) collective-permute-start(bf16[32,64,256]{2,1,0:T(8,128)(2,1)S(1)} %constant_dynamic-update-slice_fusion.5.here), channel_id=1, source_target_pairs={{0,1},{1,0},{2,3},{3,2},{4,5},{5,4},{6,7},{7,6},{8,9},{9,8},{10,11... | collective-permute-start | bytes 3145736 | tf_op jit(solution)/shard_map/ppermute | solution.py:382
  57.9 15.6 %face_tiles.1 = (f32[8,32,1024]{2,1,0:T(8,128)S(1)}, f32[4,32,1024]{2,1,0:T(8,128)S(1)}, f32[4,32,1024]{2,1,0:T(8,128)S(1)}, f32[4,32,1024]{2,1,0:T(8,128)}, f32[32,128]{1,0:T(8,128)S(1)}) custom-call(s32[2,2,2]{2,1,0:T(2,128)S(1)} %copy-done.2, bf16[8,48,1024]{2,1,0:T(8,128)(2,1)S(1)} %get-tuple-element.39.refs_3_.fb, ...), custom_call_target="tpu_custom_call" | custom-call | flops 12000000000 | bytes 4194304 | tf_op jit(solution)/shard_map/face_tiles/pallas_call | solution.py:461
  73.5 1.0 collective-permute-start.12
  74.5 4.6 %locals.1 = (bf16[8,64,128]{2,1,0:T(8,128)(2,1)S(1)}, f32[256,1,128]{2,1,0:T(1,128)}) custom-call(s32[2,2,2]{2,1,0:T(2,128)S(1)} %copy-done.2, s32[2,64]{1,0:T(2,128)S(1)} %bitcast.14, s32[2,64]{1,0:T(2,128)S(1)} %bitcast.15, bf16[32,64,256]{2,1,0:T(8,128)(2,1)S(1)} %constant_dynamic-update-slice_fusion.5.here, ...), custom_call_target="tpu_custom_call" | custom-call | tf_op jit(solution)/shard_map/locals/pallas_call | solution.py:480
  79.1 15.1 %all-to-all-start = ((f32[256,1,128]{2,1,0:T(1,128)}), f32[256,1,128]{2,1,0:T(1,128)S(1)}, u32[]{:S(2)}, u32[]{:S(2)}) async-start(f32[256,1,128]{2,1,0:T(1,128)} %get-tuple-element.74), calls=%async_computation | async-start | bytes 262144 | tf_op jit(solution)/shard_map/all_to_all | solution.py:492
  94.3 1.2 %copy-done.7 = f32[8,32,1024]{2,1,0:T(8,128)S(1)} copy-done((f32[8,32,1024]{2,1,0:T(8,128)S(1)}, f32[8,32,1024]{2,1,0:T(8,128)}, u32[]{:S(2)}) %copy-start.7) | copy-done | bytes 1048600
  95.5 2.3 %total.1 = (bf16[8,32,1024]{2,1,0:T(8,128)(2,1)}, f32[8,128]{1,0:T(8,128)S(1)}) custom-call(s32[2,2,2]{2,1,0:T(2,128)S(1)} %copy-done.3, f32[8,32,1024]{2,1,0:T(8,128)S(1)} %copy-done.7, f32[4,32,1024]{2,1,0:T(8,128)S(1)} %collective-permute-done.10.r2, f32[4,32,1024]{2,1,0:T(8,128)S(1)} %collective-permute-done.11.r0, ...), custom_call_target="tpu_custom_call" | custom-call | flops 12000000000 | bytes 4194304 | tf_op jit(solution)/shard_map/total/pallas_call | solution.py:493
  97.8 9.5 %all-to-all-done.gathered = f32[256,1,128]{2,1,0:T(1,128)S(1)} async-done(((f32[256,1,128]{2,1,0:T(1,128)}), f32[256,1,128]{2,1,0:T(1,128)S(1)}, u32[]{:S(2)}, u32[]{:S(2)}) %all-to-all-start) | async-done | bytes 131104 | tf_op jit(solution)/shard_map/all_to_all | solution.py:492
  107.2 0.9 quad.1
  (42 shorter events, 0.4 us)
Async XLA Ops:
  0.6 1.0 copy-start
  1.7 0.9 copy-start.1
  2.6 0.7 copy-start.2
  5.4 23.0 %collective-permute-start = (bf16[1,64,256]{2,1,0:T(8,128)(2,1)S(1)}, bf16[1,64,256]{2,1,0:T(8,128)(2,1)S(1)}, u32[]{:S(2)}, u32[]{:S(2)}) collective-permute-start(bf16[1,64,256]{2,1,0:T(8,128)(2,1)S(1)} %bitcast.11), channel_id=1, source_target_pairs={{0,8},{1,9},{2,10},{3,11},{4,12},{5,13},{6,14},{7,15},{8,0},{9,1},... | collective-permute-start | bytes 98312 | tf_op jit(solution)/shard_map/ppermute | solution.py:382
  13.2 15.2 %collective-permute-start.1 = (bf16[4,48,1024]{2,1,0:T(8,128)(2,1)S(1)}, bf16[4,48,1024]{2,1,0:T(8,128)(2,1)S(1)}, u32[]{:S(2)}, u32[]{:S(2)}) collective-permute-start(bf16[4,48,1024]{2,1,0:T(8,128)(2,1)S(1)} %get-tuple-element.45), channel_id=1, source_target_pairs={{0,192},{64,0},{128,64},{192,128},{1,193},{65,1},{129,65},{193,129... | collective-permute-start | bytes 1179656 | tf_op jit(solution)/shard_map/ppermute | solution.py:442
  16.0 25.4 %collective-permute-start.2 = (bf16[4,48,1024]{2,1,0:T(8,128)(2,1)S(1)}, bf16[4,48,1024]{2,1,0:T(8,128)(2,1)S(1)}, u32[]{:S(2)}, u32[]{:S(2)}) collective-permute-start(bf16[4,48,1024]{2,1,0:T(8,128)(2,1)S(1)} %get-tuple-element.49), channel_id=1, source_target_pairs={{0,48},{16,0},{32,16},{48,32},{1,49},{17,1},{33,17},{49,33},{2,50}... | collective-permute-start | bytes 1179656 | tf_op jit(solution)/shard_map/ppermute | solution.py:442
  17.6 23.8 %collective-permute-start.3 = (bf16[4,48,1024]{2,1,0:T(8,128)(2,1)S(1)}, bf16[4,48,1024]{2,1,0:T(8,128)(2,1)S(1)}, u32[]{:S(2)}, u32[]{:S(2)}) collective-permute-start(bf16[4,48,1024]{2,1,0:T(8,128)(2,1)S(1)} %get-tuple-element.50), channel_id=1, source_target_pairs={{0,15},{1,0},{2,1},{3,2},{4,3},{5,4},{6,5},{7,6},{8,7},{9,8},{10,9... | collective-permute-start | bytes 1179656 | tf_op jit(solution)/shard_map/ppermute | solution.py:442
  28.5 13.0 %collective-permute-start.6 = (bf16[2,64,256]{2,1,0:T(8,128)(2,1)S(1)}, bf16[2,64,256]{2,1,0:T(8,128)(2,1)S(1)}, u32[]{:S(2)}, u32[]{:S(2)}) collective-permute-start(bf16[2,64,256]{2,1,0:T(8,128)(2,1)S(1)} %pad_maximum_fusion), channel_id=1, source_target_pairs={{0,48},{16,32},{32,16},{48,0},{1,49},{17,33},{33,17},{49,1},{2,50}... | collective-permute-start | bytes 196616 | tf_op jit(solution)/shard_map/ppermute | solution.py:382
  29.3 12.2 %collective-permute-start.5 = (bf16[2,64,256]{2,1,0:T(8,128)(2,1)S(1)}, bf16[2,64,256]{2,1,0:T(8,128)(2,1)S(1)}, u32[]{:S(2)}, u32[]{:S(2)}) collective-permute-start(bf16[2,64,256]{2,1,0:T(8,128)(2,1)S(1)} %pad_maximum_fusion), channel_id=1, source_target_pairs={{0,32},{16,48},{32,0},{48,16},{1,33},{17,49},{33,1},{49,17},{2,34}... | collective-permute-start | bytes 196616 | tf_op jit(solution)/shard_map/ppermute | solution.py:382
  29.3 12.2 %collective-permute-start.4 = (bf16[2,64,256]{2,1,0:T(8,128)(2,1)S(1)}, bf16[2,64,256]{2,1,0:T(8,128)(2,1)S(1)}, u32[]{:S(2)}, u32[]{:S(2)}) collective-permute-start(bf16[2,64,256]{2,1,0:T(8,128)(2,1)S(1)} %pad_maximum_fusion), channel_id=1, source_target_pairs={{0,16},{16,0},{32,48},{48,32},{1,17},{17,1},{33,49},{49,33},{2,18}... | collective-permute-start | bytes 196616 | tf_op jit(solution)/shard_map/ppermute | solution.py:382
  41.5 14.7 %collective-permute-start.9 = (bf16[8,64,256]{2,1,0:T(8,128)(2,1)S(1)}, bf16[8,64,256]{2,1,0:T(8,128)(2,1)S(1)}, u32[]{:S(2)}, u32[]{:S(2)}) collective-permute-start(bf16[8,64,256]{2,1,0:T(8,128)(2,1)S(1)} %get-tuple-element.77), channel_id=1, source_target_pairs={{0,6},{1,7},{2,4},{3,5},{4,2},{5,3},{6,0},{7,1},{8,14},{9,15},{10,... | collective-permute-start | bytes 786440 | tf_op jit(solution)/shard_map/ppermute | solution.py:382
  41.6 14.7 %collective-permute-start.8 = (bf16[8,64,256]{2,1,0:T(8,128)(2,1)S(1)}, bf16[8,64,256]{2,1,0:T(8,128)(2,1)S(1)}, u32[]{:S(2)}, u32[]{:S(2)}) collective-permute-start(bf16[8,64,256]{2,1,0:T(8,128)(2,1)S(1)} %get-tuple-element.77), channel_id=1, source_target_pairs={{0,4},{1,5},{2,6},{3,7},{4,0},{5,1},{6,2},{7,3},{8,12},{9,13},{10,... | collective-permute-start | bytes 786440 | tf_op jit(solution)/shard_map/ppermute | solution.py:382
  41.7 14.6 %collective-permute-start.7 = (bf16[8,64,256]{2,1,0:T(8,128)(2,1)S(1)}, bf16[8,64,256]{2,1,0:T(8,128)(2,1)S(1)}, u32[]{:S(2)}, u32[]{:S(2)}) collective-permute-start(bf16[8,64,256]{2,1,0:T(8,128)(2,1)S(1)} %get-tuple-element.77), channel_id=1, source_target_pairs={{0,2},{1,3},{2,0},{3,1},{4,6},{5,7},{6,4},{7,5},{8,10},{9,11},{10,... | collective-permute-start | bytes 786440 | tf_op jit(solution)/shard_map/ppermute | solution.py:382
  56.4 18.2 %collective-permute-start.13 = (bf16[32,64,256]{2,1,0:T(8,128)(2,1)S(1)}, bf16[32,64,256]{2,1,0:T(8,128)(2,1)S(1)}, u32[]{:S(2)}, u32[]{:S(2)}) collective-permute-start(bf16[32,64,256]{2,1,0:T(8,128)(2,1)S(1)} %constant_dynamic-update-slice_fusion.5.here), channel_id=1, source_target_pairs={{0,1},{1,0},{2,3},{3,2},{4,5},{5,4},{6,7},{7,6},{8,9},{9,8},{10,11... | collective-permute-start | bytes 3145736 | tf_op jit(solution)/shard_map/ppermute | solution.py:382
  57.9 16.6 %copy-start.4 = (s32[1,1,1,64,2]{3,4,2,1,0:T(2,128)S(1)}, s32[1,1,1,64,2]{3,4,2,1,0:T(2,128)}, u32[]{:S(2)}) copy-start(s32[1,1,1,64,2]{3,4,2,1,0:T(2,128)} %param.8) | copy-start | bytes 1540
  57.9 16.6 %copy-start.5 = (s32[1,1,1,64,2]{3,4,2,1,0:T(2,128)S(1)}, s32[1,1,1,64,2]{3,4,2,1,0:T(2,128)}, u32[]{:S(2)}) copy-start(s32[1,1,1,64,2]{3,4,2,1,0:T(2,128)} %param.9) | copy-start | bytes 1540
  73.5 5.6 %copy-start.6 = (f32[8,32,1024]{2,1,0:T(8,128)}, f32[8,32,1024]{2,1,0:T(8,128)S(1)}, u32[]{:S(2)}) copy-start(f32[8,32,1024]{2,1,0:T(8,128)S(1)} %get-tuple-element.62.near) | copy-start | bytes 3145732
  73.5 20.7 %collective-permute-start.10 = (f32[4,32,1024]{2,1,0:T(8,128)}, f32[4,32,1024]{2,1,0:T(8,128)S(1)}, u32[]{:S(2)}, u32[]{:S(2)}) collective-permute-start(f32[4,32,1024]{2,1,0:T(8,128)} %get-tuple-element.63), channel_id=1, source_target_pairs={{0,1},{1,2},{2,3},{3,4},{4,5},{5,6},{6,7},{7,8},{8,9},{9,10},{10,1... | collective-permute-start | bytes 1572872 | tf_op jit(solution)/shard_map/ppermute | solution.py:442
  73.5 20.7 %collective-permute-start.11 = (f32[4,32,1024]{2,1,0:T(8,128)S(1)}, f32[4,32,1024]{2,1,0:T(8,128)S(1)}, u32[]{:S(2)}, u32[]{:S(2)}) collective-permute-start(f32[4,32,1024]{2,1,0:T(8,128)S(1)} %get-tuple-element.64), channel_id=1, source_target_pairs={{0,64},{64,128},{128,192},{192,0},{1,65},{65,129},{129,193},{193,1... | collective-permute-start | bytes 1572872 | tf_op jit(solution)/shard_map/ppermute | solution.py:442
  73.5 20.7 %collective-permute-start.12 = (f32[4,32,1024]{2,1,0:T(8,128)S(1)}, f32[4,32,1024]{2,1,0:T(8,128)}, u32[]{:S(2)}, u32[]{:S(2)}) collective-permute-start(f32[4,32,1024]{2,1,0:T(8,128)S(1)} %get-tuple-element.65), channel_id=1, source_target_pairs={{0,16},{16,32},{32,48},{48,0},{1,17},{17,33},{33,49},{49,1},{2,18}... | collective-permute-start | bytes 1572872 | tf_op jit(solution)/shard_map/ppermute | solution.py:442
  74.5 19.7 %copy-start.3 = (s32[2,2,2]{2,1,0:T(2,128)S(1)}, s32[2,2,2]{2,1,0:T(2,128)}, u32[]{:S(2)}) copy-start(s32[2,2,2]{2,1,0:T(2,128)} %counts.7) | copy-start | bytes 100
  79.1 28.1 %all-to-all-start = ((f32[256,1,128]{2,1,0:T(1,128)}), f32[256,1,128]{2,1,0:T(1,128)S(1)}, u32[]{:S(2)}, u32[]{:S(2)}) async-start(f32[256,1,128]{2,1,0:T(1,128)} %get-tuple-element.74), calls=%async_computation | async-start | bytes 262144 | tf_op jit(solution)/shard_map/all_to_all | solution.py:492
  94.3 1.2 %copy-start.7 = (f32[8,32,1024]{2,1,0:T(8,128)S(1)}, f32[8,32,1024]{2,1,0:T(8,128)}, u32[]{:S(2)}) copy-start(f32[8,32,1024]{2,1,0:T(8,128)} %copy-done.6) | copy-start | bytes 3145732

commit v2 on v1

--- a/solution.py
+++ b/solution.py
@@ -444,18 +444,19 @@
     block = mom.reshape(1, 64, 256)
     twin = xor_permute(block, "gz", 8)
     got = [None] * 3
-    for axis in (2, 0, 1):
-        got[axis] = along(axis, faces[axis], -1)
+    got[2] = along(2, faces[2], -1)
     acc_self, tick = inner("self_tiles", list(range(BOXES)), lambda b: [b], False, None, mom)
-    tick, twin, got[0] = join("join_first", tick, twin, got[0])
+    tick, twin, face_x = join("join_first", tick, twin, faces[0])
     block = jnp.concatenate([block, twin], axis=0)
     more = [xor_permute(block, "gy", k) for k in (1, 2, 3)]
+    got[0] = along(0, face_x, -1)
     acc, tick = inner("pairs_low", [1, 2, 4, 3], lambda b: INNER[b], True, None, tick)
-    tick, got[1], got[2], *more = join("join_second", tick, got[1], got[2], *more)
+    tick, got[0], got[2], face_y, *more = join("join_second", tick, got[0], got[2], faces[1], *more)
     block = jnp.concatenate([block] + more, axis=0)
     more = [xor_permute(block, "gz", 2 * k) for k in (1, 2, 3)]
+    got[1] = along(1, face_y, -1)
     acc, tick = inner("pairs_high", [5, 6, 7], lambda b: INNER[b], True, acc, tick)
-    tick, *more = join("join_third", tick, *more)
+    tick, got[1], *more = join("join_third", tick, got[1], *more)
     block = jnp.concatenate([block] + more, axis=0)
     other = xor_permute(block, "gz", 1)
     near, *backs, probe_sums = pl.pallas_call(

time: 108 us -> 107 us (level)
  Pallas kernels: 55.2 us -> 48.9 us
  starting transfers between devices: 38.4 us -> 43.6 us
    pallas_call x3, Pallas kernels: 29.8 us -> 24 us  [inner(): pl.pallas_call(kernel, out_shape=[shape((BOXES + 1, 32, points), F32), sh...]
    ppermute x6, starting transfers between devices: 6.9 us -> 10.6 us  [along(): lax.ppermute(value, name, [(i, (i + step) % size) for i in range(size)])]
    ppermute x8, starting transfers between devices: 16.4 us -> 19.6 us  [xor_permute(): return lax.ppermute(value, axis, [(i, i ^ bits) for i in range(count)])]
    all_to_all x1, starting transfers between devices: 15.1 us -> 13.4 us  [shards(): gathered = lax.all_to_all(sums, ('gx', 'gy', 'gz'), 0, 0, tiled=True)]
  transfers between devices with their start and end apart: 15 -> 15, of which waited for: 2 -> 3; matrix products, arithmetic and copies ran while one was open for 0% -> 0% of each run, Pallas kernels for 48% -> 43%
where the time goes in v2:
time: 107 us
  Pallas kernels  48.9 us (46%)
  starting transfers between devices  43.6 us (41%)
  waiting for transfers between devices  10.1 us (9%)
  local copies, waits for them, and re-layouts  3.95 us (4%)
    pallas_call x3, Pallas kernels, inner(): pl.pallas_call(kernel, out_shape=[shape((BOXES + 1, 32, points), F32), sh...  24 us
    ppermute x8, starting transfers between devices, xor_permute(): return lax.ppermute(value, axis, [(i, i ^ bits) for i in range(count)])  19.6 us
    pallas_call x1, Pallas kernels, shards(): pl.pallas_call(outer_kernel, out_shape=[acc_shape] + [shape((4, 32, point...  15.1 us
    all_to_all x1, starting transfers between devices, shards(): gathered = lax.all_to_all(sums, ('gx', 'gy', 'gz'), 0, 0, tiled=True)  13.4 us
    ppermute x6, starting transfers between devices, along(): lax.ppermute(value, name, [(i, (i + step) % size) for i in range(size)])  10.6 us
    all_to_all x1, waiting for transfers between devices, shards(): gathered = lax.all_to_all(sums, ('gx', 'gy', 'gz'), 0, 0, tiled=True)  9.46 us
    pallas_call x1, Pallas kernels, shards(): pl.pallas_call(local_kernel, out_shape=[shape((BOXES, 64, 128), BF16), sh...  4.58 us
    unnamed x23, local copies, waits for them, and re-layouts  3.93 us
  transfers between devices with their start and end apart: 15, of which 3 were waited for; matrix products, arithmetic and copies ran while one was open for 0% of the time, Pallas kernels for 43%

profile of v2, /device:TPU:1, one launch (start us, length us, event | category | flops | bytes accessed | tf_op | source)
XLA Modules:
  0.0 107.4 jit_solution(4188401859503006200)
XLA Ops:
  0.6 1.0 copy-done
  1.7 0.9 copy-done.1
  3.2 2.2 %prep.1 = (bf16[9,48,1024]{2,1,0:T(8,128)(2,1)S(1)}, bf16[9,48,1024]{2,1,0:T(8,128)(2,1)S(1)}, bf16[8,48,1024]{2,1,0:T(8,128)(2,1)S(1)}, bf16[8,64,1024]{2,1,0:T...) custom-call(s32[2,2,2]{2,1,0:T(2,128)S(1)} %copy-done.2, ...), custom_call_target="tpu_custom_call" | custom-call | tf_op jit(solution)/shard_map/prep/pallas_call | solution.py:389
  5.4 7.8 %collective-permute-start = (bf16[1,64,256]{2,1,0:T(8,128)(2,1)S(1)}, bf16[1,64,256]{2,1,0:T(8,128)(2,1)S(1)}, u32[]{:S(2)}, u32[]{:S(2)}) collective-permute-start(bf16[1,64,256]{2,1,0:T(8,128)(2,1)S(1)} %bitcast.11), channel_id=1, source_target_pairs={{0,8},{1,9},{2,10},{3,11},{4,12},{5,13},{6,14},{7,15},{8,0},{9,1},... | collective-permute-start | bytes 98312 | tf_op jit(solution)/shard_map/ppermute | solution.py:382
  13.2 1.0 collective-permute-start.2
  14.2 7.2 %self_tiles.1 = (f32[9,32,1024]{2,1,0:T(8,128)S(1)}, f32[8,128]{1,0:T(8,128)S(1)}) custom-call(s32[2,2,2]{2,1,0:T(2,128)S(1)} %copy-done.2, bf16[9,48,1024]{2,1,0:T(8,128)(2,1)S(1)} %get-tuple-element.43.refs_1_, bf16[9,48,1024]{2,1,0:T(8,128)(2,1)S(1)} %get-tuple-element.42.refs_2_.pay, bf16[8,48,1024]{2,1,0:T(8,128)(2,1)S(1)} %get-tuple-element.41.refs_3_.fb, ...), custom_call_target="tpu_custom_call" | custom-call | flops 12000000000 | bytes 4194304 | tf_op jit(solution)/shard_map/self_tiles/pallas_call | solution.py:428
  21.5 2.4 %collective-permute-start.5 = (bf16[2,64,256]{2,1,0:T(8,128)(2,1)S(1)}, bf16[2,64,256]{2,1,0:T(8,128)(2,1)S(1)}, u32[]{:S(2)}, u32[]{:S(2)}) collective-permute-start(bf16[2,64,256]{2,1,0:T(8,128)(2,1)S(1)} %pad_maximum_fusion), channel_id=1, source_target_pairs={{0,48},{16,32},{32,16},{48,0},{1,49},{17,33},{33,17},{49,1},{2,50}... | collective-permute-start | bytes 196616 | tf_op jit(solution)/shard_map/ppermute | solution.py:382
  23.9 1.2 %collective-permute-start.3 = (bf16[2,64,256]{2,1,0:T(8,128)(2,1)S(1)}, bf16[2,64,256]{2,1,0:T(8,128)(2,1)S(1)}, u32[]{:S(2)}, u32[]{:S(2)}) collective-permute-start(bf16[2,64,256]{2,1,0:T(8,128)(2,1)S(1)} %pad_maximum_fusion), channel_id=1, source_target_pairs={{0,16},{16,0},{32,48},{48,32},{1,17},{17,1},{33,49},{49,33},{2,18}... | collective-permute-start | bytes 196616 | tf_op jit(solution)/shard_map/ppermute | solution.py:382
  25.1 4.7 %collective-permute-start.1 = (bf16[4,48,1024]{2,1,0:T(8,128)(2,1)S(1)}, bf16[4,48,1024]{2,1,0:T(8,128)(2,1)S(1)}, u32[]{:S(2)}, u32[]{:S(2)}) collective-permute-start(bf16[4,48,1024]{2,1,0:T(8,128)(2,1)S(1)} %get-tuple-element.51), channel_id=1, source_target_pairs={{0,192},{64,0},{128,64},{192,128},{1,193},{65,1},{129,65},{193,129... | collective-permute-start | bytes 1179656 | tf_op jit(solution)/shard_map/ppermute | solution.py:442
  29.9 8.5 %pairs_low.1 = (f32[9,32,1024]{2,1,0:T(8,128)S(1)}, f32[8,128]{1,0:T(8,128)S(1)}) custom-call(s32[2,2,2]{2,1,0:T(2,128)S(1)} %copy-done.2, bf16[9,48,1024]{2,1,0:T(8,128)(2,1)S(1)} %get-tuple-element.43.refs_1_, bf16[9,48,1024]{2,1,0:T(8,128)(2,1)S(1)} %get-tuple-element.42.refs_2_.pay, bf16[8,48,1024]{2,1,0:T(8,128)(2,1)S(1)} %get-tuple-element.41.refs_3_.fb, ...), custom_call_target="tpu_custom_call" | custom-call | flops 12000000000 | bytes 4194304 | tf_op jit(solution)/shard_map/pairs_low/pallas_call | solution.py:428
  38.5 1.7 %collective-permute-start.9 = (bf16[8,64,256]{2,1,0:T(8,128)(2,1)S(1)}, bf16[8,64,256]{2,1,0:T(8,128)(2,1)S(1)}, u32[]{:S(2)}, u32[]{:S(2)}) collective-permute-start(bf16[8,64,256]{2,1,0:T(8,128)(2,1)S(1)} %get-tuple-element.81), channel_id=1, source_target_pairs={{0,6},{1,7},{2,4},{3,5},{4,2},{5,3},{6,0},{7,1},{8,14},{9,15},{10,... | collective-permute-start | bytes 786440 | tf_op jit(solution)/shard_map/ppermute | solution.py:382
  40.2 1.6 %collective-permute-start.7 = (bf16[8,64,256]{2,1,0:T(8,128)(2,1)S(1)}, bf16[8,64,256]{2,1,0:T(8,128)(2,1)S(1)}, u32[]{:S(2)}, u32[]{:S(2)}) collective-permute-start(bf16[8,64,256]{2,1,0:T(8,128)(2,1)S(1)} %get-tuple-element.81), channel_id=1, source_target_pairs={{0,2},{1,3},{2,0},{3,1},{4,6},{5,7},{6,4},{7,5},{8,10},{9,11},{10,... | collective-permute-start | bytes 786440 | tf_op jit(solution)/shard_map/ppermute | solution.py:382
  41.8 1.1 %collective-permute-start.6 = (bf16[4,48,1024]{2,1,0:T(8,128)(2,1)S(1)}, bf16[4,48,1024]{2,1,0:T(8,128)(2,1)S(1)}, u32[]{:S(2)}, u32[]{:S(2)}) collective-permute-start(bf16[4,48,1024]{2,1,0:T(8,128)(2,1)S(1)} %get-tuple-element.58), channel_id=1, source_target_pairs={{0,48},{16,0},{32,16},{48,32},{1,49},{17,1},{33,17},{49,33},{2,50}... | collective-permute-start | bytes 1179656 | tf_op jit(solution)/shard_map/ppermute | solution.py:442
  42.9 8.2 %pairs_high.1 = (f32[9,32,1024]{2,1,0:T(8,128)S(1)}, f32[8,128]{1,0:T(8,128)S(1)}) custom-call(s32[2,2,2]{2,1,0:T(2,128)S(1)} %copy-done.2, bf16[9,48,1024]{2,1,0:T(8,128)(2,1)S(1)} %get-tuple-element.43.refs_1_, bf16[9,48,1024]{2,1,0:T(8,128)(2,1)S(1)} %get-tuple-element.42.refs_2_.pay, bf16[8,48,1024]{2,1,0:T(8,128)(2,1)S(1)} %get-tuple-element.41.refs_3_.fb, ...), custom_call_target="tpu_custom_call" | custom-call | flops 12000000000 | bytes 4194304 | tf_op jit(solution)/shard_map/pairs_high/pallas_call | solution.py:428
  51.9 4.8 %collective-permute-start.13 = (bf16[32,64,256]{2,1,0:T(8,128)(2,1)S(1)}, bf16[32,64,256]{2,1,0:T(8,128)(2,1)S(1)}, u32[]{:S(2)}, u32[]{:S(2)}) collective-permute-start(bf16[32,64,256]{2,1,0:T(8,128)(2,1)S(1)} %constant_dynamic-update-slice_fusion.5.here), channel_id=1, source_target_pairs={{0,1},{1,0},{2,3},{3,2},{4,5},{5,4},{6,7},{7,6},{8,9},{9,8},{10,11... | collective-permute-start | bytes 3145736 | tf_op jit(solution)/shard_map/ppermute | solution.py:382
  56.7 15.1 %face_tiles.1 = (f32[8,32,1024]{2,1,0:T(8,128)S(1)}, f32[4,32,1024]{2,1,0:T(8,128)S(1)}, f32[4,32,1024]{2,1,0:T(8,128)S(1)}, f32[4,32,1024]{2,1,0:T(8,128)}, f32[32,128]{1,0:T(8,128)S(1)}) custom-call(s32[2,2,2]{2,1,0:T(2,128)S(1)} %copy-done.2, bf16[8,48,1024]{2,1,0:T(8,128)(2,1)S(1)} %get-tuple-element.41.refs_3_.fb, ...), custom_call_target="tpu_custom_call" | custom-call | flops 12000000000 | bytes 4194304 | tf_op jit(solution)/shard_map/face_tiles/pallas_call | solution.py:462
  71.8 0.9 collective-permute-start.11
  72.7 2.9 %collective-permute-start.12 = (f32[4,32,1024]{2,1,0:T(8,128)S(1)}, f32[4,32,1024]{2,1,0:T(8,128)}, u32[]{:S(2)}, u32[]{:S(2)}) collective-permute-start(f32[4,32,1024]{2,1,0:T(8,128)S(1)} %get-tuple-element.69), channel_id=1, source_target_pairs={{0,16},{16,32},{32,48},{48,0},{1,17},{17,33},{33,49},{49,1},{2,18}... | collective-permute-start | bytes 1572872 | tf_op jit(solution)/shard_map/ppermute | solution.py:442
  75.6 4.6 %locals.1 = (bf16[8,64,128]{2,1,0:T(8,128)(2,1)S(1)}, f32[256,1,128]{2,1,0:T(1,128)}) custom-call(s32[2,2,2]{2,1,0:T(2,128)S(1)} %copy-done.2, s32[2,64]{1,0:T(2,128)S(1)} %bitcast.14, s32[2,64]{1,0:T(2,128)S(1)} %bitcast.15, bf16[32,64,256]{2,1,0:T(8,128)(2,1)S(1)} %constant_dynamic-update-slice_fusion.5.here, ...), custom_call_target="tpu_custom_call" | custom-call | tf_op jit(solution)/shard_map/locals/pallas_call | solution.py:481
  80.1 13.4 %all-to-all-start = ((f32[256,1,128]{2,1,0:T(1,128)}), f32[256,1,128]{2,1,0:T(1,128)S(1)}, u32[]{:S(2)}, u32[]{:S(2)}) async-start(f32[256,1,128]{2,1,0:T(1,128)} %get-tuple-element.78), calls=%async_computation | async-start | bytes 262144 | tf_op jit(solution)/shard_map/all_to_all | solution.py:493
  93.6 1.2 %copy-done.7 = f32[8,32,1024]{2,1,0:T(8,128)S(1)} copy-done((f32[8,32,1024]{2,1,0:T(8,128)S(1)}, f32[8,32,1024]{2,1,0:T(8,128)}, u32[]{:S(2)}) %copy-start.7) | copy-done | bytes 1048600
  94.8 2.3 %total.1 = (bf16[8,32,1024]{2,1,0:T(8,128)(2,1)}, f32[8,128]{1,0:T(8,128)S(1)}) custom-call(s32[2,2,2]{2,1,0:T(2,128)S(1)} %copy-done.3, f32[8,32,1024]{2,1,0:T(8,128)S(1)} %copy-done.7, f32[4,32,1024]{2,1,0:T(8,128)S(1)} %collective-permute-done.10.r2, f32[4,32,1024]{2,1,0:T(8,128)S(1)} %collective-permute-done.11.r0, ...), custom_call_target="tpu_custom_call" | custom-call | flops 12000000000 | bytes 4194304 | tf_op jit(solution)/shard_map/total/pallas_call | solution.py:494
  97.1 9.5 %all-to-all-done.gathered = f32[256,1,128]{2,1,0:T(1,128)S(1)} async-done(((f32[256,1,128]{2,1,0:T(1,128)}), f32[256,1,128]{2,1,0:T(1,128)S(1)}, u32[]{:S(2)}, u32[]{:S(2)}) %all-to-all-start) | async-done | bytes 131104 | tf_op jit(solution)/shard_map/all_to_all | solution.py:493
  106.6 0.9 quad.1
  (42 shorter events, 1.5 us)
Async XLA Ops:
  0.6 1.0 copy-start
  1.7 0.9 copy-start.1
  2.6 0.7 copy-start.2
  5.4 16.0 %collective-permute-start = (bf16[1,64,256]{2,1,0:T(8,128)(2,1)S(1)}, bf16[1,64,256]{2,1,0:T(8,128)(2,1)S(1)}, u32[]{:S(2)}, u32[]{:S(2)}) collective-permute-start(bf16[1,64,256]{2,1,0:T(8,128)(2,1)S(1)} %bitcast.11), channel_id=1, source_target_pairs={{0,8},{1,9},{2,10},{3,11},{4,12},{5,13},{6,14},{7,15},{8,0},{9,1},... | collective-permute-start | bytes 98312 | tf_op jit(solution)/shard_map/ppermute | solution.py:382
  13.2 25.2 %collective-permute-start.2 = (bf16[4,48,1024]{2,1,0:T(8,128)(2,1)S(1)}, bf16[4,48,1024]{2,1,0:T(8,128)(2,1)S(1)}, u32[]{:S(2)}, u32[]{:S(2)}) collective-permute-start(bf16[4,48,1024]{2,1,0:T(8,128)(2,1)S(1)} %get-tuple-element.52), channel_id=1, source_target_pairs={{0,15},{1,0},{2,1},{3,2},{4,3},{5,4},{6,5},{7,6},{8,7},{9,8},{10,9... | collective-permute-start | bytes 1179656 | tf_op jit(solution)/shard_map/ppermute | solution.py:442
  21.5 16.9 %collective-permute-start.5 = (bf16[2,64,256]{2,1,0:T(8,128)(2,1)S(1)}, bf16[2,64,256]{2,1,0:T(8,128)(2,1)S(1)}, u32[]{:S(2)}, u32[]{:S(2)}) collective-permute-start(bf16[2,64,256]{2,1,0:T(8,128)(2,1)S(1)} %pad_maximum_fusion), channel_id=1, source_target_pairs={{0,48},{16,32},{32,16},{48,0},{1,49},{17,33},{33,17},{49,1},{2,50}... | collective-permute-start | bytes 196616 | tf_op jit(solution)/shard_map/ppermute | solution.py:382
  23.9 14.5 %collective-permute-start.4 = (bf16[2,64,256]{2,1,0:T(8,128)(2,1)S(1)}, bf16[2,64,256]{2,1,0:T(8,128)(2,1)S(1)}, u32[]{:S(2)}, u32[]{:S(2)}) collective-permute-start(bf16[2,64,256]{2,1,0:T(8,128)(2,1)S(1)} %pad_maximum_fusion), channel_id=1, source_target_pairs={{0,32},{16,48},{32,0},{48,16},{1,33},{17,49},{33,1},{49,17},{2,34}... | collective-permute-start | bytes 196616 | tf_op jit(solution)/shard_map/ppermute | solution.py:382
  23.9 14.5 %collective-permute-start.3 = (bf16[2,64,256]{2,1,0:T(8,128)(2,1)S(1)}, bf16[2,64,256]{2,1,0:T(8,128)(2,1)S(1)}, u32[]{:S(2)}, u32[]{:S(2)}) collective-permute-start(bf16[2,64,256]{2,1,0:T(8,128)(2,1)S(1)} %pad_maximum_fusion), channel_id=1, source_target_pairs={{0,16},{16,0},{32,48},{48,32},{1,17},{17,1},{33,49},{49,33},{2,18}... | collective-permute-start | bytes 196616 | tf_op jit(solution)/shard_map/ppermute | solution.py:382
  25.1 13.3 %collective-permute-start.1 = (bf16[4,48,1024]{2,1,0:T(8,128)(2,1)S(1)}, bf16[4,48,1024]{2,1,0:T(8,128)(2,1)S(1)}, u32[]{:S(2)}, u32[]{:S(2)}) collective-permute-start(bf16[4,48,1024]{2,1,0:T(8,128)(2,1)S(1)} %get-tuple-element.51), channel_id=1, source_target_pairs={{0,192},{64,0},{128,64},{192,128},{1,193},{65,1},{129,65},{193,129... | collective-permute-start | bytes 1179656 | tf_op jit(solution)/shard_map/ppermute | solution.py:442
  38.5 13.1 %collective-permute-start.9 = (bf16[8,64,256]{2,1,0:T(8,128)(2,1)S(1)}, bf16[8,64,256]{2,1,0:T(8,128)(2,1)S(1)}, u32[]{:S(2)}, u32[]{:S(2)}) collective-permute-start(bf16[8,64,256]{2,1,0:T(8,128)(2,1)S(1)} %get-tuple-element.81), channel_id=1, source_target_pairs={{0,6},{1,7},{2,4},{3,5},{4,2},{5,3},{6,0},{7,1},{8,14},{9,15},{10,... | collective-permute-start | bytes 786440 | tf_op jit(solution)/shard_map/ppermute | solution.py:382
  40.2 11.4 %collective-permute-start.8 = (bf16[8,64,256]{2,1,0:T(8,128)(2,1)S(1)}, bf16[8,64,256]{2,1,0:T(8,128)(2,1)S(1)}, u32[]{:S(2)}, u32[]{:S(2)}) collective-permute-start(bf16[8,64,256]{2,1,0:T(8,128)(2,1)S(1)} %get-tuple-element.81), channel_id=1, source_target_pairs={{0,4},{1,5},{2,6},{3,7},{4,0},{5,1},{6,2},{7,3},{8,12},{9,13},{10,... | collective-permute-start | bytes 786440 | tf_op jit(solution)/shard_map/ppermute | solution.py:382
  40.2 11.5 %collective-permute-start.7 = (bf16[8,64,256]{2,1,0:T(8,128)(2,1)S(1)}, bf16[8,64,256]{2,1,0:T(8,128)(2,1)S(1)}, u32[]{:S(2)}, u32[]{:S(2)}) collective-permute-start(bf16[8,64,256]{2,1,0:T(8,128)(2,1)S(1)} %get-tuple-element.81), channel_id=1, source_target_pairs={{0,2},{1,3},{2,0},{3,1},{4,6},{5,7},{6,4},{7,5},{8,10},{9,11},{10,... | collective-permute-start | bytes 786440 | tf_op jit(solution)/shard_map/ppermute | solution.py:382
  41.8 9.9 %collective-permute-start.6 = (bf16[4,48,1024]{2,1,0:T(8,128)(2,1)S(1)}, bf16[4,48,1024]{2,1,0:T(8,128)(2,1)S(1)}, u32[]{:S(2)}, u32[]{:S(2)}) collective-permute-start(bf16[4,48,1024]{2,1,0:T(8,128)(2,1)S(1)} %get-tuple-element.58), channel_id=1, source_target_pairs={{0,48},{16,0},{32,16},{48,32},{1,49},{17,1},{33,17},{49,33},{2,50}... | collective-permute-start | bytes 1179656 | tf_op jit(solution)/shard_map/ppermute | solution.py:442
  51.9 23.7 %collective-permute-start.13 = (bf16[32,64,256]{2,1,0:T(8,128)(2,1)S(1)}, bf16[32,64,256]{2,1,0:T(8,128)(2,1)S(1)}, u32[]{:S(2)}, u32[]{:S(2)}) collective-permute-start(bf16[32,64,256]{2,1,0:T(8,128)(2,1)S(1)} %constant_dynamic-update-slice_fusion.5.here), channel_id=1, source_target_pairs={{0,1},{1,0},{2,3},{3,2},{4,5},{5,4},{6,7},{7,6},{8,9},{9,8},{10,11... | collective-permute-start | bytes 3145736 | tf_op jit(solution)/shard_map/ppermute | solution.py:382
  56.7 18.9 %copy-start.4 = (s32[1,1,1,64,2]{3,4,2,1,0:T(2,128)S(1)}, s32[1,1,1,64,2]{3,4,2,1,0:T(2,128)}, u32[]{:S(2)}) copy-start(s32[1,1,1,64,2]{3,4,2,1,0:T(2,128)} %param.8) | copy-start | bytes 1540
  56.7 18.9 %copy-start.5 = (s32[1,1,1,64,2]{3,4,2,1,0:T(2,128)S(1)}, s32[1,1,1,64,2]{3,4,2,1,0:T(2,128)}, u32[]{:S(2)}) copy-start(s32[1,1,1,64,2]{3,4,2,1,0:T(2,128)} %param.9) | copy-start | bytes 1540
  71.8 8.4 %copy-start.6 = (f32[8,32,1024]{2,1,0:T(8,128)}, f32[8,32,1024]{2,1,0:T(8,128)S(1)}, u32[]{:S(2)}) copy-start(f32[8,32,1024]{2,1,0:T(8,128)S(1)} %get-tuple-element.66.near) | copy-start | bytes 3145732
  71.8 21.8 %collective-permute-start.10 = (f32[4,32,1024]{2,1,0:T(8,128)}, f32[4,32,1024]{2,1,0:T(8,128)S(1)}, u32[]{:S(2)}, u32[]{:S(2)}) collective-permute-start(f32[4,32,1024]{2,1,0:T(8,128)} %get-tuple-element.67), channel_id=1, source_target_pairs={{0,1},{1,2},{2,3},{3,4},{4,5},{5,6},{6,7},{7,8},{8,9},{9,10},{10,1... | collective-permute-start | bytes 1572872 | tf_op jit(solution)/shard_map/ppermute | solution.py:442
  71.8 21.8 %collective-permute-start.11 = (f32[4,32,1024]{2,1,0:T(8,128)S(1)}, f32[4,32,1024]{2,1,0:T(8,128)S(1)}, u32[]{:S(2)}, u32[]{:S(2)}) collective-permute-start(f32[4,32,1024]{2,1,0:T(8,128)S(1)} %get-tuple-element.68), channel_id=1, source_target_pairs={{0,64},{64,128},{128,192},{192,0},{1,65},{65,129},{129,193},{193,1... | collective-permute-start | bytes 1572872 | tf_op jit(solution)/shard_map/ppermute | solution.py:442
  72.7 20.9 %collective-permute-start.12 = (f32[4,32,1024]{2,1,0:T(8,128)S(1)}, f32[4,32,1024]{2,1,0:T(8,128)}, u32[]{:S(2)}, u32[]{:S(2)}) collective-permute-start(f32[4,32,1024]{2,1,0:T(8,128)S(1)} %get-tuple-element.69), channel_id=1, source_target_pairs={{0,16},{16,32},{32,48},{48,0},{1,17},{17,33},{33,49},{49,1},{2,18}... | collective-permute-start | bytes 1572872 | tf_op jit(solution)/shard_map/ppermute | solution.py:442
  75.5 18.1 %copy-start.3 = (s32[2,2,2]{2,1,0:T(2,128)S(1)}, s32[2,2,2]{2,1,0:T(2,128)}, u32[]{:S(2)}) copy-start(s32[2,2,2]{2,1,0:T(2,128)} %counts.7) | copy-start | bytes 100
  80.1 26.4 %all-to-all-start = ((f32[256,1,128]{2,1,0:T(1,128)}), f32[256,1,128]{2,1,0:T(1,128)S(1)}, u32[]{:S(2)}, u32[]{:S(2)}) async-start(f32[256,1,128]{2,1,0:T(1,128)} %get-tuple-element.78), calls=%async_computation | async-start | bytes 262144 | tf_op jit(solution)/shard_map/all_to_all | solution.py:493
  93.6 1.2 %copy-start.7 = (f32[8,32,1024]{2,1,0:T(8,128)S(1)}, f32[8,32,1024]{2,1,0:T(8,128)}, u32[]{:S(2)}) copy-start(f32[8,32,1024]{2,1,0:T(8,128)} %copy-done.6) | copy-start | bytes 3145732

commit v3 on v2

--- a/solution.py
+++ b/solution.py
@@ -191,7 +191,19 @@
                 use(t + 1, 1)
                 return carry
 
-            lax.fori_loop(0, (total + 1) >> 1, body, 0)
+            whole = (total - 1) >> 1
+            lax.fori_loop(0, whole, body, 0)
+            last = first_step + 2 * whole
+
+            @pl.when((total & 1) == 1)
+            def _():
+                use(last, 0)
+
+            @pl.when((total & 1) == 0)
+            def _():
+                make(last + 1, 1)
+                use(last, 0)
+                use(last + 1, 1)
 
 
 INNER = {4: (0,), 2: (0,), 1: (0,), 6: (2, 4), 5: (1, 4), 3: (1, 2), 7: (3, 5, 6)}
@@ -451,12 +463,12 @@
     more = [xor_permute(block, "gy", k) for k in (1, 2, 3)]
     got[0] = along(0, face_x, -1)
     acc, tick = inner("pairs_low", [1, 2, 4, 3], lambda b: INNER[b], True, None, tick)
-    tick, got[0], got[2], face_y, *more = join("join_second", tick, got[0], got[2], faces[1], *more)
+    tick, got[2], face_y, *more = join("join_second", tick, got[2], faces[1], *more)
     block = jnp.concatenate([block] + more, axis=0)
     more = [xor_permute(block, "gz", 2 * k) for k in (1, 2, 3)]
     got[1] = along(1, face_y, -1)
     acc, tick = inner("pairs_high", [5, 6, 7], lambda b: INNER[b], True, acc, tick)
-    tick, got[1], *more = join("join_third", tick, got[1], *more)
+    tick, got[0], got[1], *more = join("join_third", tick, got[0], got[1], *more)
     block = jnp.concatenate([block] + more, axis=0)
     other = xor_permute(block, "gz", 1)
     near, *backs, probe_sums = pl.pallas_call(

time: 107 us -> 106 us (level); the launches traced: 107 us -> 105 us
  Pallas kernels: 48.9 us -> 44.5 us
  starting transfers between devices: 43.6 us -> 45.4 us
    pallas_call x3, Pallas kernels: 24 us -> 19.9 us  [inner(): pl.pallas_call(kernel, out_shape=[shape((BOXES + 1, 32, points), F32), sh...]
    all_to_all x1, starting transfers between devices: 13.4 us -> 15.5 us  [shards(): gathered = lax.all_to_all(sums, ('gx', 'gy', 'gz'), 0, 0, tiled=True)]
  transfers between devices with their start and end apart: 15 -> 15, of which waited for: 3 -> 3; matrix products, arithmetic and copies ran while one was open for 0% -> 0% of each run, Pallas kernels for 43% -> 40%
where the time goes in v3:
time: 106 us; the launch traced here: 105 us
  starting transfers between devices  45.4 us (43%)
  Pallas kernels  44.5 us (42%)
  waiting for transfers between devices  9.77 us (9%)
  local copies, waits for them, and re-layouts  3.95 us (4%)
    pallas_call x3, Pallas kernels, inner(): pl.pallas_call(kernel, out_shape=[shape((BOXES + 1, 32, points), F32), sh...  19.9 us
    ppermute x8, starting transfers between devices, xor_permute(): return lax.ppermute(value, axis, [(i, i ^ bits) for i in range(count)])  19.1 us
    all_to_all x1, starting transfers between devices, shards(): gathered = lax.all_to_all(sums, ('gx', 'gy', 'gz'), 0, 0, tiled=True)  15.5 us
    pallas_call x1, Pallas kernels, shards(): pl.pallas_call(outer_kernel, out_shape=[acc_shape] + [shape((4, 32, point...  15.1 us
    ppermute x6, starting transfers between devices, along(): lax.ppermute(value, name, [(i, (i + step) % size) for i in range(size)])  10.8 us
    all_to_all x1, waiting for transfers between devices, shards(): gathered = lax.all_to_all(sums, ('gx', 'gy', 'gz'), 0, 0, tiled=True)  9.46 us
    pallas_call x1, Pallas kernels, shards(): pl.pallas_call(local_kernel, out_shape=[shape((BOXES, 64, 128), BF16), sh...  4.29 us
    unnamed x23, local copies, waits for them, and re-layouts  3.93 us
  transfers between devices with their start and end apart: 15, of which 3 were waited for; matrix products, arithmetic and copies ran while one was open for 0% of the time, Pallas kernels for 40%

profile of v3, /device:TPU:1, one launch (start us, length us, event | category | flops | bytes accessed | tf_op | source)
XLA Modules:
  0.0 104.5 jit_solution(16148023407121500146)
XLA Ops:
  0.6 1.0 copy-done
  1.7 0.9 copy-done.1
  2.6 0.7 copy-done.2
  3.2 2.2 %prep.1 = (bf16[9,48,1024]{2,1,0:T(8,128)(2,1)S(1)}, bf16[9,48,1024]{2,1,0:T(8,128)(2,1)S(1)}, bf16[8,48,1024]{2,1,0:T(8,128)(2,1)S(1)}, bf16[8,64,1024]{2,1,0:T...) custom-call(s32[2,2,2]{2,1,0:T(2,128)S(1)} %copy-done.2, ...), custom_call_target="tpu_custom_call" | custom-call | tf_op jit(solution)/shard_map/prep/pallas_call | solution.py:401
  5.4 7.8 %collective-permute-start = (bf16[1,64,256]{2,1,0:T(8,128)(2,1)S(1)}, bf16[1,64,256]{2,1,0:T(8,128)(2,1)S(1)}, u32[]{:S(2)}, u32[]{:S(2)}) collective-permute-start(bf16[1,64,256]{2,1,0:T(8,128)(2,1)S(1)} %bitcast.11), channel_id=1, source_target_pairs={{0,8},{1,9},{2,10},{3,11},{4,12},{5,13},{6,14},{7,15},{8,0},{9,1},... | collective-permute-start | bytes 98312 | tf_op jit(solution)/shard_map/ppermute | solution.py:394
  13.2 1.0 collective-permute-start.1
  14.2 6.6 %self_tiles.1 = (f32[9,32,1024]{2,1,0:T(8,128)S(1)}, f32[8,128]{1,0:T(8,128)S(1)}) custom-call(s32[2,2,2]{2,1,0:T(2,128)S(1)} %copy-done.2, bf16[9,48,1024]{2,1,0:T(8,128)(2,1)S(1)} %get-tuple-element.43.refs_1_, bf16[9,48,1024]{2,1,0:T(8,128)(2,1)S(1)} %get-tuple-element.42.refs_2_.pay, bf16[8,48,1024]{2,1,0:T(8,128)(2,1)S(1)} %get-tuple-element.41.refs_3_.fb, ...), custom_call_target="tpu_custom_call" | custom-call | flops 12000000000 | bytes 4194304 | tf_op jit(solution)/shard_map/self_tiles/pallas_call | solution.py:440
  20.9 3.8 %collective-permute-start.4 = (bf16[2,64,256]{2,1,0:T(8,128)(2,1)S(1)}, bf16[2,64,256]{2,1,0:T(8,128)(2,1)S(1)}, u32[]{:S(2)}, u32[]{:S(2)}) collective-permute-start(bf16[2,64,256]{2,1,0:T(8,128)(2,1)S(1)} %pad_maximum_fusion), channel_id=1, source_target_pairs={{0,48},{16,32},{32,16},{48,0},{1,49},{17,33},{33,17},{49,1},{2,50}... | collective-permute-start | bytes 196616 | tf_op jit(solution)/shard_map/ppermute | solution.py:394
  25.0 3.8 %collective-permute-start.5 = (bf16[4,48,1024]{2,1,0:T(8,128)(2,1)S(1)}, bf16[4,48,1024]{2,1,0:T(8,128)(2,1)S(1)}, u32[]{:S(2)}, u32[]{:S(2)}) collective-permute-start(bf16[4,48,1024]{2,1,0:T(8,128)(2,1)S(1)} %get-tuple-element.57), channel_id=1, source_target_pairs={{0,192},{64,0},{128,64},{192,128},{1,193},{65,1},{129,65},{193,129... | collective-permute-start | bytes 1179656 | tf_op jit(solution)/shard_map/ppermute | solution.py:454
  28.8 6.4 %pairs_low.1 = (f32[9,32,1024]{2,1,0:T(8,128)S(1)}, f32[8,128]{1,0:T(8,128)S(1)}) custom-call(s32[2,2,2]{2,1,0:T(2,128)S(1)} %copy-done.2, bf16[9,48,1024]{2,1,0:T(8,128)(2,1)S(1)} %get-tuple-element.43.refs_1_, bf16[9,48,1024]{2,1,0:T(8,128)(2,1)S(1)} %get-tuple-element.42.refs_2_.pay, bf16[8,48,1024]{2,1,0:T(8,128)(2,1)S(1)} %get-tuple-element.41.refs_3_.fb, ...), custom_call_target="tpu_custom_call" | custom-call | flops 12000000000 | bytes 4194304 | tf_op jit(solution)/shard_map/pairs_low/pallas_call | solution.py:440
  35.4 2.6 %collective-permute-start.9 = (bf16[8,64,256]{2,1,0:T(8,128)(2,1)S(1)}, bf16[8,64,256]{2,1,0:T(8,128)(2,1)S(1)}, u32[]{:S(2)}, u32[]{:S(2)}) collective-permute-start(bf16[8,64,256]{2,1,0:T(8,128)(2,1)S(1)} %get-tuple-element.81), channel_id=1, source_target_pairs={{0,6},{1,7},{2,4},{3,5},{4,2},{5,3},{6,0},{7,1},{8,14},{9,15},{10,... | collective-permute-start | bytes 786440 | tf_op jit(solution)/shard_map/ppermute | solution.py:394
  37.9 1.3 %collective-permute-start.8 = (bf16[8,64,256]{2,1,0:T(8,128)(2,1)S(1)}, bf16[8,64,256]{2,1,0:T(8,128)(2,1)S(1)}, u32[]{:S(2)}, u32[]{:S(2)}) collective-permute-start(bf16[8,64,256]{2,1,0:T(8,128)(2,1)S(1)} %get-tuple-element.81), channel_id=1, source_target_pairs={{0,4},{1,5},{2,6},{3,7},{4,0},{5,1},{6,2},{7,3},{8,12},{9,13},{10,... | collective-permute-start | bytes 786440 | tf_op jit(solution)/shard_map/ppermute | solution.py:394
  39.3 2.4 %collective-permute-start.6 = (bf16[4,48,1024]{2,1,0:T(8,128)(2,1)S(1)}, bf16[4,48,1024]{2,1,0:T(8,128)(2,1)S(1)}, u32[]{:S(2)}, u32[]{:S(2)}) collective-permute-start(bf16[4,48,1024]{2,1,0:T(8,128)(2,1)S(1)} %get-tuple-element.58), channel_id=1, source_target_pairs={{0,48},{16,0},{32,16},{48,32},{1,49},{17,1},{33,17},{49,33},{2,50}... | collective-permute-start | bytes 1179656 | tf_op jit(solution)/shard_map/ppermute | solution.py:454
  41.7 6.8 %pairs_high.1 = (f32[9,32,1024]{2,1,0:T(8,128)S(1)}, f32[8,128]{1,0:T(8,128)S(1)}) custom-call(s32[2,2,2]{2,1,0:T(2,128)S(1)} %copy-done.2, bf16[9,48,1024]{2,1,0:T(8,128)(2,1)S(1)} %get-tuple-element.43.refs_1_, bf16[9,48,1024]{2,1,0:T(8,128)(2,1)S(1)} %get-tuple-element.42.refs_2_.pay, bf16[8,48,1024]{2,1,0:T(8,128)(2,1)S(1)} %get-tuple-element.41.refs_3_.fb, ...), custom_call_target="tpu_custom_call" | custom-call | flops 12000000000 | bytes 4194304 | tf_op jit(solution)/shard_map/pairs_high/pallas_call | solution.py:440
  48.9 3.2 %collective-permute-start.13 = (bf16[32,64,256]{2,1,0:T(8,128)(2,1)S(1)}, bf16[32,64,256]{2,1,0:T(8,128)(2,1)S(1)}, u32[]{:S(2)}, u32[]{:S(2)}) collective-permute-start(bf16[32,64,256]{2,1,0:T(8,128)(2,1)S(1)} %constant_dynamic-update-slice_fusion.5.here), channel_id=1, source_target_pairs={{0,1},{1,0},{2,3},{3,2},{4,5},{5,4},{6,7},{7,6},{8,9},{9,8},{10,11... | collective-permute-start | bytes 3145736 | tf_op jit(solution)/shard_map/ppermute | solution.py:394
  52.1 15.1 %face_tiles.1 = (f32[8,32,1024]{2,1,0:T(8,128)S(1)}, f32[4,32,1024]{2,1,0:T(8,128)S(1)}, f32[4,32,1024]{2,1,0:T(8,128)S(1)}, f32[4,32,1024]{2,1,0:T(8,128)}, f32[32,128]{1,0:T(8,128)S(1)}) custom-call(s32[2,2,2]{2,1,0:T(2,128)S(1)} %copy-done.2, bf16[8,48,1024]{2,1,0:T(8,128)(2,1)S(1)} %get-tuple-element.41.refs_3_.fb, ...), custom_call_target="tpu_custom_call" | custom-call | flops 12000000000 | bytes 4194304 | tf_op jit(solution)/shard_map/face_tiles/pallas_call | solution.py:474
  67.2 1.2 %collective-permute-start.10 = (f32[4,32,1024]{2,1,0:T(8,128)}, f32[4,32,1024]{2,1,0:T(8,128)S(1)}, u32[]{:S(2)}, u32[]{:S(2)}) collective-permute-start(f32[4,32,1024]{2,1,0:T(8,128)} %get-tuple-element.67), channel_id=1, source_target_pairs={{0,1},{1,2},{2,3},{3,4},{4,5},{5,6},{6,7},{7,8},{8,9},{9,10},{10,1... | collective-permute-start | bytes 1572872 | tf_op jit(solution)/shard_map/ppermute | solution.py:454
  68.4 2.5 %collective-permute-start.11 = (f32[4,32,1024]{2,1,0:T(8,128)S(1)}, f32[4,32,1024]{2,1,0:T(8,128)S(1)}, u32[]{:S(2)}, u32[]{:S(2)}) collective-permute-start(f32[4,32,1024]{2,1,0:T(8,128)S(1)} %get-tuple-element.68), channel_id=1, source_target_pairs={{0,64},{64,128},{128,192},{192,0},{1,65},{65,129},{129,193},{193,1... | collective-permute-start | bytes 1572872 | tf_op jit(solution)/shard_map/ppermute | solution.py:454
  70.9 4.3 %locals.1 = (bf16[8,64,128]{2,1,0:T(8,128)(2,1)S(1)}, f32[256,1,128]{2,1,0:T(1,128)}) custom-call(s32[2,2,2]{2,1,0:T(2,128)S(1)} %copy-done.2, s32[2,64]{1,0:T(2,128)S(1)} %bitcast.14, s32[2,64]{1,0:T(2,128)S(1)} %bitcast.15, bf16[32,64,256]{2,1,0:T(8,128)(2,1)S(1)} %constant_dynamic-update-slice_fusion.5.here, ...), custom_call_target="tpu_custom_call" | custom-call | tf_op jit(solution)/shard_map/locals/pallas_call | solution.py:493
  75.2 15.5 %all-to-all-start = ((f32[256,1,128]{2,1,0:T(1,128)}), f32[256,1,128]{2,1,0:T(1,128)S(1)}, u32[]{:S(2)}, u32[]{:S(2)}) async-start(f32[256,1,128]{2,1,0:T(1,128)} %get-tuple-element.78), calls=%async_computation | async-start | bytes 262144 | tf_op jit(solution)/shard_map/all_to_all | solution.py:505
  90.7 1.2 %copy-done.7 = f32[8,32,1024]{2,1,0:T(8,128)S(1)} copy-done((f32[8,32,1024]{2,1,0:T(8,128)S(1)}, f32[8,32,1024]{2,1,0:T(8,128)}, u32[]{:S(2)}) %copy-start.7) | copy-done | bytes 1048600
  91.9 2.3 %total.1 = (bf16[8,32,1024]{2,1,0:T(8,128)(2,1)}, f32[8,128]{1,0:T(8,128)S(1)}) custom-call(s32[2,2,2]{2,1,0:T(2,128)S(1)} %copy-done.3, f32[8,32,1024]{2,1,0:T(8,128)S(1)} %copy-done.7, f32[4,32,1024]{2,1,0:T(8,128)S(1)} %collective-permute-done.10.r2, f32[4,32,1024]{2,1,0:T(8,128)S(1)} %collective-permute-done.11.r0, ...), custom_call_target="tpu_custom_call" | custom-call | flops 12000000000 | bytes 4194304 | tf_op jit(solution)/shard_map/total/pallas_call | solution.py:506
  94.2 9.5 %all-to-all-done.gathered = f32[256,1,128]{2,1,0:T(1,128)S(1)} async-done(((f32[256,1,128]{2,1,0:T(1,128)}), f32[256,1,128]{2,1,0:T(1,128)S(1)}, u32[]{:S(2)}, u32[]{:S(2)}) %all-to-all-start) | async-done | bytes 131104 | tf_op jit(solution)/shard_map/all_to_all | solution.py:505
  103.7 0.9 quad.1
  (42 shorter events, 0.8 us)
Async XLA Ops:
  0.6 1.0 copy-start
  1.7 0.9 copy-start.1
  2.6 0.7 copy-start.2
  5.4 15.4 %collective-permute-start = (bf16[1,64,256]{2,1,0:T(8,128)(2,1)S(1)}, bf16[1,64,256]{2,1,0:T(8,128)(2,1)S(1)}, u32[]{:S(2)}, u32[]{:S(2)}) collective-permute-start(bf16[1,64,256]{2,1,0:T(8,128)(2,1)S(1)} %bitcast.11), channel_id=1, source_target_pairs={{0,8},{1,9},{2,10},{3,11},{4,12},{5,13},{6,14},{7,15},{8,0},{9,1},... | collective-permute-start | bytes 98312 | tf_op jit(solution)/shard_map/ppermute | solution.py:394
  13.2 22.1 %collective-permute-start.1 = (bf16[4,48,1024]{2,1,0:T(8,128)(2,1)S(1)}, bf16[4,48,1024]{2,1,0:T(8,128)(2,1)S(1)}, u32[]{:S(2)}, u32[]{:S(2)}) collective-permute-start(bf16[4,48,1024]{2,1,0:T(8,128)(2,1)S(1)} %get-tuple-element.51), channel_id=1, source_target_pairs={{0,15},{1,0},{2,1},{3,2},{4,3},{5,4},{6,5},{7,6},{8,7},{9,8},{10,9... | collective-permute-start | bytes 1179656 | tf_op jit(solution)/shard_map/ppermute | solution.py:454
  20.9 14.4 %collective-permute-start.4 = (bf16[2,64,256]{2,1,0:T(8,128)(2,1)S(1)}, bf16[2,64,256]{2,1,0:T(8,128)(2,1)S(1)}, u32[]{:S(2)}, u32[]{:S(2)}) collective-permute-start(bf16[2,64,256]{2,1,0:T(8,128)(2,1)S(1)} %pad_maximum_fusion), channel_id=1, source_target_pairs={{0,48},{16,32},{32,16},{48,0},{1,49},{17,33},{33,17},{49,1},{2,50}... | collective-permute-start | bytes 196616 | tf_op jit(solution)/shard_map/ppermute | solution.py:394
  24.6 10.6 %collective-permute-start.3 = (bf16[2,64,256]{2,1,0:T(8,128)(2,1)S(1)}, bf16[2,64,256]{2,1,0:T(8,128)(2,1)S(1)}, u32[]{:S(2)}, u32[]{:S(2)}) collective-permute-start(bf16[2,64,256]{2,1,0:T(8,128)(2,1)S(1)} %pad_maximum_fusion), channel_id=1, source_target_pairs={{0,32},{16,48},{32,0},{48,16},{1,33},{17,49},{33,1},{49,17},{2,34}... | collective-permute-start | bytes 196616 | tf_op jit(solution)/shard_map/ppermute | solution.py:394
  24.6 10.6 %collective-permute-start.2 = (bf16[2,64,256]{2,1,0:T(8,128)(2,1)S(1)}, bf16[2,64,256]{2,1,0:T(8,128)(2,1)S(1)}, u32[]{:S(2)}, u32[]{:S(2)}) collective-permute-start(bf16[2,64,256]{2,1,0:T(8,128)(2,1)S(1)} %pad_maximum_fusion), channel_id=1, source_target_pairs={{0,16},{16,0},{32,48},{48,32},{1,17},{17,1},{33,49},{49,33},{2,18}... | collective-permute-start | bytes 196616 | tf_op jit(solution)/shard_map/ppermute | solution.py:394
  25.0 23.5 %collective-permute-start.5 = (bf16[4,48,1024]{2,1,0:T(8,128)(2,1)S(1)}, bf16[4,48,1024]{2,1,0:T(8,128)(2,1)S(1)}, u32[]{:S(2)}, u32[]{:S(2)}) collective-permute-start(bf16[4,48,1024]{2,1,0:T(8,128)(2,1)S(1)} %get-tuple-element.57), channel_id=1, source_target_pairs={{0,192},{64,0},{128,64},{192,128},{1,193},{65,1},{129,65},{193,129... | collective-permute-start | bytes 1179656 | tf_op jit(solution)/shard_map/ppermute | solution.py:454
  35.4 13.3 %collective-permute-start.9 = (bf16[8,64,256]{2,1,0:T(8,128)(2,1)S(1)}, bf16[8,64,256]{2,1,0:T(8,128)(2,1)S(1)}, u32[]{:S(2)}, u32[]{:S(2)}) collective-permute-start(bf16[8,64,256]{2,1,0:T(8,128)(2,1)S(1)} %get-tuple-element.81), channel_id=1, source_target_pairs={{0,6},{1,7},{2,4},{3,5},{4,2},{5,3},{6,0},{7,1},{8,14},{9,15},{10,... | collective-permute-start | bytes 786440 | tf_op jit(solution)/shard_map/ppermute | solution.py:394
  37.9 10.8 %collective-permute-start.8 = (bf16[8,64,256]{2,1,0:T(8,128)(2,1)S(1)}, bf16[8,64,256]{2,1,0:T(8,128)(2,1)S(1)}, u32[]{:S(2)}, u32[]{:S(2)}) collective-permute-start(bf16[8,64,256]{2,1,0:T(8,128)(2,1)S(1)} %get-tuple-element.81), channel_id=1, source_target_pairs={{0,4},{1,5},{2,6},{3,7},{4,0},{5,1},{6,2},{7,3},{8,12},{9,13},{10,... | collective-permute-start | bytes 786440 | tf_op jit(solution)/shard_map/ppermute | solution.py:394
  39.3 9.5 %collective-permute-start.7 = (bf16[8,64,256]{2,1,0:T(8,128)(2,1)S(1)}, bf16[8,64,256]{2,1,0:T(8,128)(2,1)S(1)}, u32[]{:S(2)}, u32[]{:S(2)}) collective-permute-start(bf16[8,64,256]{2,1,0:T(8,128)(2,1)S(1)} %get-tuple-element.81), channel_id=1, source_target_pairs={{0,2},{1,3},{2,0},{3,1},{4,6},{5,7},{6,4},{7,5},{8,10},{9,11},{10,... | collective-permute-start | bytes 786440 | tf_op jit(solution)/shard_map/ppermute | solution.py:394
  39.3 9.5 %collective-permute-start.6 = (bf16[4,48,1024]{2,1,0:T(8,128)(2,1)S(1)}, bf16[4,48,1024]{2,1,0:T(8,128)(2,1)S(1)}, u32[]{:S(2)}, u32[]{:S(2)}) collective-permute-start(bf16[4,48,1024]{2,1,0:T(8,128)(2,1)S(1)} %get-tuple-element.58), channel_id=1, source_target_pairs={{0,48},{16,0},{32,16},{48,32},{1,49},{17,1},{33,17},{49,33},{2,50}... | collective-permute-start | bytes 1179656 | tf_op jit(solution)/shard_map/ppermute | solution.py:454
  48.9 22.0 %collective-permute-start.13 = (bf16[32,64,256]{2,1,0:T(8,128)(2,1)S(1)}, bf16[32,64,256]{2,1,0:T(8,128)(2,1)S(1)}, u32[]{:S(2)}, u32[]{:S(2)}) collective-permute-start(bf16[32,64,256]{2,1,0:T(8,128)(2,1)S(1)} %constant_dynamic-update-slice_fusion.5.here), channel_id=1, source_target_pairs={{0,1},{1,0},{2,3},{3,2},{4,5},{5,4},{6,7},{7,6},{8,9},{9,8},{10,11... | collective-permute-start | bytes 3145736 | tf_op jit(solution)/shard_map/ppermute | solution.py:394
  52.1 18.8 %copy-start.4 = (s32[1,1,1,64,2]{3,4,2,1,0:T(2,128)S(1)}, s32[1,1,1,64,2]{3,4,2,1,0:T(2,128)}, u32[]{:S(2)}) copy-start(s32[1,1,1,64,2]{3,4,2,1,0:T(2,128)} %param.8) | copy-start | bytes 1540
  52.1 18.8 %copy-start.5 = (s32[1,1,1,64,2]{3,4,2,1,0:T(2,128)S(1)}, s32[1,1,1,64,2]{3,4,2,1,0:T(2,128)}, u32[]{:S(2)}) copy-start(s32[1,1,1,64,2]{3,4,2,1,0:T(2,128)} %param.9) | copy-start | bytes 1540
  67.2 8.0 %copy-start.6 = (f32[8,32,1024]{2,1,0:T(8,128)}, f32[8,32,1024]{2,1,0:T(8,128)S(1)}, u32[]{:S(2)}) copy-start(f32[8,32,1024]{2,1,0:T(8,128)S(1)} %get-tuple-element.66.near) | copy-start | bytes 3145732
  67.2 23.5 %collective-permute-start.10 = (f32[4,32,1024]{2,1,0:T(8,128)}, f32[4,32,1024]{2,1,0:T(8,128)S(1)}, u32[]{:S(2)}, u32[]{:S(2)}) collective-permute-start(f32[4,32,1024]{2,1,0:T(8,128)} %get-tuple-element.67), channel_id=1, source_target_pairs={{0,1},{1,2},{2,3},{3,4},{4,5},{5,6},{6,7},{7,8},{8,9},{9,10},{10,1... | collective-permute-start | bytes 1572872 | tf_op jit(solution)/shard_map/ppermute | solution.py:454
  68.4 22.3 %collective-permute-start.11 = (f32[4,32,1024]{2,1,0:T(8,128)S(1)}, f32[4,32,1024]{2,1,0:T(8,128)S(1)}, u32[]{:S(2)}, u32[]{:S(2)}) collective-permute-start(f32[4,32,1024]{2,1,0:T(8,128)S(1)} %get-tuple-element.68), channel_id=1, source_target_pairs={{0,64},{64,128},{128,192},{192,0},{1,65},{65,129},{129,193},{193,1... | collective-permute-start | bytes 1572872 | tf_op jit(solution)/shard_map/ppermute | solution.py:454
  70.9 19.8 %collective-permute-start.12 = (f32[4,32,1024]{2,1,0:T(8,128)S(1)}, f32[4,32,1024]{2,1,0:T(8,128)}, u32[]{:S(2)}, u32[]{:S(2)}) collective-permute-start(f32[4,32,1024]{2,1,0:T(8,128)S(1)} %get-tuple-element.69), channel_id=1, source_target_pairs={{0,16},{16,32},{32,48},{48,0},{1,17},{17,33},{33,49},{49,1},{2,18}... | collective-permute-start | bytes 1572872 | tf_op jit(solution)/shard_map/ppermute | solution.py:454
  70.9 19.8 %copy-start.3 = (s32[2,2,2]{2,1,0:T(2,128)S(1)}, s32[2,2,2]{2,1,0:T(2,128)}, u32[]{:S(2)}) copy-start(s32[2,2,2]{2,1,0:T(2,128)} %counts.7) | copy-start | bytes 100
  75.2 28.5 %all-to-all-start = ((f32[256,1,128]{2,1,0:T(1,128)}), f32[256,1,128]{2,1,0:T(1,128)S(1)}, u32[]{:S(2)}, u32[]{:S(2)}) async-start(f32[256,1,128]{2,1,0:T(1,128)} %get-tuple-element.78), calls=%async_computation | async-start | bytes 262144 | tf_op jit(solution)/shard_map/all_to_all | solution.py:505
  90.7 1.2 %copy-start.7 = (f32[8,32,1024]{2,1,0:T(8,128)S(1)}, f32[8,32,1024]{2,1,0:T(8,128)}, u32[]{:S(2)}) copy-start(f32[8,32,1024]{2,1,0:T(8,128)} %copy-done.6) | copy-start | bytes 3145732

commit v4 on v2

--- a/solution.py
+++ b/solution.py
@@ -149,49 +149,71 @@
     def columns(index):
         return pl.ds(pl.multiple_of((index & 7) * CHUNK, CHUNK), CHUNK)
 
+    def flip(t, slot):
+        for h in range(2):
+            index = steps[2 * t + h]
+            flips[slot, h * CHUNK:(h + 1) * CHUNK, :] = fa[index >> 3, :, columns(index)].T
+
+    def make(t, slot, width):
+        target = fb[owner[t], :, 0:width]
+        squares = jnp.dot(flips[slot], target, preferred_element_type=F32)
+        tiles[slot, :, 0:width] = lax.rsqrt(squares).astype(BF16)
+
+    def use(t, slot, width):
+        b = owner[t]
+        first = steps[2 * t]
+        second = steps[2 * t + 1]
+        tile = tiles[slot, :, 0:width]
+        both = jnp.concatenate([vec[first >> 3, 0:32, columns(first)], vec[second >> 3, 0:32, columns(second)]], axis=1)
+        out[b, :, 0:width] += jnp.dot(both, tile, preferred_element_type=F32)
+        if back is not None:
+            sent = lax.dot_general(own[b, 0:32, 0:width], tile, (((1,), (1,)), ((), ())), preferred_element_type=F32)
+            back[first >> 3, :, columns(first)] += sent[:, 0:CHUNK]
+            back[second >> 3, :, columns(second)] += sent[:, CHUNK:]
+
+    def begin(c):
+        if c < len(WIDTHS):
+            flip(c * (REGION // 2), 2 * c)
+            flip(c * (REGION // 2) + 1, 2 * c + 1)
+            make(c * (REGION // 2), 2 * c, WIDTHS[c])
+
+    begin(0)
     for c, width in enumerate(WIDTHS):
         first_step = c * (REGION // 2)
         total = filled[c] >> 1
-
-        def flip(t, slot):
-            for h in range(2):
-                index = steps[2 * t + h]
-                flips[slot, h * CHUNK:(h + 1) * CHUNK, :] = fa[index >> 3, :, columns(index)].T
-
-        def make(t, slot, width=width):
-            target = fb[owner[t], :, 0:width]
-            squares = jnp.dot(flips[slot], target, preferred_element_type=F32)
-            tiles[slot, :, 0:width] = lax.rsqrt(squares).astype(BF16)
-
-        def use(t, slot, width=width):
-            b = owner[t]
-            first = steps[2 * t]
-            second = steps[2 * t + 1]
-            tile = tiles[slot, :, 0:width]
-            both = jnp.concatenate([vec[first >> 3, 0:32, columns(first)], vec[second >> 3, 0:32, columns(second)]], axis=1)
-            out[b, :, 0:width] += jnp.dot(both, tile, preferred_element_type=F32)
-            if back is not None:
-                sent = lax.dot_general(own[b, 0:32, 0:width], tile, (((1,), (1,)), ((), ())), preferred_element_type=F32)
-                back[first >> 3, :, columns(first)] += sent[:, 0:CHUNK]
-                back[second >> 3, :, columns(second)] += sent[:, CHUNK:]
-
-        @pl.when(total > 0)
-        def _(flip=flip, make=make, use=use, first_step=first_step, total=total):
-            flip(first_step, 0)
-            flip(first_step + 1, 1)
-            make(first_step, 0)
-
-            def body(k, carry):
-                t = first_step + 2 * k
-                make(t + 1, 1)
-                flip(t + 2, 0)
-                use(t, 0)
-                make(t + 2, 0)
-                flip(t + 3, 1)
-                use(t + 1, 1)
-                return carry
-
-            lax.fori_loop(0, (total + 1) >> 1, body, 0)
+        even, odd = 2 * c, 2 * c + 1
+
+        def body(k, carry, first_step=first_step, width=width, even=even, odd=odd):
+            t = first_step + 2 * k
+            make(t + 1, odd, width)
+            flip(t + 2, even)
+            use(t, even, width)
+            make(t + 2, even, width)
+            flip(t + 3, odd)
+            use(t + 1, odd, width)
+            return carry
+
+        whole = jnp.maximum(total - 1, 0) >> 1
+        lax.fori_loop(0, whole, body, 0)
+        last = first_step + 2 * whole
+        left = total - 2 * whole
+
+        if c + 1 < len(WIDTHS):
+            @pl.when(left == 0)
+            def _(c=c):
+                begin(c + 1)
+
+        @pl.when(left == 1)
+        def _(c=c, last=last, width=width, even=even):
+            use(last, even, width)
+            begin(c + 1)
+
+        @pl.when(left == 2)
+        def _(c=c, last=last, width=width, even=even, odd=odd):
+            make(last + 1, odd, width)
+            use(last, even, width)
+            begin(c + 1)
+            use(last + 1, odd, width)
 
 
 INNER = {4: (0,), 2: (0,), 1: (0,), 6: (2, 4), 5: (1, 4), 3: (1, 2), 7: (3, 5, 6)}
@@ -332,7 +354,7 @@
     sums[...] = jnp.broadcast_to(row_sums.reshape(1, 1, 128), sums.shape)
 
 
-def total_kernel(counts, near, r2, r0, r1, loc, tab, kv, done):
+def total_kernel(counts, near, r2, r1, r0, loc, tab, kv, done):
     points = tab.shape[-1]
     lane = lax.broadcasted_iota(jnp.int32, (1, points), 1)
     for b in range(BOXES):
@@ -407,8 +429,8 @@
 
     acc_shape = shape((BOXES, 32, points), F32)
     lists = [
-        pltpu.VMEM((2, 2 * CHUNK, points), BF16),
-        pltpu.VMEM((2, 2 * CHUNK, FEATS), BF16),
+        pltpu.VMEM((2 * len(WIDTHS), 2 * CHUNK, points), BF16),
+        pltpu.VMEM((2 * len(WIDTHS), 2 * CHUNK, FEATS), BF16),
         pltpu.SMEM((len(WIDTHS) * REGION,), jnp.int32),
         pltpu.SMEM((len(WIDTHS) * REGION // 2,), jnp.int32),
         pltpu.SMEM((8,), jnp.int32),
@@ -451,12 +473,12 @@
     more = [xor_permute(block, "gy", k) for k in (1, 2, 3)]
     got[0] = along(0, face_x, -1)
     acc, tick = inner("pairs_low", [1, 2, 4, 3], lambda b: INNER[b], True, None, tick)
-    tick, got[0], got[2], face_y, *more = join("join_second", tick, got[0], got[2], faces[1], *more)
+    tick, got[2], face_y, *more = join("join_second", tick, got[2], faces[1], *more)
     block = jnp.concatenate([block] + more, axis=0)
     more = [xor_permute(block, "gz", 2 * k) for k in (1, 2, 3)]
     got[1] = along(1, face_y, -1)
     acc, tick = inner("pairs_high", [5, 6, 7], lambda b: INNER[b], True, acc, tick)
-    tick, got[1], *more = join("join_third", tick, got[1], *more)
+    tick, got[0], got[1], *more = join("join_third", tick, got[0], got[1], *more)
     block = jnp.concatenate([block] + more, axis=0)
     other = xor_permute(block, "gz", 1)
     near, *backs, probe_sums = pl.pallas_call(
@@ -499,7 +521,7 @@
         compiler_params=PARAMS,
         cost_estimate=COST,
         name="total",
-    )(counts, near, returned[2], returned[0], returned[1], loc, tab)
+    )(counts, near, returned[2], returned[1], returned[0], loc, tab)
     quad = pl.pallas_call(
         quad_kernel,
         out_shape=shape((32,), F32),

time: 107 us -> 104 us (0.972); the launches traced: 107 us -> 103 us
  starting transfers between devices: 43.6 us -> 39.5 us
    all_to_all x1, starting transfers between devices: 13.4 us -> 9.89 us  [shards(): gathered = lax.all_to_all(sums, ('gx', 'gy', 'gz'), 0, 0, tiled=True)]
    pallas_call x3, Pallas kernels: 24 us -> 22.8 us  [inner(): pl.pallas_call(kernel, out_shape=[shape((BOXES + 1, 32, points), F32), sh...]
  transfers between devices with their start and end apart: 15 -> 15, of which waited for: 3 -> 2; matrix products, arithmetic and copies ran while one was open for 0% -> 0% of each run, Pallas kernels for 43% -> 44%
where the time goes in v4:
time: 104 us; the launch traced here: 103 us
  Pallas kernels  48.7 us (47%)
  starting transfers between devices  39.5 us (38%)
  waiting for transfers between devices  10.2 us (10%)
  local copies, waits for them, and re-layouts  3.95 us (4%)
    pallas_call x3, Pallas kernels, inner(): pl.pallas_call(kernel, out_shape=[shape((BOXES + 1, 32, points), F32), sh...  22.8 us
    ppermute x8, starting transfers between devices, xor_permute(): return lax.ppermute(value, axis, [(i, i ^ bits) for i in range(count)])  19.9 us
    pallas_call x1, Pallas kernels, shards(): pl.pallas_call(outer_kernel, out_shape=[acc_shape] + [shape((4, 32, point...  15.7 us
    all_to_all x1, starting transfers between devices, shards(): gathered = lax.all_to_all(sums, ('gx', 'gy', 'gz'), 0, 0, tiled=True)  9.89 us
    ppermute x6, starting transfers between devices, along(): lax.ppermute(value, name, [(i, (i + step) % size) for i in range(size)])  9.75 us
    all_to_all x1, waiting for transfers between devices, shards(): gathered = lax.all_to_all(sums, ('gx', 'gy', 'gz'), 0, 0, tiled=True)  9.46 us
    pallas_call x1, Pallas kernels, shards(): pl.pallas_call(local_kernel, out_shape=[shape((BOXES, 64, 128), BF16), sh...  4.87 us
    unnamed x23, local copies, waits for them, and re-layouts  3.93 us
  transfers between devices with their start and end apart: 15, of which 2 were waited for; matrix products, arithmetic and copies ran while one was open for 0% of the time, Pallas kernels for 44%

profile of v4, /device:TPU:1, one launch (start us, length us, event | category | flops | bytes accessed | tf_op | source)
XLA Modules:
  0.0 103.2 jit_solution(5712759628044773167)
XLA Ops:
  0.6 1.0 %copy-done = bf16[2,2,2,32,1024]{4,3,2,1,0:T(8,128)(2,1)S(1)} copy-done((bf16[2,2,2,32,1024]{4,3,2,1,0:T(8,128)(2,1)S(1)}, bf16[2,2,2,32,1024]{4,3,2,1,0:T(8,128)(2,1)}, u32[]{:S(2)}) %copy-start) | copy-done | bytes 524312
  1.7 0.9 copy-done.1
  3.2 2.2 %prep.1 = (bf16[9,48,1024]{2,1,0:T(8,128)(2,1)S(1)}, bf16[9,48,1024]{2,1,0:T(8,128)(2,1)S(1)}, bf16[8,48,1024]{2,1,0:T(8,128)(2,1)S(1)}, bf16[8,64,1024]{2,1,0:T...) custom-call(s32[2,2,2]{2,1,0:T(2,128)S(1)} %copy-done.2, ...), custom_call_target="tpu_custom_call" | custom-call | tf_op jit(solution)/shard_map/prep/pallas_call | solution.py:411
  5.4 7.8 %collective-permute-start = (bf16[1,64,256]{2,1,0:T(8,128)(2,1)S(1)}, bf16[1,64,256]{2,1,0:T(8,128)(2,1)S(1)}, u32[]{:S(2)}, u32[]{:S(2)}) collective-permute-start(bf16[1,64,256]{2,1,0:T(8,128)(2,1)S(1)} %bitcast.11), channel_id=1, source_target_pairs={{0,8},{1,9},{2,10},{3,11},{4,12},{5,13},{6,14},{7,15},{8,0},{9,1},... | collective-permute-start | bytes 98312 | tf_op jit(solution)/shard_map/ppermute | solution.py:404
  13.2 1.0 collective-permute-start.1
  14.2 7.2 %self_tiles.1 = (f32[9,32,1024]{2,1,0:T(8,128)S(1)}, f32[8,128]{1,0:T(8,128)S(1)}) custom-call(s32[2,2,2]{2,1,0:T(2,128)S(1)} %copy-done.2, bf16[9,48,1024]{2,1,0:T(8,128)(2,1)S(1)} %get-tuple-element.43.refs_1_, bf16[9,48,1024]{2,1,0:T(8,128)(2,1)S(1)} %get-tuple-element.42.refs_2_.pay, bf16[8,48,1024]{2,1,0:T(8,128)(2,1)S(1)} %get-tuple-element.41.refs_3_.fb, ...), custom_call_target="tpu_custom_call" | custom-call | flops 12000000000 | bytes 4194304 | tf_op jit(solution)/shard_map/self_tiles/pallas_call | solution.py:450
  22.2 1.6 %collective-permute-start.3 = (bf16[2,64,256]{2,1,0:T(8,128)(2,1)S(1)}, bf16[2,64,256]{2,1,0:T(8,128)(2,1)S(1)}, u32[]{:S(2)}, u32[]{:S(2)}) collective-permute-start(bf16[2,64,256]{2,1,0:T(8,128)(2,1)S(1)} %pad_maximum_fusion), channel_id=1, source_target_pairs={{0,32},{16,48},{32,0},{48,16},{1,33},{17,49},{33,1},{49,17},{2,34}... | collective-permute-start | bytes 196616 | tf_op jit(solution)/shard_map/ppermute | solution.py:404
  23.8 1.3 %collective-permute-start.2 = (bf16[2,64,256]{2,1,0:T(8,128)(2,1)S(1)}, bf16[2,64,256]{2,1,0:T(8,128)(2,1)S(1)}, u32[]{:S(2)}, u32[]{:S(2)}) collective-permute-start(bf16[2,64,256]{2,1,0:T(8,128)(2,1)S(1)} %pad_maximum_fusion), channel_id=1, source_target_pairs={{0,16},{16,0},{32,48},{48,32},{1,17},{17,1},{33,49},{49,33},{2,18}... | collective-permute-start | bytes 196616 | tf_op jit(solution)/shard_map/ppermute | solution.py:404
  25.0 1.4 %collective-permute-start.5 = (bf16[4,48,1024]{2,1,0:T(8,128)(2,1)S(1)}, bf16[4,48,1024]{2,1,0:T(8,128)(2,1)S(1)}, u32[]{:S(2)}, u32[]{:S(2)}) collective-permute-start(bf16[4,48,1024]{2,1,0:T(8,128)(2,1)S(1)} %get-tuple-element.57), channel_id=1, source_target_pairs={{0,192},{64,0},{128,64},{192,128},{1,193},{65,1},{129,65},{193,129... | collective-permute-start | bytes 1179656 | tf_op jit(solution)/shard_map/ppermute | solution.py:464
  26.5 7.5 %pairs_low.1 = (f32[9,32,1024]{2,1,0:T(8,128)S(1)}, f32[8,128]{1,0:T(8,128)S(1)}) custom-call(s32[2,2,2]{2,1,0:T(2,128)S(1)} %copy-done.2, bf16[9,48,1024]{2,1,0:T(8,128)(2,1)S(1)} %get-tuple-element.43.refs_1_, bf16[9,48,1024]{2,1,0:T(8,128)(2,1)S(1)} %get-tuple-element.42.refs_2_.pay, bf16[8,48,1024]{2,1,0:T(8,128)(2,1)S(1)} %get-tuple-element.41.refs_3_.fb, ...), custom_call_target="tpu_custom_call" | custom-call | flops 12000000000 | bytes 4194304 | tf_op jit(solution)/shard_map/pairs_low/pallas_call | solution.py:450
  34.2 3.4 %collective-permute-start.9 = (bf16[8,64,256]{2,1,0:T(8,128)(2,1)S(1)}, bf16[8,64,256]{2,1,0:T(8,128)(2,1)S(1)}, u32[]{:S(2)}, u32[]{:S(2)}) collective-permute-start(bf16[8,64,256]{2,1,0:T(8,128)(2,1)S(1)} %get-tuple-element.81), channel_id=1, source_target_pairs={{0,6},{1,7},{2,4},{3,5},{4,2},{5,3},{6,0},{7,1},{8,14},{9,15},{10,... | collective-permute-start | bytes 786440 | tf_op jit(solution)/shard_map/ppermute | solution.py:404
  37.5 2.1 %collective-permute-start.8 = (bf16[8,64,256]{2,1,0:T(8,128)(2,1)S(1)}, bf16[8,64,256]{2,1,0:T(8,128)(2,1)S(1)}, u32[]{:S(2)}, u32[]{:S(2)}) collective-permute-start(bf16[8,64,256]{2,1,0:T(8,128)(2,1)S(1)} %get-tuple-element.81), channel_id=1, source_target_pairs={{0,4},{1,5},{2,6},{3,7},{4,0},{5,1},{6,2},{7,3},{8,12},{9,13},{10,... | collective-permute-start | bytes 786440 | tf_op jit(solution)/shard_map/ppermute | solution.py:404
  39.7 2.6 %collective-permute-start.6 = (bf16[4,48,1024]{2,1,0:T(8,128)(2,1)S(1)}, bf16[4,48,1024]{2,1,0:T(8,128)(2,1)S(1)}, u32[]{:S(2)}, u32[]{:S(2)}) collective-permute-start(bf16[4,48,1024]{2,1,0:T(8,128)(2,1)S(1)} %get-tuple-element.58), channel_id=1, source_target_pairs={{0,48},{16,0},{32,16},{48,32},{1,49},{17,1},{33,17},{49,33},{2,50}... | collective-permute-start | bytes 1179656 | tf_op jit(solution)/shard_map/ppermute | solution.py:464
  42.3 8.1 %pairs_high.1 = (f32[9,32,1024]{2,1,0:T(8,128)S(1)}, f32[8,128]{1,0:T(8,128)S(1)}) custom-call(s32[2,2,2]{2,1,0:T(2,128)S(1)} %copy-done.2, bf16[9,48,1024]{2,1,0:T(8,128)(2,1)S(1)} %get-tuple-element.43.refs_1_, bf16[9,48,1024]{2,1,0:T(8,128)(2,1)S(1)} %get-tuple-element.42.refs_2_.pay, bf16[8,48,1024]{2,1,0:T(8,128)(2,1)S(1)} %get-tuple-element.41.refs_3_.fb, ...), custom_call_target="tpu_custom_call" | custom-call | flops 12000000000 | bytes 4194304 | tf_op jit(solution)/shard_map/pairs_high/pallas_call | solution.py:450
  51.2 2.9 %collective-permute-start.13 = (bf16[32,64,256]{2,1,0:T(8,128)(2,1)S(1)}, bf16[32,64,256]{2,1,0:T(8,128)(2,1)S(1)}, u32[]{:S(2)}, u32[]{:S(2)}) collective-permute-start(bf16[32,64,256]{2,1,0:T(8,128)(2,1)S(1)} %constant_dynamic-update-slice_fusion.5.here), channel_id=1, source_target_pairs={{0,1},{1,0},{2,3},{3,2},{4,5},{5,4},{6,7},{7,6},{8,9},{9,8},{10,11... | collective-permute-start | bytes 3145736 | tf_op jit(solution)/shard_map/ppermute | solution.py:404
  54.1 15.7 %face_tiles.1 = (f32[8,32,1024]{2,1,0:T(8,128)S(1)}, f32[4,32,1024]{2,1,0:T(8,128)S(1)}, f32[4,32,1024]{2,1,0:T(8,128)S(1)}, f32[4,32,1024]{2,1,0:T(8,128)}, f32[32,128]{1,0:T(8,128)S(1)}) custom-call(s32[2,2,2]{2,1,0:T(2,128)S(1)} %copy-done.2, bf16[8,48,1024]{2,1,0:T(8,128)(2,1)S(1)} %get-tuple-element.41.refs_3_.fb, ...), custom_call_target="tpu_custom_call" | custom-call | flops 12000000000 | bytes 4194304 | tf_op jit(solution)/shard_map/face_tiles/pallas_call | solution.py:484
  69.8 1.3 %collective-permute-start.10 = (f32[4,32,1024]{2,1,0:T(8,128)}, f32[4,32,1024]{2,1,0:T(8,128)S(1)}, u32[]{:S(2)}, u32[]{:S(2)}) collective-permute-start(f32[4,32,1024]{2,1,0:T(8,128)} %get-tuple-element.67), channel_id=1, source_target_pairs={{0,1},{1,2},{2,3},{3,4},{4,5},{5,6},{6,7},{7,8},{8,9},{9,10},{10,1... | collective-permute-start | bytes 1572872 | tf_op jit(solution)/shard_map/ppermute | solution.py:464
  71.2 3.4 %collective-permute-start.12 = (f32[4,32,1024]{2,1,0:T(8,128)S(1)}, f32[4,32,1024]{2,1,0:T(8,128)}, u32[]{:S(2)}, u32[]{:S(2)}) collective-permute-start(f32[4,32,1024]{2,1,0:T(8,128)S(1)} %get-tuple-element.69), channel_id=1, source_target_pairs={{0,64},{64,128},{128,192},{192,0},{1,65},{65,129},{129,193},{193,1... | collective-permute-start | bytes 1572872 | tf_op jit(solution)/shard_map/ppermute | solution.py:464
  74.6 4.9 %locals.1 = (bf16[8,64,128]{2,1,0:T(8,128)(2,1)S(1)}, f32[256,1,128]{2,1,0:T(1,128)}) custom-call(s32[2,2,2]{2,1,0:T(2,128)S(1)} %copy-done.2, s32[2,64]{1,0:T(2,128)S(1)} %bitcast.14, s32[2,64]{1,0:T(2,128)S(1)} %bitcast.15, bf16[32,64,256]{2,1,0:T(8,128)(2,1)S(1)} %constant_dynamic-update-slice_fusion.5.here, ...), custom_call_target="tpu_custom_call" | custom-call | tf_op jit(solution)/shard_map/locals/pallas_call | solution.py:503
  79.5 9.9 %all-to-all-start = ((f32[256,1,128]{2,1,0:T(1,128)}), f32[256,1,128]{2,1,0:T(1,128)S(1)}, u32[]{:S(2)}, u32[]{:S(2)}) async-start(f32[256,1,128]{2,1,0:T(1,128)} %get-tuple-element.78), calls=%async_computation | async-start | bytes 262144 | tf_op jit(solution)/shard_map/all_to_all | solution.py:515
  89.4 1.2 %copy-done.7 = f32[8,32,1024]{2,1,0:T(8,128)S(1)} copy-done((f32[8,32,1024]{2,1,0:T(8,128)S(1)}, f32[8,32,1024]{2,1,0:T(8,128)}, u32[]{:S(2)}) %copy-start.7) | copy-done | bytes 1048600
  90.6 2.3 %total.1 = (bf16[8,32,1024]{2,1,0:T(8,128)(2,1)}, f32[8,128]{1,0:T(8,128)S(1)}) custom-call(s32[2,2,2]{2,1,0:T(2,128)S(1)} %copy-done.3, f32[8,32,1024]{2,1,0:T(8,128)S(1)} %copy-done.7, f32[4,32,1024]{2,1,0:T(8,128)S(1)} %collective-permute-done.10.r2, f32[4,32,1024]{2,1,0:T(8,128)S(1)} %collective-permute-done.11.r1, ...), custom_call_target="tpu_custom_call" | custom-call | flops 12000000000 | bytes 4194304 | tf_op jit(solution)/shard_map/total/pallas_call | solution.py:516
  92.9 9.5 %all-to-all-done.gathered = f32[256,1,128]{2,1,0:T(1,128)S(1)} async-done(((f32[256,1,128]{2,1,0:T(1,128)}), f32[256,1,128]{2,1,0:T(1,128)S(1)}, u32[]{:S(2)}, u32[]{:S(2)}) %all-to-all-start) | async-done | bytes 131104 | tf_op jit(solution)/shard_map/all_to_all | solution.py:515
  102.3 0.9 quad.1
  (42 shorter events, 2.3 us)
Async XLA Ops:
  0.6 1.0 %copy-start = (bf16[2,2,2,32,1024]{4,3,2,1,0:T(8,128)(2,1)S(1)}, bf16[2,2,2,32,1024]{4,3,2,1,0:T(8,128)(2,1)}, u32[]{:S(2)}) copy-start(bf16[2,2,2,32,1024]{4,3,2,1,0:T(8,128)(2,1)} %probes.1) | copy-start | bytes 1572868
  1.7 0.9 copy-start.1
  2.6 0.7 copy-start.2
  5.4 16.0 %collective-permute-start = (bf16[1,64,256]{2,1,0:T(8,128)(2,1)S(1)}, bf16[1,64,256]{2,1,0:T(8,128)(2,1)S(1)}, u32[]{:S(2)}, u32[]{:S(2)}) collective-permute-start(bf16[1,64,256]{2,1,0:T(8,128)(2,1)S(1)} %bitcast.11), channel_id=1, source_target_pairs={{0,8},{1,9},{2,10},{3,11},{4,12},{5,13},{6,14},{7,15},{8,0},{9,1},... | collective-permute-start | bytes 98312 | tf_op jit(solution)/shard_map/ppermute | solution.py:404
  13.2 20.8 %collective-permute-start.1 = (bf16[4,48,1024]{2,1,0:T(8,128)(2,1)S(1)}, bf16[4,48,1024]{2,1,0:T(8,128)(2,1)S(1)}, u32[]{:S(2)}, u32[]{:S(2)}) collective-permute-start(bf16[4,48,1024]{2,1,0:T(8,128)(2,1)S(1)} %get-tuple-element.51), channel_id=1, source_target_pairs={{0,15},{1,0},{2,1},{3,2},{4,3},{5,4},{6,5},{7,6},{8,7},{9,8},{10,9... | collective-permute-start | bytes 1179656 | tf_op jit(solution)/shard_map/ppermute | solution.py:464
  21.4 12.6 %collective-permute-start.4 = (bf16[2,64,256]{2,1,0:T(8,128)(2,1)S(1)}, bf16[2,64,256]{2,1,0:T(8,128)(2,1)S(1)}, u32[]{:S(2)}, u32[]{:S(2)}) collective-permute-start(bf16[2,64,256]{2,1,0:T(8,128)(2,1)S(1)} %pad_maximum_fusion), channel_id=1, source_target_pairs={{0,48},{16,32},{32,16},{48,0},{1,49},{17,33},{33,17},{49,1},{2,50}... | collective-permute-start | bytes 196616 | tf_op jit(solution)/shard_map/ppermute | solution.py:404
  22.2 11.9 %collective-permute-start.3 = (bf16[2,64,256]{2,1,0:T(8,128)(2,1)S(1)}, bf16[2,64,256]{2,1,0:T(8,128)(2,1)S(1)}, u32[]{:S(2)}, u32[]{:S(2)}) collective-permute-start(bf16[2,64,256]{2,1,0:T(8,128)(2,1)S(1)} %pad_maximum_fusion), channel_id=1, source_target_pairs={{0,32},{16,48},{32,0},{48,16},{1,33},{17,49},{33,1},{49,17},{2,34}... | collective-permute-start | bytes 196616 | tf_op jit(solution)/shard_map/ppermute | solution.py:404
  23.8 10.3 %collective-permute-start.2 = (bf16[2,64,256]{2,1,0:T(8,128)(2,1)S(1)}, bf16[2,64,256]{2,1,0:T(8,128)(2,1)S(1)}, u32[]{:S(2)}, u32[]{:S(2)}) collective-permute-start(bf16[2,64,256]{2,1,0:T(8,128)(2,1)S(1)} %pad_maximum_fusion), channel_id=1, source_target_pairs={{0,16},{16,0},{32,48},{48,32},{1,17},{17,1},{33,49},{49,33},{2,18}... | collective-permute-start | bytes 196616 | tf_op jit(solution)/shard_map/ppermute | solution.py:404
  25.0 25.4 %collective-permute-start.5 = (bf16[4,48,1024]{2,1,0:T(8,128)(2,1)S(1)}, bf16[4,48,1024]{2,1,0:T(8,128)(2,1)S(1)}, u32[]{:S(2)}, u32[]{:S(2)}) collective-permute-start(bf16[4,48,1024]{2,1,0:T(8,128)(2,1)S(1)} %get-tuple-element.57), channel_id=1, source_target_pairs={{0,192},{64,0},{128,64},{192,128},{1,193},{65,1},{129,65},{193,129... | collective-permute-start | bytes 1179656 | tf_op jit(solution)/shard_map/ppermute | solution.py:464
  34.2 16.3 %collective-permute-start.9 = (bf16[8,64,256]{2,1,0:T(8,128)(2,1)S(1)}, bf16[8,64,256]{2,1,0:T(8,128)(2,1)S(1)}, u32[]{:S(2)}, u32[]{:S(2)}) collective-permute-start(bf16[8,64,256]{2,1,0:T(8,128)(2,1)S(1)} %get-tuple-element.81), channel_id=1, source_target_pairs={{0,6},{1,7},{2,4},{3,5},{4,2},{5,3},{6,0},{7,1},{8,14},{9,15},{10,... | collective-permute-start | bytes 786440 | tf_op jit(solution)/shard_map/ppermute | solution.py:404
  37.5 12.9 %collective-permute-start.8 = (bf16[8,64,256]{2,1,0:T(8,128)(2,1)S(1)}, bf16[8,64,256]{2,1,0:T(8,128)(2,1)S(1)}, u32[]{:S(2)}, u32[]{:S(2)}) collective-permute-start(bf16[8,64,256]{2,1,0:T(8,128)(2,1)S(1)} %get-tuple-element.81), channel_id=1, source_target_pairs={{0,4},{1,5},{2,6},{3,7},{4,0},{5,1},{6,2},{7,3},{8,12},{9,13},{10,... | collective-permute-start | bytes 786440 | tf_op jit(solution)/shard_map/ppermute | solution.py:404
  39.7 11.5 %collective-permute-start.7 = (bf16[8,64,256]{2,1,0:T(8,128)(2,1)S(1)}, bf16[8,64,256]{2,1,0:T(8,128)(2,1)S(1)}, u32[]{:S(2)}, u32[]{:S(2)}) collective-permute-start(bf16[8,64,256]{2,1,0:T(8,128)(2,1)S(1)} %get-tuple-element.81), channel_id=1, source_target_pairs={{0,2},{1,3},{2,0},{3,1},{4,6},{5,7},{6,4},{7,5},{8,10},{9,11},{10,... | collective-permute-start | bytes 786440 | tf_op jit(solution)/shard_map/ppermute | solution.py:404
  39.7 11.5 %collective-permute-start.6 = (bf16[4,48,1024]{2,1,0:T(8,128)(2,1)S(1)}, bf16[4,48,1024]{2,1,0:T(8,128)(2,1)S(1)}, u32[]{:S(2)}, u32[]{:S(2)}) collective-permute-start(bf16[4,48,1024]{2,1,0:T(8,128)(2,1)S(1)} %get-tuple-element.58), channel_id=1, source_target_pairs={{0,48},{16,0},{32,16},{48,32},{1,49},{17,1},{33,17},{49,33},{2,50}... | collective-permute-start | bytes 1179656 | tf_op jit(solution)/shard_map/ppermute | solution.py:464
  51.2 23.3 %collective-permute-start.13 = (bf16[32,64,256]{2,1,0:T(8,128)(2,1)S(1)}, bf16[32,64,256]{2,1,0:T(8,128)(2,1)S(1)}, u32[]{:S(2)}, u32[]{:S(2)}) collective-permute-start(bf16[32,64,256]{2,1,0:T(8,128)(2,1)S(1)} %constant_dynamic-update-slice_fusion.5.here), channel_id=1, source_target_pairs={{0,1},{1,0},{2,3},{3,2},{4,5},{5,4},{6,7},{7,6},{8,9},{9,8},{10,11... | collective-permute-start | bytes 3145736 | tf_op jit(solution)/shard_map/ppermute | solution.py:404
  54.1 20.4 %copy-start.4 = (s32[1,1,1,64,2]{3,4,2,1,0:T(2,128)S(1)}, s32[1,1,1,64,2]{3,4,2,1,0:T(2,128)}, u32[]{:S(2)}) copy-start(s32[1,1,1,64,2]{3,4,2,1,0:T(2,128)} %param.8) | copy-start | bytes 1540
  54.1 20.4 %copy-start.5 = (s32[1,1,1,64,2]{3,4,2,1,0:T(2,128)S(1)}, s32[1,1,1,64,2]{3,4,2,1,0:T(2,128)}, u32[]{:S(2)}) copy-start(s32[1,1,1,64,2]{3,4,2,1,0:T(2,128)} %param.9) | copy-start | bytes 1540
  69.8 9.6 %copy-start.6 = (f32[8,32,1024]{2,1,0:T(8,128)}, f32[8,32,1024]{2,1,0:T(8,128)S(1)}, u32[]{:S(2)}) copy-start(f32[8,32,1024]{2,1,0:T(8,128)S(1)} %get-tuple-element.66.near) | copy-start | bytes 3145732
  69.8 19.5 %collective-permute-start.10 = (f32[4,32,1024]{2,1,0:T(8,128)}, f32[4,32,1024]{2,1,0:T(8,128)S(1)}, u32[]{:S(2)}, u32[]{:S(2)}) collective-permute-start(f32[4,32,1024]{2,1,0:T(8,128)} %get-tuple-element.67), channel_id=1, source_target_pairs={{0,1},{1,2},{2,3},{3,4},{4,5},{5,6},{6,7},{7,8},{8,9},{9,10},{10,1... | collective-permute-start | bytes 1572872 | tf_op jit(solution)/shard_map/ppermute | solution.py:464
  71.2 18.2 %collective-permute-start.11 = (f32[4,32,1024]{2,1,0:T(8,128)S(1)}, f32[4,32,1024]{2,1,0:T(8,128)S(1)}, u32[]{:S(2)}, u32[]{:S(2)}) collective-permute-start(f32[4,32,1024]{2,1,0:T(8,128)S(1)} %get-tuple-element.68), channel_id=1, source_target_pairs={{0,16},{16,32},{32,48},{48,0},{1,17},{17,33},{33,49},{49,1},{2,18}... | collective-permute-start | bytes 1572872 | tf_op jit(solution)/shard_map/ppermute | solution.py:464
  71.2 18.2 %collective-permute-start.12 = (f32[4,32,1024]{2,1,0:T(8,128)S(1)}, f32[4,32,1024]{2,1,0:T(8,128)}, u32[]{:S(2)}, u32[]{:S(2)}) collective-permute-start(f32[4,32,1024]{2,1,0:T(8,128)S(1)} %get-tuple-element.69), channel_id=1, source_target_pairs={{0,64},{64,128},{128,192},{192,0},{1,65},{65,129},{129,193},{193,1... | collective-permute-start | bytes 1572872 | tf_op jit(solution)/shard_map/ppermute | solution.py:464
  74.6 14.8 %copy-start.3 = (s32[2,2,2]{2,1,0:T(2,128)S(1)}, s32[2,2,2]{2,1,0:T(2,128)}, u32[]{:S(2)}) copy-start(s32[2,2,2]{2,1,0:T(2,128)} %counts.7) | copy-start | bytes 100
  79.5 22.9 %all-to-all-start = ((f32[256,1,128]{2,1,0:T(1,128)}), f32[256,1,128]{2,1,0:T(1,128)S(1)}, u32[]{:S(2)}, u32[]{:S(2)}) async-start(f32[256,1,128]{2,1,0:T(1,128)} %get-tuple-element.78), calls=%async_computation | async-start | bytes 262144 | tf_op jit(solution)/shard_map/all_to_all | solution.py:515
  89.4 1.2 %copy-start.7 = (f32[8,32,1024]{2,1,0:T(8,128)S(1)}, f32[8,32,1024]{2,1,0:T(8,128)}, u32[]{:S(2)}) copy-start(f32[8,32,1024]{2,1,0:T(8,128)} %copy-done.6) | copy-start | bytes 3145732

commit v5 on v4

--- a/solution.py
+++ b/solution.py
@@ -354,7 +354,7 @@
     sums[...] = jnp.broadcast_to(row_sums.reshape(1, 1, 128), sums.shape)
 
 
-def total_kernel(counts, near, r2, r1, r0, loc, tab, kv, done):
+def total_kernel(counts, near, r2, r0, r1, loc, tab, kv, done):
     points = tab.shape[-1]
     lane = lax.broadcasted_iota(jnp.int32, (1, points), 1)
     for b in range(BOXES):
@@ -521,7 +521,7 @@
         compiler_params=PARAMS,
         cost_estimate=COST,
         name="total",
-    )(counts, near, returned[2], returned[1], returned[0], loc, tab)
+    )(counts, near, returned[2], returned[0], returned[1], loc, tab)
     quad = pl.pallas_call(
         quad_kernel,
         out_shape=shape((32,), F32),

time: 104 us -> 105 us (level); the launches traced: 103 us -> 106 us
  Pallas kernels: 48.7 us -> 53.3 us
  starting transfers between devices: 39.5 us -> 38.4 us
    all_to_all x1, starting transfers between devices: 9.89 us -> 16.3 us  [shards(): gathered = lax.all_to_all(sums, ('gx', 'gy', 'gz'), 0, 0, tiled=True)]
    ppermute x6, starting transfers between devices: 9.75 us -> 4.62 us  [along(): lax.ppermute(value, name, [(i, (i + step) % size) for i in range(size)])]
    pallas_call x3, Pallas kernels: 22.8 us -> 26.8 us  [inner(): pl.pallas_call(kernel, out_shape=[shape((BOXES + 1, 32, points), F32), sh...]
    ppermute x8, starting transfers between devices: 19.9 us -> 17.4 us  [xor_permute(): return lax.ppermute(value, axis, [(i, i ^ bits) for i in range(count)])]
  transfers between devices with their start and end apart: 15 -> 15, of which waited for: 2 -> 2; matrix products, arithmetic and copies ran while one was open for 0% -> 0% of each run, Pallas kernels for 44% -> 47%
where the time goes in v5:
time: 105 us; the launch traced here: 106 us
  Pallas kernels  53.3 us (51%)
  starting transfers between devices  38.4 us (37%)
  waiting for transfers between devices  9.89 us (9%)
  local copies, waits for them, and re-layouts  3.95 us (4%)
    pallas_call x3, Pallas kernels, inner(): pl.pallas_call(kernel, out_shape=[shape((BOXES + 1, 32, points), F32), sh...  26.8 us
    ppermute x8, starting transfers between devices, xor_permute(): return lax.ppermute(value, axis, [(i, i ^ bits) for i in range(count)])  17.4 us
    all_to_all x1, starting transfers between devices, shards(): gathered = lax.all_to_all(sums, ('gx', 'gy', 'gz'), 0, 0, tiled=True)  16.3 us
    pallas_call x1, Pallas kernels, shards(): pl.pallas_call(outer_kernel, out_shape=[acc_shape] + [shape((4, 32, point...  16.3 us
    all_to_all x1, waiting for transfers between devices, shards(): gathered = lax.all_to_all(sums, ('gx', 'gy', 'gz'), 0, 0, tiled=True)  9.46 us
    pallas_call x1, Pallas kernels, shards(): pl.pallas_call(local_kernel, out_shape=[shape((BOXES, 64, 128), BF16), sh...  4.87 us
    ppermute x6, starting transfers between devices, along(): lax.ppermute(value, name, [(i, (i + step) % size) for i in range(size)])  4.62 us
    unnamed x23, local copies, waits for them, and re-layouts  3.93 us
  transfers between devices with their start and end apart: 15, of which 2 were waited for; matrix products, arithmetic and copies ran while one was open for 0% of the time, Pallas kernels for 47%

profile of v5, /device:TPU:1, one launch (start us, length us, event | category | flops | bytes accessed | tf_op | source)
XLA Modules:
  0.0 106.4 jit_solution(9411423250740631762)
XLA Ops:
  0.6 1.0 copy-done
  1.7 0.9 copy-done.1
  2.6 0.7 copy-done.2
  3.2 2.2 %prep.1 = (bf16[9,48,1024]{2,1,0:T(8,128)(2,1)S(1)}, bf16[9,48,1024]{2,1,0:T(8,128)(2,1)S(1)}, bf16[8,48,1024]{2,1,0:T(8,128)(2,1)S(1)}, bf16[8,64,1024]{2,1,0:T...) custom-call(s32[2,2,2]{2,1,0:T(2,128)S(1)} %copy-done.2, ...), custom_call_target="tpu_custom_call" | custom-call | tf_op jit(solution)/shard_map/prep/pallas_call | solution.py:411
  5.4 7.8 %collective-permute-start = (bf16[1,64,256]{2,1,0:T(8,128)(2,1)S(1)}, bf16[1,64,256]{2,1,0:T(8,128)(2,1)S(1)}, u32[]{:S(2)}, u32[]{:S(2)}) collective-permute-start(bf16[1,64,256]{2,1,0:T(8,128)(2,1)S(1)} %bitcast.11), channel_id=1, source_target_pairs={{0,8},{1,9},{2,10},{3,11},{4,12},{5,13},{6,14},{7,15},{8,0},{9,1},... | collective-permute-start | bytes 98312 | tf_op jit(solution)/shard_map/ppermute | solution.py:404
  13.2 1.0 collective-permute-start.1
  14.2 8.4 %self_tiles.1 = (f32[9,32,1024]{2,1,0:T(8,128)S(1)}, f32[8,128]{1,0:T(8,128)S(1)}) custom-call(s32[2,2,2]{2,1,0:T(2,128)S(1)} %copy-done.2, bf16[9,48,1024]{2,1,0:T(8,128)(2,1)S(1)} %get-tuple-element.43.refs_1_, bf16[9,48,1024]{2,1,0:T(8,128)(2,1)S(1)} %get-tuple-element.42.refs_2_.pay, bf16[8,48,1024]{2,1,0:T(8,128)(2,1)S(1)} %get-tuple-element.41.refs_3_.fb, ...), custom_call_target="tpu_custom_call" | custom-call | flops 12000000000 | bytes 4194304 | tf_op jit(solution)/shard_map/self_tiles/pallas_call | solution.py:450
  22.6 1.3 %collective-permute-start.4 = (bf16[2,64,256]{2,1,0:T(8,128)(2,1)S(1)}, bf16[2,64,256]{2,1,0:T(8,128)(2,1)S(1)}, u32[]{:S(2)}, u32[]{:S(2)}) collective-permute-start(bf16[2,64,256]{2,1,0:T(8,128)(2,1)S(1)} %pad_maximum_fusion), channel_id=1, source_target_pairs={{0,48},{16,32},{32,16},{48,0},{1,49},{17,33},{33,17},{49,1},{2,50}... | collective-permute-start | bytes 196616 | tf_op jit(solution)/shard_map/ppermute | solution.py:404
  23.9 2.3 %collective-permute-start.2 = (bf16[2,64,256]{2,1,0:T(8,128)(2,1)S(1)}, bf16[2,64,256]{2,1,0:T(8,128)(2,1)S(1)}, u32[]{:S(2)}, u32[]{:S(2)}) collective-permute-start(bf16[2,64,256]{2,1,0:T(8,128)(2,1)S(1)} %pad_maximum_fusion), channel_id=1, source_target_pairs={{0,16},{16,0},{32,48},{48,32},{1,17},{17,1},{33,49},{49,33},{2,18}... | collective-permute-start | bytes 196616 | tf_op jit(solution)/shard_map/ppermute | solution.py:404
  26.3 1.0 collective-permute-start.5
  27.3 8.4 %pairs_low.1 = (f32[9,32,1024]{2,1,0:T(8,128)S(1)}, f32[8,128]{1,0:T(8,128)S(1)}) custom-call(s32[2,2,2]{2,1,0:T(2,128)S(1)} %copy-done.2, bf16[9,48,1024]{2,1,0:T(8,128)(2,1)S(1)} %get-tuple-element.43.refs_1_, bf16[9,48,1024]{2,1,0:T(8,128)(2,1)S(1)} %get-tuple-element.42.refs_2_.pay, bf16[8,48,1024]{2,1,0:T(8,128)(2,1)S(1)} %get-tuple-element.41.refs_3_.fb, ...), custom_call_target="tpu_custom_call" | custom-call | flops 12000000000 | bytes 4194304 | tf_op jit(solution)/shard_map/pairs_low/pallas_call | solution.py:450
  35.9 2.6 %collective-permute-start.9 = (bf16[8,64,256]{2,1,0:T(8,128)(2,1)S(1)}, bf16[8,64,256]{2,1,0:T(8,128)(2,1)S(1)}, u32[]{:S(2)}, u32[]{:S(2)}) collective-permute-start(bf16[8,64,256]{2,1,0:T(8,128)(2,1)S(1)} %get-tuple-element.81), channel_id=1, source_target_pairs={{0,6},{1,7},{2,4},{3,5},{4,2},{5,3},{6,0},{7,1},{8,14},{9,15},{10,... | collective-permute-start | bytes 786440 | tf_op jit(solution)/shard_map/ppermute | solution.py:404
  38.4 2.2 %collective-permute-start.8 = (bf16[8,64,256]{2,1,0:T(8,128)(2,1)S(1)}, bf16[8,64,256]{2,1,0:T(8,128)(2,1)S(1)}, u32[]{:S(2)}, u32[]{:S(2)}) collective-permute-start(bf16[8,64,256]{2,1,0:T(8,128)(2,1)S(1)} %get-tuple-element.81), channel_id=1, source_target_pairs={{0,4},{1,5},{2,6},{3,7},{4,0},{5,1},{6,2},{7,3},{8,12},{9,13},{10,... | collective-permute-start | bytes 786440 | tf_op jit(solution)/shard_map/ppermute | solution.py:404
  40.7 10.0 %pairs_high.1 = (f32[9,32,1024]{2,1,0:T(8,128)S(1)}, f32[8,128]{1,0:T(8,128)S(1)}) custom-call(s32[2,2,2]{2,1,0:T(2,128)S(1)} %copy-done.2, bf16[9,48,1024]{2,1,0:T(8,128)(2,1)S(1)} %get-tuple-element.43.refs_1_, bf16[9,48,1024]{2,1,0:T(8,128)(2,1)S(1)} %get-tuple-element.42.refs_2_.pay, bf16[8,48,1024]{2,1,0:T(8,128)(2,1)S(1)} %get-tuple-element.41.refs_3_.fb, ...), custom_call_target="tpu_custom_call" | custom-call | flops 12000000000 | bytes 4194304 | tf_op jit(solution)/shard_map/pairs_high/pallas_call | solution.py:450
  51.2 1.2 %collective-permute-start.13 = (bf16[32,64,256]{2,1,0:T(8,128)(2,1)S(1)}, bf16[32,64,256]{2,1,0:T(8,128)(2,1)S(1)}, u32[]{:S(2)}, u32[]{:S(2)}) collective-permute-start(bf16[32,64,256]{2,1,0:T(8,128)(2,1)S(1)} %constant_dynamic-update-slice_fusion.5.here), channel_id=1, source_target_pairs={{0,1},{1,0},{2,3},{3,2},{4,5},{5,4},{6,7},{7,6},{8,9},{9,8},{10,11... | collective-permute-start | bytes 3145736 | tf_op jit(solution)/shard_map/ppermute | solution.py:404
  52.4 16.3 %face_tiles.1 = (f32[8,32,1024]{2,1,0:T(8,128)S(1)}, f32[4,32,1024]{2,1,0:T(8,128)S(1)}, f32[4,32,1024]{2,1,0:T(8,128)S(1)}, f32[4,32,1024]{2,1,0:T(8,128)}, f32[32,128]{1,0:T(8,128)S(1)}) custom-call(s32[2,2,2]{2,1,0:T(2,128)S(1)} %copy-done.2, bf16[8,48,1024]{2,1,0:T(8,128)(2,1)S(1)} %get-tuple-element.41.refs_3_.fb, ...), custom_call_target="tpu_custom_call" | custom-call | flops 12000000000 | bytes 4194304 | tf_op jit(solution)/shard_map/face_tiles/pallas_call | solution.py:484
  68.7 2.0 %collective-permute-start.11 = (f32[4,32,1024]{2,1,0:T(8,128)S(1)}, f32[4,32,1024]{2,1,0:T(8,128)S(1)}, u32[]{:S(2)}, u32[]{:S(2)}) collective-permute-start(f32[4,32,1024]{2,1,0:T(8,128)S(1)} %get-tuple-element.68), channel_id=1, source_target_pairs={{0,64},{64,128},{128,192},{192,0},{1,65},{65,129},{129,193},{193,1... | collective-permute-start | bytes 1572872 | tf_op jit(solution)/shard_map/ppermute | solution.py:464
  70.7 0.7 collective-permute-start.12
  71.3 4.9 %locals.1 = (bf16[8,64,128]{2,1,0:T(8,128)(2,1)S(1)}, f32[256,1,128]{2,1,0:T(1,128)}) custom-call(s32[2,2,2]{2,1,0:T(2,128)S(1)} %copy-done.2, s32[2,64]{1,0:T(2,128)S(1)} %bitcast.14, s32[2,64]{1,0:T(2,128)S(1)} %bitcast.15, bf16[32,64,256]{2,1,0:T(8,128)(2,1)S(1)} %constant_dynamic-update-slice_fusion.5.here, ...), custom_call_target="tpu_custom_call" | custom-call | tf_op jit(solution)/shard_map/locals/pallas_call | solution.py:503
  76.2 16.3 %all-to-all-start = ((f32[256,1,128]{2,1,0:T(1,128)}), f32[256,1,128]{2,1,0:T(1,128)S(1)}, u32[]{:S(2)}, u32[]{:S(2)}) async-start(f32[256,1,128]{2,1,0:T(1,128)} %get-tuple-element.78), calls=%async_computation | async-start | bytes 262144 | tf_op jit(solution)/shard_map/all_to_all | solution.py:515
  92.6 1.2 %copy-done.7 = f32[8,32,1024]{2,1,0:T(8,128)S(1)} copy-done((f32[8,32,1024]{2,1,0:T(8,128)S(1)}, f32[8,32,1024]{2,1,0:T(8,128)}, u32[]{:S(2)}) %copy-start.7) | copy-done | bytes 1048600
  93.8 2.3 %total.1 = (bf16[8,32,1024]{2,1,0:T(8,128)(2,1)}, f32[8,128]{1,0:T(8,128)S(1)}) custom-call(s32[2,2,2]{2,1,0:T(2,128)S(1)} %copy-done.3, f32[8,32,1024]{2,1,0:T(8,128)S(1)} %copy-done.7, f32[4,32,1024]{2,1,0:T(8,128)S(1)} %collective-permute-done.10.r2, f32[4,32,1024]{2,1,0:T(8,128)S(1)} %collective-permute-done.11.r0, ...), custom_call_target="tpu_custom_call" | custom-call | flops 12000000000 | bytes 4194304 | tf_op jit(solution)/shard_map/total/pallas_call | solution.py:516
  96.1 9.5 %all-to-all-done.gathered = f32[256,1,128]{2,1,0:T(1,128)S(1)} async-done(((f32[256,1,128]{2,1,0:T(1,128)}), f32[256,1,128]{2,1,0:T(1,128)S(1)}, u32[]{:S(2)}, u32[]{:S(2)}) %all-to-all-start) | async-done | bytes 131104 | tf_op jit(solution)/shard_map/all_to_all | solution.py:515
  105.6 0.9 quad.1
  (42 shorter events, 0.6 us)
Async XLA Ops:
  0.6 1.0 copy-start
  1.7 0.9 copy-start.1
  2.6 0.7 copy-start.2
  5.4 17.2 %collective-permute-start = (bf16[1,64,256]{2,1,0:T(8,128)(2,1)S(1)}, bf16[1,64,256]{2,1,0:T(8,128)(2,1)S(1)}, u32[]{:S(2)}, u32[]{:S(2)}) collective-permute-start(bf16[1,64,256]{2,1,0:T(8,128)(2,1)S(1)} %bitcast.11), channel_id=1, source_target_pairs={{0,8},{1,9},{2,10},{3,11},{4,12},{5,13},{6,14},{7,15},{8,0},{9,1},... | collective-permute-start | bytes 98312 | tf_op jit(solution)/shard_map/ppermute | solution.py:404
  13.2 22.5 %collective-permute-start.1 = (bf16[4,48,1024]{2,1,0:T(8,128)(2,1)S(1)}, bf16[4,48,1024]{2,1,0:T(8,128)(2,1)S(1)}, u32[]{:S(2)}, u32[]{:S(2)}) collective-permute-start(bf16[4,48,1024]{2,1,0:T(8,128)(2,1)S(1)} %get-tuple-element.51), channel_id=1, source_target_pairs={{0,15},{1,0},{2,1},{3,2},{4,3},{5,4},{6,5},{7,6},{8,7},{9,8},{10,9... | collective-permute-start | bytes 1179656 | tf_op jit(solution)/shard_map/ppermute | solution.py:464
  22.6 13.1 %collective-permute-start.4 = (bf16[2,64,256]{2,1,0:T(8,128)(2,1)S(1)}, bf16[2,64,256]{2,1,0:T(8,128)(2,1)S(1)}, u32[]{:S(2)}, u32[]{:S(2)}) collective-permute-start(bf16[2,64,256]{2,1,0:T(8,128)(2,1)S(1)} %pad_maximum_fusion), channel_id=1, source_target_pairs={{0,48},{16,32},{32,16},{48,0},{1,49},{17,33},{33,17},{49,1},{2,50}... | collective-permute-start | bytes 196616 | tf_op jit(solution)/shard_map/ppermute | solution.py:404
  23.9 11.8 %collective-permute-start.3 = (bf16[2,64,256]{2,1,0:T(8,128)(2,1)S(1)}, bf16[2,64,256]{2,1,0:T(8,128)(2,1)S(1)}, u32[]{:S(2)}, u32[]{:S(2)}) collective-permute-start(bf16[2,64,256]{2,1,0:T(8,128)(2,1)S(1)} %pad_maximum_fusion), channel_id=1, source_target_pairs={{0,32},{16,48},{32,0},{48,16},{1,33},{17,49},{33,1},{49,17},{2,34}... | collective-permute-start | bytes 196616 | tf_op jit(solution)/shard_map/ppermute | solution.py:404
  23.9 11.8 %collective-permute-start.2 = (bf16[2,64,256]{2,1,0:T(8,128)(2,1)S(1)}, bf16[2,64,256]{2,1,0:T(8,128)(2,1)S(1)}, u32[]{:S(2)}, u32[]{:S(2)}) collective-permute-start(bf16[2,64,256]{2,1,0:T(8,128)(2,1)S(1)} %pad_maximum_fusion), channel_id=1, source_target_pairs={{0,16},{16,0},{32,48},{48,32},{1,17},{17,1},{33,49},{49,33},{2,18}... | collective-permute-start | bytes 196616 | tf_op jit(solution)/shard_map/ppermute | solution.py:404
  26.3 24.4 %collective-permute-start.5 = (bf16[4,48,1024]{2,1,0:T(8,128)(2,1)S(1)}, bf16[4,48,1024]{2,1,0:T(8,128)(2,1)S(1)}, u32[]{:S(2)}, u32[]{:S(2)}) collective-permute-start(bf16[4,48,1024]{2,1,0:T(8,128)(2,1)S(1)} %get-tuple-element.57), channel_id=1, source_target_pairs={{0,192},{64,0},{128,64},{192,128},{1,193},{65,1},{129,65},{193,129... | collective-permute-start | bytes 1179656 | tf_op jit(solution)/shard_map/ppermute | solution.py:464
  35.9 14.8 %collective-permute-start.9 = (bf16[8,64,256]{2,1,0:T(8,128)(2,1)S(1)}, bf16[8,64,256]{2,1,0:T(8,128)(2,1)S(1)}, u32[]{:S(2)}, u32[]{:S(2)}) collective-permute-start(bf16[8,64,256]{2,1,0:T(8,128)(2,1)S(1)} %get-tuple-element.81), channel_id=1, source_target_pairs={{0,6},{1,7},{2,4},{3,5},{4,2},{5,3},{6,0},{7,1},{8,14},{9,15},{10,... | collective-permute-start | bytes 786440 | tf_op jit(solution)/shard_map/ppermute | solution.py:404
  38.4 12.3 %collective-permute-start.8 = (bf16[8,64,256]{2,1,0:T(8,128)(2,1)S(1)}, bf16[8,64,256]{2,1,0:T(8,128)(2,1)S(1)}, u32[]{:S(2)}, u32[]{:S(2)}) collective-permute-start(bf16[8,64,256]{2,1,0:T(8,128)(2,1)S(1)} %get-tuple-element.81), channel_id=1, source_target_pairs={{0,4},{1,5},{2,6},{3,7},{4,0},{5,1},{6,2},{7,3},{8,12},{9,13},{10,... | collective-permute-start | bytes 786440 | tf_op jit(solution)/shard_map/ppermute | solution.py:404
  40.7 10.4 %collective-permute-start.7 = (bf16[8,64,256]{2,1,0:T(8,128)(2,1)S(1)}, bf16[8,64,256]{2,1,0:T(8,128)(2,1)S(1)}, u32[]{:S(2)}, u32[]{:S(2)}) collective-permute-start(bf16[8,64,256]{2,1,0:T(8,128)(2,1)S(1)} %get-tuple-element.81), channel_id=1, source_target_pairs={{0,2},{1,3},{2,0},{3,1},{4,6},{5,7},{6,4},{7,5},{8,10},{9,11},{10,... | collective-permute-start | bytes 786440 | tf_op jit(solution)/shard_map/ppermute | solution.py:404
  40.7 10.5 %collective-permute-start.6 = (bf16[4,48,1024]{2,1,0:T(8,128)(2,1)S(1)}, bf16[4,48,1024]{2,1,0:T(8,128)(2,1)S(1)}, u32[]{:S(2)}, u32[]{:S(2)}) collective-permute-start(bf16[4,48,1024]{2,1,0:T(8,128)(2,1)S(1)} %get-tuple-element.58), channel_id=1, source_target_pairs={{0,48},{16,0},{32,16},{48,32},{1,49},{17,1},{33,17},{49,33},{2,50}... | collective-permute-start | bytes 1179656 | tf_op jit(solution)/shard_map/ppermute | solution.py:464
  51.2 20.1 %collective-permute-start.13 = (bf16[32,64,256]{2,1,0:T(8,128)(2,1)S(1)}, bf16[32,64,256]{2,1,0:T(8,128)(2,1)S(1)}, u32[]{:S(2)}, u32[]{:S(2)}) collective-permute-start(bf16[32,64,256]{2,1,0:T(8,128)(2,1)S(1)} %constant_dynamic-update-slice_fusion.5.here), channel_id=1, source_target_pairs={{0,1},{1,0},{2,3},{3,2},{4,5},{5,4},{6,7},{7,6},{8,9},{9,8},{10,11... | collective-permute-start | bytes 3145736 | tf_op jit(solution)/shard_map/ppermute | solution.py:404
  52.4 19.0 %copy-start.4 = (s32[1,1,1,64,2]{3,4,2,1,0:T(2,128)S(1)}, s32[1,1,1,64,2]{3,4,2,1,0:T(2,128)}, u32[]{:S(2)}) copy-start(s32[1,1,1,64,2]{3,4,2,1,0:T(2,128)} %param.8) | copy-start | bytes 1540
  52.4 19.0 %copy-start.5 = (s32[1,1,1,64,2]{3,4,2,1,0:T(2,128)S(1)}, s32[1,1,1,64,2]{3,4,2,1,0:T(2,128)}, u32[]{:S(2)}) copy-start(s32[1,1,1,64,2]{3,4,2,1,0:T(2,128)} %param.9) | copy-start | bytes 1540
  68.7 7.6 %copy-start.6 = (f32[8,32,1024]{2,1,0:T(8,128)}, f32[8,32,1024]{2,1,0:T(8,128)S(1)}, u32[]{:S(2)}) copy-start(f32[8,32,1024]{2,1,0:T(8,128)S(1)} %get-tuple-element.66.near) | copy-start | bytes 3145732
  68.7 23.9 %collective-permute-start.10 = (f32[4,32,1024]{2,1,0:T(8,128)}, f32[4,32,1024]{2,1,0:T(8,128)S(1)}, u32[]{:S(2)}, u32[]{:S(2)}) collective-permute-start(f32[4,32,1024]{2,1,0:T(8,128)} %get-tuple-element.67), channel_id=1, source_target_pairs={{0,1},{1,2},{2,3},{3,4},{4,5},{5,6},{6,7},{7,8},{8,9},{9,10},{10,1... | collective-permute-start | bytes 1572872 | tf_op jit(solution)/shard_map/ppermute | solution.py:464
  68.7 23.9 %collective-permute-start.11 = (f32[4,32,1024]{2,1,0:T(8,128)S(1)}, f32[4,32,1024]{2,1,0:T(8,128)S(1)}, u32[]{:S(2)}, u32[]{:S(2)}) collective-permute-start(f32[4,32,1024]{2,1,0:T(8,128)S(1)} %get-tuple-element.68), channel_id=1, source_target_pairs={{0,64},{64,128},{128,192},{192,0},{1,65},{65,129},{129,193},{193,1... | collective-permute-start | bytes 1572872 | tf_op jit(solution)/shard_map/ppermute | solution.py:464
  70.7 21.9 %collective-permute-start.12 = (f32[4,32,1024]{2,1,0:T(8,128)S(1)}, f32[4,32,1024]{2,1,0:T(8,128)}, u32[]{:S(2)}, u32[]{:S(2)}) collective-permute-start(f32[4,32,1024]{2,1,0:T(8,128)S(1)} %get-tuple-element.69), channel_id=1, source_target_pairs={{0,16},{16,32},{32,48},{48,0},{1,17},{17,33},{33,49},{49,1},{2,18}... | collective-permute-start | bytes 1572872 | tf_op jit(solution)/shard_map/ppermute | solution.py:464
  71.3 21.3 %copy-start.3 = (s32[2,2,2]{2,1,0:T(2,128)S(1)}, s32[2,2,2]{2,1,0:T(2,128)}, u32[]{:S(2)}) copy-start(s32[2,2,2]{2,1,0:T(2,128)} %counts.7) | copy-start | bytes 100
  76.2 29.3 %all-to-all-start = ((f32[256,1,128]{2,1,0:T(1,128)}), f32[256,1,128]{2,1,0:T(1,128)S(1)}, u32[]{:S(2)}, u32[]{:S(2)}) async-start(f32[256,1,128]{2,1,0:T(1,128)} %get-tuple-element.78), calls=%async_computation | async-start | bytes 262144 | tf_op jit(solution)/shard_map/all_to_all | solution.py:515
  92.6 1.2 %copy-start.7 = (f32[8,32,1024]{2,1,0:T(8,128)S(1)}, f32[8,32,1024]{2,1,0:T(8,128)}, u32[]{:S(2)}) copy-start(f32[8,32,1024]{2,1,0:T(8,128)} %copy-done.6) | copy-start | bytes 3145732

commit v6 on v5

--- a/solution.py
+++ b/solution.py
@@ -305,8 +305,8 @@
     group = lax.broadcasted_iota(jnp.int32, (64, 256), 1) >> 5
 
     def step(g, carry):
-        for u in range(8):
-            k = g * 8 + u
+        for u in range(16):
+            k = g * 16 + u
             i = live[jnp.minimum(k, used - 1)]
             peer = i & 63
             box = req_box[i >> 6, peer]
@@ -329,7 +329,7 @@
             far_acc[tgt] += jnp.where(group == wanted, term, 0.0)
         return carry
 
-    lax.fori_loop(0, (used + 7) >> 3, step, 0)
+    lax.fori_loop(0, (used + 15) >> 4, step, 0)
     lane = lax.broadcasted_iota(jnp.int32, (64, 128), 1)
     far_sums = jnp.zeros((64, 128), F32)
     live_points = jnp.int32(0)

time: 105 us -> 106 us (level)
  starting transfers between devices: 38.4 us -> 46.5 us
  Pallas kernels: 53.3 us -> 46.9 us
    pallas_call x3, Pallas kernels: 26.8 us -> 20.9 us  [inner(): pl.pallas_call(kernel, out_shape=[shape((BOXES + 1, 32, points), F32), sh...]
    ppermute x6, starting transfers between devices: 4.62 us -> 9.56 us  [along(): lax.ppermute(value, name, [(i, (i + step) % size) for i in range(size)])]
    ppermute x8, starting transfers between devices: 17.4 us -> 20.2 us  [xor_permute(): return lax.ppermute(value, axis, [(i, i ^ bits) for i in range(count)])]
  transfers between devices with their start and end apart: 15 -> 15, of which waited for: 2 -> 1; matrix products, arithmetic and copies ran while one was open for 0% -> 0% of each run, Pallas kernels for 47% -> 41%
where the time goes in v6:
time: 106 us; the launch traced here: 108 us
  Pallas kernels  46.9 us (44%)
  starting transfers between devices  46.5 us (44%)
  waiting for transfers between devices  9.5 us (9%)
  local copies, waits for them, and re-layouts  3.95 us (4%)
    pallas_call x3, Pallas kernels, inner(): pl.pallas_call(kernel, out_shape=[shape((BOXES + 1, 32, points), F32), sh...  20.9 us
    ppermute x8, starting transfers between devices, xor_permute(): return lax.ppermute(value, axis, [(i, i ^ bits) for i in range(count)])  20.2 us
    all_to_all x1, starting transfers between devices, shards(): gathered = lax.all_to_all(sums, ('gx', 'gy', 'gz'), 0, 0, tiled=True)  16.8 us
    pallas_call x1, Pallas kernels, shards(): pl.pallas_call(outer_kernel, out_shape=[acc_shape] + [shape((4, 32, point...  15.9 us
    ppermute x6, starting transfers between devices, along(): lax.ppermute(value, name, [(i, (i + step) % size) for i in range(size)])  9.56 us
    all_to_all x1, waiting for transfers between devices, shards(): gathered = lax.all_to_all(sums, ('gx', 'gy', 'gz'), 0, 0, tiled=True)  9.46 us
    pallas_call x1, Pallas kernels, shards(): pl.pallas_call(local_kernel, out_shape=[shape((BOXES, 64, 128), BF16), sh...  4.72 us
    unnamed x23, local copies, waits for them, and re-layouts  3.93 us
  transfers between devices with their start and end apart: 15, of which 1 were waited for; matrix products, arithmetic and copies ran while one was open for 0% of the time, Pallas kernels for 41%

profile of v6, /device:TPU:1, one launch (start us, length us, event | category | flops | bytes accessed | tf_op | source)
XLA Modules:
  0.0 107.8 jit_solution(8183824074299442627)
XLA Ops:
  0.6 1.0 copy-done
  1.7 0.9 copy-done.1
  2.6 0.7 copy-done.2
  3.2 2.2 %prep.1 = (bf16[9,48,1024]{2,1,0:T(8,128)(2,1)S(1)}, bf16[9,48,1024]{2,1,0:T(8,128)(2,1)S(1)}, bf16[8,48,1024]{2,1,0:T(8,128)(2,1)S(1)}, bf16[8,64,1024]{2,1,0:T...) custom-call(s32[2,2,2]{2,1,0:T(2,128)S(1)} %copy-done.2, ...), custom_call_target="tpu_custom_call" | custom-call | tf_op jit(solution)/shard_map/prep/pallas_call | solution.py:411
  5.4 7.8 %collective-permute-start = (bf16[1,64,256]{2,1,0:T(8,128)(2,1)S(1)}, bf16[1,64,256]{2,1,0:T(8,128)(2,1)S(1)}, u32[]{:S(2)}, u32[]{:S(2)}) collective-permute-start(bf16[1,64,256]{2,1,0:T(8,128)(2,1)S(1)} %bitcast.11), channel_id=1, source_target_pairs={{0,8},{1,9},{2,10},{3,11},{4,12},{5,13},{6,14},{7,15},{8,0},{9,1},... | collective-permute-start | bytes 98312 | tf_op jit(solution)/shard_map/ppermute | solution.py:404
  13.2 1.0 collective-permute-start.1
  14.2 6.7 %self_tiles.1 = (f32[9,32,1024]{2,1,0:T(8,128)S(1)}, f32[8,128]{1,0:T(8,128)S(1)}) custom-call(s32[2,2,2]{2,1,0:T(2,128)S(1)} %copy-done.2, bf16[9,48,1024]{2,1,0:T(8,128)(2,1)S(1)} %get-tuple-element.43.refs_1_, bf16[9,48,1024]{2,1,0:T(8,128)(2,1)S(1)} %get-tuple-element.42.refs_2_.pay, bf16[8,48,1024]{2,1,0:T(8,128)(2,1)S(1)} %get-tuple-element.41.refs_3_.fb, ...), custom_call_target="tpu_custom_call" | custom-call | flops 12000000000 | bytes 4194304 | tf_op jit(solution)/shard_map/self_tiles/pallas_call | solution.py:450
  21.0 1.0 collective-permute-start.4
  22.0 2.4 %collective-permute-start.3 = (bf16[2,64,256]{2,1,0:T(8,128)(2,1)S(1)}, bf16[2,64,256]{2,1,0:T(8,128)(2,1)S(1)}, u32[]{:S(2)}, u32[]{:S(2)}) collective-permute-start(bf16[2,64,256]{2,1,0:T(8,128)(2,1)S(1)} %pad_maximum_fusion), channel_id=1, source_target_pairs={{0,32},{16,48},{32,0},{48,16},{1,33},{17,49},{33,1},{49,17},{2,34}... | collective-permute-start | bytes 196616 | tf_op jit(solution)/shard_map/ppermute | solution.py:404
  24.6 3.0 %collective-permute-start.5 = (bf16[4,48,1024]{2,1,0:T(8,128)(2,1)S(1)}, bf16[4,48,1024]{2,1,0:T(8,128)(2,1)S(1)}, u32[]{:S(2)}, u32[]{:S(2)}) collective-permute-start(bf16[4,48,1024]{2,1,0:T(8,128)(2,1)S(1)} %get-tuple-element.57), channel_id=1, source_target_pairs={{0,192},{64,0},{128,64},{192,128},{1,193},{65,1},{129,65},{193,129... | collective-permute-start | bytes 1179656 | tf_op jit(solution)/shard_map/ppermute | solution.py:464
  27.7 6.9 %pairs_low.1 = (f32[9,32,1024]{2,1,0:T(8,128)S(1)}, f32[8,128]{1,0:T(8,128)S(1)}) custom-call(s32[2,2,2]{2,1,0:T(2,128)S(1)} %copy-done.2, bf16[9,48,1024]{2,1,0:T(8,128)(2,1)S(1)} %get-tuple-element.43.refs_1_, bf16[9,48,1024]{2,1,0:T(8,128)(2,1)S(1)} %get-tuple-element.42.refs_2_.pay, bf16[8,48,1024]{2,1,0:T(8,128)(2,1)S(1)} %get-tuple-element.41.refs_3_.fb, ...), custom_call_target="tpu_custom_call" | custom-call | flops 12000000000 | bytes 4194304 | tf_op jit(solution)/shard_map/pairs_low/pallas_call | solution.py:450
  34.7 3.1 %collective-permute-start.9 = (bf16[8,64,256]{2,1,0:T(8,128)(2,1)S(1)}, bf16[8,64,256]{2,1,0:T(8,128)(2,1)S(1)}, u32[]{:S(2)}, u32[]{:S(2)}) collective-permute-start(bf16[8,64,256]{2,1,0:T(8,128)(2,1)S(1)} %get-tuple-element.81), channel_id=1, source_target_pairs={{0,6},{1,7},{2,4},{3,5},{4,2},{5,3},{6,0},{7,1},{8,14},{9,15},{10,... | collective-permute-start | bytes 786440 | tf_op jit(solution)/shard_map/ppermute | solution.py:404
  38.7 4.1 %collective-permute-start.6 = (bf16[4,48,1024]{2,1,0:T(8,128)(2,1)S(1)}, bf16[4,48,1024]{2,1,0:T(8,128)(2,1)S(1)}, u32[]{:S(2)}, u32[]{:S(2)}) collective-permute-start(bf16[4,48,1024]{2,1,0:T(8,128)(2,1)S(1)} %get-tuple-element.58), channel_id=1, source_target_pairs={{0,48},{16,0},{32,16},{48,32},{1,49},{17,1},{33,17},{49,33},{2,50}... | collective-permute-start | bytes 1179656 | tf_op jit(solution)/shard_map/ppermute | solution.py:464
  42.9 7.3 %pairs_high.1 = (f32[9,32,1024]{2,1,0:T(8,128)S(1)}, f32[8,128]{1,0:T(8,128)S(1)}) custom-call(s32[2,2,2]{2,1,0:T(2,128)S(1)} %copy-done.2, bf16[9,48,1024]{2,1,0:T(8,128)(2,1)S(1)} %get-tuple-element.43.refs_1_, bf16[9,48,1024]{2,1,0:T(8,128)(2,1)S(1)} %get-tuple-element.42.refs_2_.pay, bf16[8,48,1024]{2,1,0:T(8,128)(2,1)S(1)} %get-tuple-element.41.refs_3_.fb, ...), custom_call_target="tpu_custom_call" | custom-call | flops 12000000000 | bytes 4194304 | tf_op jit(solution)/shard_map/pairs_high/pallas_call | solution.py:450
  50.3 4.7 %collective-permute-start.13 = (bf16[32,64,256]{2,1,0:T(8,128)(2,1)S(1)}, bf16[32,64,256]{2,1,0:T(8,128)(2,1)S(1)}, u32[]{:S(2)}, u32[]{:S(2)}) collective-permute-start(bf16[32,64,256]{2,1,0:T(8,128)(2,1)S(1)} %constant_dynamic-update-slice_fusion.5.here), channel_id=1, source_target_pairs={{0,1},{1,0},{2,3},{3,2},{4,5},{5,4},{6,7},{7,6},{8,9},{9,8},{10,11... | collective-permute-start | bytes 3145736 | tf_op jit(solution)/shard_map/ppermute | solution.py:404
  55.0 15.9 %face_tiles.1 = (f32[8,32,1024]{2,1,0:T(8,128)S(1)}, f32[4,32,1024]{2,1,0:T(8,128)S(1)}, f32[4,32,1024]{2,1,0:T(8,128)S(1)}, f32[4,32,1024]{2,1,0:T(8,128)}, f32[32,128]{1,0:T(8,128)S(1)}) custom-call(s32[2,2,2]{2,1,0:T(2,128)S(1)} %copy-done.2, bf16[8,48,1024]{2,1,0:T(8,128)(2,1)S(1)} %get-tuple-element.41.refs_3_.fb, ...), custom_call_target="tpu_custom_call" | custom-call | flops 12000000000 | bytes 4194304 | tf_op jit(solution)/shard_map/face_tiles/pallas_call | solution.py:484
  71.0 0.7 collective-permute-start.10
  71.6 0.8 collective-permute-start.12
  72.4 4.7 %locals.1 = (bf16[8,64,128]{2,1,0:T(8,128)(2,1)S(1)}, f32[256,1,128]{2,1,0:T(1,128)}) custom-call(s32[2,2,2]{2,1,0:T(2,128)S(1)} %copy-done.2, s32[2,64]{1,0:T(2,128)S(1)} %bitcast.14, s32[2,64]{1,0:T(2,128)S(1)} %bitcast.15, bf16[32,64,256]{2,1,0:T(8,128)(2,1)S(1)} %constant_dynamic-update-slice_fusion.5.here, ...), custom_call_target="tpu_custom_call" | custom-call | tf_op jit(solution)/shard_map/locals/pallas_call | solution.py:503
  77.1 16.8 %all-to-all-start = ((f32[256,1,128]{2,1,0:T(1,128)}), f32[256,1,128]{2,1,0:T(1,128)S(1)}, u32[]{:S(2)}, u32[]{:S(2)}) async-start(f32[256,1,128]{2,1,0:T(1,128)} %get-tuple-element.78), calls=%async_computation | async-start | bytes 262144 | tf_op jit(solution)/shard_map/all_to_all | solution.py:515
  94.0 1.2 %copy-done.7 = f32[8,32,1024]{2,1,0:T(8,128)S(1)} copy-done((f32[8,32,1024]{2,1,0:T(8,128)S(1)}, f32[8,32,1024]{2,1,0:T(8,128)}, u32[]{:S(2)}) %copy-start.7) | copy-done | bytes 1048600
  95.2 2.3 %total.1 = (bf16[8,32,1024]{2,1,0:T(8,128)(2,1)}, f32[8,128]{1,0:T(8,128)S(1)}) custom-call(s32[2,2,2]{2,1,0:T(2,128)S(1)} %copy-done.3, f32[8,32,1024]{2,1,0:T(8,128)S(1)} %copy-done.7, f32[4,32,1024]{2,1,0:T(8,128)S(1)} %collective-permute-done.10.r2, f32[4,32,1024]{2,1,0:T(8,128)S(1)} %collective-permute-done.11.r0, ...), custom_call_target="tpu_custom_call" | custom-call | flops 12000000000 | bytes 4194304 | tf_op jit(solution)/shard_map/total/pallas_call | solution.py:516
  97.4 9.5 %all-to-all-done.gathered = f32[256,1,128]{2,1,0:T(1,128)S(1)} async-done(((f32[256,1,128]{2,1,0:T(1,128)}), f32[256,1,128]{2,1,0:T(1,128)S(1)}, u32[]{:S(2)}, u32[]{:S(2)}) %all-to-all-start) | async-done | bytes 131104 | tf_op jit(solution)/shard_map/all_to_all | solution.py:515
  106.9 0.9 quad.1
  (42 shorter events, 1.3 us)
Async XLA Ops:
  0.6 1.0 copy-start
  1.7 0.9 copy-start.1
  2.6 0.7 copy-start.2
  5.4 15.5 %collective-permute-start = (bf16[1,64,256]{2,1,0:T(8,128)(2,1)S(1)}, bf16[1,64,256]{2,1,0:T(8,128)(2,1)S(1)}, u32[]{:S(2)}, u32[]{:S(2)}) collective-permute-start(bf16[1,64,256]{2,1,0:T(8,128)(2,1)S(1)} %bitcast.11), channel_id=1, source_target_pairs={{0,8},{1,9},{2,10},{3,11},{4,12},{5,13},{6,14},{7,15},{8,0},{9,1},... | collective-permute-start | bytes 98312 | tf_op jit(solution)/shard_map/ppermute | solution.py:404
  13.2 21.4 %collective-permute-start.1 = (bf16[4,48,1024]{2,1,0:T(8,128)(2,1)S(1)}, bf16[4,48,1024]{2,1,0:T(8,128)(2,1)S(1)}, u32[]{:S(2)}, u32[]{:S(2)}) collective-permute-start(bf16[4,48,1024]{2,1,0:T(8,128)(2,1)S(1)} %get-tuple-element.51), channel_id=1, source_target_pairs={{0,15},{1,0},{2,1},{3,2},{4,3},{5,4},{6,5},{7,6},{8,7},{9,8},{10,9... | collective-permute-start | bytes 1179656 | tf_op jit(solution)/shard_map/ppermute | solution.py:464
  21.0 13.6 %collective-permute-start.4 = (bf16[2,64,256]{2,1,0:T(8,128)(2,1)S(1)}, bf16[2,64,256]{2,1,0:T(8,128)(2,1)S(1)}, u32[]{:S(2)}, u32[]{:S(2)}) collective-permute-start(bf16[2,64,256]{2,1,0:T(8,128)(2,1)S(1)} %pad_maximum_fusion), channel_id=1, source_target_pairs={{0,48},{16,32},{32,16},{48,0},{1,49},{17,33},{33,17},{49,1},{2,50}... | collective-permute-start | bytes 196616 | tf_op jit(solution)/shard_map/ppermute | solution.py:404
  22.0 12.6 %collective-permute-start.3 = (bf16[2,64,256]{2,1,0:T(8,128)(2,1)S(1)}, bf16[2,64,256]{2,1,0:T(8,128)(2,1)S(1)}, u32[]{:S(2)}, u32[]{:S(2)}) collective-permute-start(bf16[2,64,256]{2,1,0:T(8,128)(2,1)S(1)} %pad_maximum_fusion), channel_id=1, source_target_pairs={{0,32},{16,48},{32,0},{48,16},{1,33},{17,49},{33,1},{49,17},{2,34}... | collective-permute-start | bytes 196616 | tf_op jit(solution)/shard_map/ppermute | solution.py:404
  24.4 10.2 %collective-permute-start.2 = (bf16[2,64,256]{2,1,0:T(8,128)(2,1)S(1)}, bf16[2,64,256]{2,1,0:T(8,128)(2,1)S(1)}, u32[]{:S(2)}, u32[]{:S(2)}) collective-permute-start(bf16[2,64,256]{2,1,0:T(8,128)(2,1)S(1)} %pad_maximum_fusion), channel_id=1, source_target_pairs={{0,16},{16,0},{32,48},{48,32},{1,17},{17,1},{33,49},{49,33},{2,18}... | collective-permute-start | bytes 196616 | tf_op jit(solution)/shard_map/ppermute | solution.py:404
  24.6 25.5 %collective-permute-start.5 = (bf16[4,48,1024]{2,1,0:T(8,128)(2,1)S(1)}, bf16[4,48,1024]{2,1,0:T(8,128)(2,1)S(1)}, u32[]{:S(2)}, u32[]{:S(2)}) collective-permute-start(bf16[4,48,1024]{2,1,0:T(8,128)(2,1)S(1)} %get-tuple-element.57), channel_id=1, source_target_pairs={{0,192},{64,0},{128,64},{192,128},{1,193},{65,1},{129,65},{193,129... | collective-permute-start | bytes 1179656 | tf_op jit(solution)/shard_map/ppermute | solution.py:464
  34.7 15.4 %collective-permute-start.9 = (bf16[8,64,256]{2,1,0:T(8,128)(2,1)S(1)}, bf16[8,64,256]{2,1,0:T(8,128)(2,1)S(1)}, u32[]{:S(2)}, u32[]{:S(2)}) collective-permute-start(bf16[8,64,256]{2,1,0:T(8,128)(2,1)S(1)} %get-tuple-element.81), channel_id=1, source_target_pairs={{0,6},{1,7},{2,4},{3,5},{4,2},{5,3},{6,0},{7,1},{8,14},{9,15},{10,... | collective-permute-start | bytes 786440 | tf_op jit(solution)/shard_map/ppermute | solution.py:404
  37.8 12.3 %collective-permute-start.8 = (bf16[8,64,256]{2,1,0:T(8,128)(2,1)S(1)}, bf16[8,64,256]{2,1,0:T(8,128)(2,1)S(1)}, u32[]{:S(2)}, u32[]{:S(2)}) collective-permute-start(bf16[8,64,256]{2,1,0:T(8,128)(2,1)S(1)} %get-tuple-element.81), channel_id=1, source_target_pairs={{0,4},{1,5},{2,6},{3,7},{4,0},{5,1},{6,2},{7,3},{8,12},{9,13},{10,... | collective-permute-start | bytes 786440 | tf_op jit(solution)/shard_map/ppermute | solution.py:404
  38.3 11.9 %collective-permute-start.7 = (bf16[8,64,256]{2,1,0:T(8,128)(2,1)S(1)}, bf16[8,64,256]{2,1,0:T(8,128)(2,1)S(1)}, u32[]{:S(2)}, u32[]{:S(2)}) collective-permute-start(bf16[8,64,256]{2,1,0:T(8,128)(2,1)S(1)} %get-tuple-element.81), channel_id=1, source_target_pairs={{0,2},{1,3},{2,0},{3,1},{4,6},{5,7},{6,4},{7,5},{8,10},{9,11},{10,... | collective-permute-start | bytes 786440 | tf_op jit(solution)/shard_map/ppermute | solution.py:404
  38.7 11.5 %collective-permute-start.6 = (bf16[4,48,1024]{2,1,0:T(8,128)(2,1)S(1)}, bf16[4,48,1024]{2,1,0:T(8,128)(2,1)S(1)}, u32[]{:S(2)}, u32[]{:S(2)}) collective-permute-start(bf16[4,48,1024]{2,1,0:T(8,128)(2,1)S(1)} %get-tuple-element.58), channel_id=1, source_target_pairs={{0,48},{16,0},{32,16},{48,32},{1,49},{17,1},{33,17},{49,33},{2,50}... | collective-permute-start | bytes 1179656 | tf_op jit(solution)/shard_map/ppermute | solution.py:464
  50.3 22.1 %collective-permute-start.13 = (bf16[32,64,256]{2,1,0:T(8,128)(2,1)S(1)}, bf16[32,64,256]{2,1,0:T(8,128)(2,1)S(1)}, u32[]{:S(2)}, u32[]{:S(2)}) collective-permute-start(bf16[32,64,256]{2,1,0:T(8,128)(2,1)S(1)} %constant_dynamic-update-slice_fusion.5.here), channel_id=1, source_target_pairs={{0,1},{1,0},{2,3},{3,2},{4,5},{5,4},{6,7},{7,6},{8,9},{9,8},{10,11... | collective-permute-start | bytes 3145736 | tf_op jit(solution)/shard_map/ppermute | solution.py:404
  55.0 17.4 %copy-start.4 = (s32[1,1,1,64,2]{3,4,2,1,0:T(2,128)S(1)}, s32[1,1,1,64,2]{3,4,2,1,0:T(2,128)}, u32[]{:S(2)}) copy-start(s32[1,1,1,64,2]{3,4,2,1,0:T(2,128)} %param.8) | copy-start | bytes 1540
  55.0 17.4 %copy-start.5 = (s32[1,1,1,64,2]{3,4,2,1,0:T(2,128)S(1)}, s32[1,1,1,64,2]{3,4,2,1,0:T(2,128)}, u32[]{:S(2)}) copy-start(s32[1,1,1,64,2]{3,4,2,1,0:T(2,128)} %param.9) | copy-start | bytes 1540
  71.0 6.2 %copy-start.6 = (f32[8,32,1024]{2,1,0:T(8,128)}, f32[8,32,1024]{2,1,0:T(8,128)S(1)}, u32[]{:S(2)}) copy-start(f32[8,32,1024]{2,1,0:T(8,128)S(1)} %get-tuple-element.66.near) | copy-start | bytes 3145732
  71.0 23.0 %collective-permute-start.10 = (f32[4,32,1024]{2,1,0:T(8,128)}, f32[4,32,1024]{2,1,0:T(8,128)S(1)}, u32[]{:S(2)}, u32[]{:S(2)}) collective-permute-start(f32[4,32,1024]{2,1,0:T(8,128)} %get-tuple-element.67), channel_id=1, source_target_pairs={{0,1},{1,2},{2,3},{3,4},{4,5},{5,6},{6,7},{7,8},{8,9},{9,10},{10,1... | collective-permute-start | bytes 1572872 | tf_op jit(solution)/shard_map/ppermute | solution.py:464
  71.6 22.3 %collective-permute-start.11 = (f32[4,32,1024]{2,1,0:T(8,128)S(1)}, f32[4,32,1024]{2,1,0:T(8,128)S(1)}, u32[]{:S(2)}, u32[]{:S(2)}) collective-permute-start(f32[4,32,1024]{2,1,0:T(8,128)S(1)} %get-tuple-element.68), channel_id=1, source_target_pairs={{0,64},{64,128},{128,192},{192,0},{1,65},{65,129},{129,193},{193,1... | collective-permute-start | bytes 1572872 | tf_op jit(solution)/shard_map/ppermute | solution.py:464
  71.6 22.3 %collective-permute-start.12 = (f32[4,32,1024]{2,1,0:T(8,128)S(1)}, f32[4,32,1024]{2,1,0:T(8,128)}, u32[]{:S(2)}, u32[]{:S(2)}) collective-permute-start(f32[4,32,1024]{2,1,0:T(8,128)S(1)} %get-tuple-element.69), channel_id=1, source_target_pairs={{0,16},{16,32},{32,48},{48,0},{1,17},{17,33},{33,49},{49,1},{2,18}... | collective-permute-start | bytes 1572872 | tf_op jit(solution)/shard_map/ppermute | solution.py:464
  72.4 21.5 %copy-start.3 = (s32[2,2,2]{2,1,0:T(2,128)S(1)}, s32[2,2,2]{2,1,0:T(2,128)}, u32[]{:S(2)}) copy-start(s32[2,2,2]{2,1,0:T(2,128)} %counts.7) | copy-start | bytes 100
  77.1 29.8 %all-to-all-start = ((f32[256,1,128]{2,1,0:T(1,128)}), f32[256,1,128]{2,1,0:T(1,128)S(1)}, u32[]{:S(2)}, u32[]{:S(2)}) async-start(f32[256,1,128]{2,1,0:T(1,128)} %get-tuple-element.78), calls=%async_computation | async-start | bytes 262144 | tf_op jit(solution)/shard_map/all_to_all | solution.py:515
  93.9 1.2 %copy-start.7 = (f32[8,32,1024]{2,1,0:T(8,128)S(1)}, f32[8,32,1024]{2,1,0:T(8,128)}, u32[]{:S(2)}) copy-start(f32[8,32,1024]{2,1,0:T(8,128)} %copy-done.6) | copy-start | bytes 3145732
